TPU v7x, 32 devices: a whole 2x2x4 slice. The times are simulated.
32 devices in a mesh: frame: 4 (over z), patch: 8 (over y, x, core).
Axes of the slice: x: 2, y: 2, z: 4, core: 2. Of those that a mesh axis runs over, the one named last changes fastest.
Arguments:
- video: bfloat16 [8, 512, 1152], P('frame', 'patch'), may hold values from -6 to 6
- cotangent: bfloat16 [8, 512, 1152], P('frame', 'patch'), may hold values from -6 to 6
- frame_mask: int32 [8], replicated, may hold values 0 or 1
- spatial_project: bfloat16 [1152, 3456], replicated, may hold values from -0.1875 to 0.1875
- spatial_output: bfloat16 [1152, 1152], replicated, may hold values from -0.1875 to 0.1875
- temporal_project: bfloat16 [1152, 3456], replicated, may hold values from -0.1875 to 0.1875
- temporal_output: bfloat16 [1152, 1152], replicated, may hold values from -0.1875 to 0.1875
- spatial_inward: float32 [36, 32, 32], replicated, may hold values from -0.25 to 1.25, as said below
- spatial_outward: float32 [36, 32, 32], replicated, may hold values from -0.25 to 1.25, as said below
- temporal_inward: float32 [36, 32, 32], replicated, may hold values from -0.25 to 1.25, as said below
- temporal_outward: float32 [36, 32, 32], replicated, may hold values from -0.25 to 1.25, as said below
Outputs:
- video_gradient: bfloat16 [8, 512, 1152], P('frame', 'patch')
- gradient_spatial_inward: float32 [36, 32, 32], replicated
- gradient_spatial_outward: float32 [36, 32, 32], replicated
- gradient_temporal_inward: float32 [36, 32, 32], replicated
- gradient_temporal_outward: float32 [36, 32, 32], replicated
Inputs may be any that keep to these rules, and one draw needn't show every extreme that they name: `spatial_inward`: identity blocks plus independent entries. `spatial_outward`: identity blocks plus independent entries. `temporal_inward`: identity blocks plus independent entries. `temporal_outward`: identity blocks plus independent entries.
All inputs are finite; a program needn't handle non-finite values.
Results may differ from a plain program's by a relative error of at most 0.028.
Values may be sent and summed in bfloat16 or wider, within the bound.
No kernel may reach another device: no remote copies, remote signals or barrier semaphores. Data moves between devices by JAX's collectives and lax.ppermute only.
A program may use at most 192 MiB of HBM per device.

v0:
```python
import functools
import math

import jax
import jax.numpy as jnp
from jax import lax
from jax.experimental import pallas as pl
from jax.experimental.pallas import tpu as pltpu
from jax.sharding import PartitionSpec as P

D = 1152
HEADS = 16
HEAD_DIM = 72
BLOCK = 32
LANES = 128
TILE = 16
SPANS = ((0, 640), (640, 512))
CHUNKS = D // LANES
EPSILON = 1e-06
NEGATIVE = -1e30
SCALE = 1.0 / math.sqrt(HEAD_DIM)
F32 = jnp.float32
BF16 = jnp.bfloat16
VMEM = pl.BlockSpec(memory_space=pltpu.VMEM)
SMEM = pl.BlockSpec(memory_space=pltpu.SMEM)
HBM = pl.BlockSpec(memory_space=pltpu.HBM)
MIB = 1024 * 1024


def dot(a, b):
    return jnp.dot(a, b, preferred_element_type=F32)


def dot_nt(a, b):
    return lax.dot_general(a, b, (((1,), (1,)), ((), ())), preferred_element_type=F32)


def dot_tn(a, b):
    return lax.dot_general(a, b, (((0,), (0,)), ((), ())), preferred_element_type=F32)


def normalize(rows):
    average = jnp.mean(rows, axis=-1, keepdims=True)
    centered = rows - average
    variance = jnp.mean(centered * centered, axis=-1, keepdims=True)
    inverse = lax.rsqrt(variance + EPSILON)
    return centered * inverse, inverse


def normalize_backward(adjoint, normed, inverse):
    grad_mean = jnp.mean(adjoint, axis=-1, keepdims=True)
    grad_cross = jnp.mean(adjoint * normed, axis=-1, keepdims=True)
    return inverse * (adjoint - grad_mean - normed * grad_cross)


def diagonal_mask():
    row = lax.broadcasted_iota(jnp.int32, (LANES, LANES), 0)
    column = lax.broadcasted_iota(jnp.int32, (LANES, LANES), 1)
    return (row // BLOCK) == (column // BLOCK)


def lanes_of(chunk):
    return slice(chunk * LANES, (chunk + 1) * LANES)


def diagonal_spans(blocks_ref):
    width = blocks_ref.shape[1]
    return [(low, min(width, D - low)) for low in range(0, D, width)]


def rotate(rows, blocks_ref):
    return jnp.concatenate(
        [
            dot(rows[:, low : low + size], blocks_ref[low : low + size, 0:size])
            for low, size in diagonal_spans(blocks_ref)
        ],
        axis=1,
    )


def rotate_transposed(rows, blocks_ref):
    return jnp.concatenate(
        [
            dot_nt(rows[:, low : low + size], blocks_ref[low : low + size, 0:size])
            for low, size in diagonal_spans(blocks_ref)
        ],
        axis=1,
    )


def rotation_gradient(left, right, mask, term_ref, base, width=LANES):
    for low in range(0, D, width):
        span = slice(low, min(low + width, D))
        product = dot_tn(left[:, span], right[:, span])
        for inner in range(0, span.stop - low, LANES):
            tile = slice(inner, inner + LANES)
            full = jnp.where(mask, product[tile, tile], 0.0)
            packed = full[0:BLOCK]
            for i in range(1, LANES // BLOCK):
                packed = packed + full[i * BLOCK : (i + 1) * BLOCK]
            start = (base + (low + inner) // LANES) * BLOCK
            term_ref[start : start + BLOCK, :] = packed


class Arriving:
    def __init__(self, source, target, sem):
        self.target = target
        self.copy = pltpu.make_async_copy(source, target, sem)
        self.waited = False

    def begin(self):
        self.copy.start()

    def __call__(self):
        if not self.waited:
            self.copy.wait()
            self.waited = True
        return self.target


class Leaving:
    def __init__(self, source, target, sems):
        self.ref, self.target, self.sems = source, target, sems
        self.started = []

    def flush(self, *parts):
        for i in parts:
            copy = pltpu.make_async_copy(self.ref.at[i], self.target.at[i], self.sems.at[i])
            copy.start()
            self.started.append(copy)

    def finish(self):
        for copy in self.started:
            copy.wait()


def call(kernel, ins, outs, scratch=(), limit=60, cost=None):
    specs = {"v": VMEM, "s": SMEM, "h": HBM, "l": HBM, "p": HBM, "d": HBM}
    loads = [array for mode, array in ins if mode in "lp"]
    stores = [out for mode, out in outs if mode == "d"]
    staging = [pltpu.VMEM(array.shape, array.dtype) for array in loads + stores]
    staging += [pltpu.SemaphoreType.DMA] * len(loads)
    staging += [pltpu.SemaphoreType.DMA((out.shape[0],)) for out in stores]

    def body(*refs):
        given = list(refs[: len(ins) + len(outs)])
        own = refs[len(given) : len(given) + len(scratch)]
        staged = list(refs[len(given) + len(scratch) :])
        buffers, sems = staged[: len(loads) + len(stores)], staged[len(loads) + len(stores) :]
        leaving = []
        for i, (mode, _) in enumerate(list(ins) + list(outs)):
            if mode in "lp":
                given[i] = Arriving(given[i], buffers.pop(0), sems.pop(0))
                if mode == "l":
                    given[i].begin()
            elif mode == "d":
                given[i] = Leaving(buffers.pop(0), given[i], sems.pop(0))
                leaving.append(given[i])
        kernel(*given, *own)
        for out in leaving:
            out.finish()

    return pl.pallas_call(
        body,
        out_shape=tuple(out for _, out in outs),
        in_specs=[specs[mode] for mode, _ in ins],
        out_specs=tuple(specs[mode] for mode, _ in outs),
        scratch_shapes=list(scratch) + staging,
        compiler_params=pltpu.CompilerParams(vmem_limit_bytes=limit * MIB),
        cost_estimate=cost,
    )(*[array for _, array in ins])


def start_all(pairs, sems):
    copies = [
        pltpu.make_async_copy(source, target, sems.at[i]) for i, (source, target) in enumerate(pairs)
    ]
    for copy in copies:
        copy.start()
    return copies


def wait_all(copies):
    for copy in copies:
        copy.wait()


class Plan:
    def __init__(self, frames_local, patches_local, frame_ways, patch_ways):
        self.frames_local = frames_local
        self.patches_local = patches_local
        self.frame_ways = frame_ways
        self.patch_ways = patch_ways
        self.devices = frame_ways * patch_ways
        self.tokens = frames_local * patches_local
        self.frames = frames_local * frame_ways
        self.patches = patches_local * patch_ways
        self.items = frames_local * HEADS // patch_ways
        self.groups = HEADS // self.items
        self.width = self.items * HEAD_DIM
        self.window = max(
            -(-((g + 1) * self.width - g * self.width // LANES * LANES) // LANES) * LANES
            for g in range(self.groups)
        )
        self.padded = self.items * LANES
        self.own_patches = patches_local // frame_ways
        self.own_rows = frames_local * self.own_patches
        self.rows = self.frames * self.own_patches
        self.part = min(self.patches, 512)
        self.parts = self.patches // self.part
        self.term_blocks = BLOCK // patch_ways
        self.term_rows = 4 * CHUNKS * self.term_blocks
        self.term_tiles = -(-self.term_rows // TILE)

    def window_start(self, group):
        return min(group * self.width // LANES * LANES, D - self.window)

    def own_window(self):
        group = lax.rem(lax.axis_index("patch"), self.groups)
        start = jnp.minimum(group * self.width // LANES * LANES, D - self.window)
        return pl.multiple_of(start, LANES), group * self.width - start

    def peer(self, distance):
        return lax.axis_index("patch") ^ distance

    def frame_of(self, distance):
        return self.peer(distance) // self.groups

    def other_frame(self, shift):
        return lax.rem(lax.axis_index("frame") + shift, self.frame_ways)


def head_selection(plan, offset):
    lane = lax.broadcasted_iota(jnp.int32, (plan.window, plan.padded), 0)
    target = lax.broadcasted_iota(jnp.int32, (plan.window, plan.padded), 1)
    inner = target % LANES
    source = offset + (target // LANES) * HEAD_DIM + inner
    return jnp.where((lane == source) & (inner < HEAD_DIM), 1.0, 0.0).astype(BF16)


def weight_windows(plan, weight_ref, windows, sems):
    start, _ = plan.own_window()
    return [
        pltpu.make_async_copy(
            weight_ref.at[:, pl.ds(pl.multiple_of(s * D + start, LANES), plan.window)],
            windows.at[:, pl.ds(s * plan.window, plan.window)],
            sems.at[s],
        )
        for s in range(3)
    ]


def pack_kernel(plan, video, cotangent, early_ref):
    own = plan.own_patches
    for t, source in enumerate((video(), cotangent())):
        for z in range(plan.frame_ways):
            for f in range(plan.frames_local):
                early_ref[z, t, f * own : (f + 1) * own, :] = source[
                    f, z * own : (z + 1) * own, :
                ]


def blocks_kernel(*refs):
    mask = diagonal_mask()
    for blocks_ref, out in zip(refs[: len(refs) // 2], refs[len(refs) // 2 :]):
        width = out.ref.shape[2]
        for c in range(CHUNKS):
            tiled = jnp.concatenate([blocks_ref[lanes_of(c), :]] * (LANES // BLOCK), axis=1)
            tile = jnp.where(mask, tiled, 0.0).astype(BF16)
            for k in range(width // LANES):
                here = c % (width // LANES) == k
                out.ref[0, lanes_of(c), lanes_of(k)] = tile if here else jnp.zeros_like(tile)
        out.flush(0)


def spatial_forward_kernel(plan, *refs):
    pieces = refs[: plan.patch_ways]
    (
        blocks,
        weight_ref,
        normed_out,
        stack_out,
        weights_out,
        send_ref,
        windows,
        attended,
        sems,
    ) = refs[plan.patch_ways :]
    copies = weight_windows(plan, weight_ref, windows, sems)
    for copy in copies:
        copy.start()
    _, offset = plan.own_window()
    chosen = head_selection(plan, offset)
    size = plan.patches_local
    for r, piece in enumerate(pieces):
        for i in range(0, size, BLOCK):
            normed = normalize(piece[i : i + BLOCK, :].astype(F32))[0].astype(BF16)
            normed_out.ref[0, r * size + i : r * size + i + BLOCK, :] = normed
    normed_out.flush(0)
    rotated = rotate(normed_out.ref[0], blocks().at[0]).astype(BF16)
    stack_ref = stack_out.ref
    wait_all(copies)
    projected = dot(rotated, windows[...]).astype(BF16)
    for s in range(3):
        part = projected[:, s * plan.window : (s + 1) * plan.window]
        stack_ref[s] = dot(part, chosen).astype(BF16)
        stack_out.flush(s)
    for h in range(plan.items):
        queries, keys, values = [stack_ref[s, :, lanes_of(h)] for s in range(3)]
        values_t = values.astype(F32).T.astype(BF16)
        for c in range(plan.parts):
            span = slice(c * plan.part, (c + 1) * plan.part)
            scores = dot_nt(keys, queries[span]) * SCALE
            top = jnp.max(scores, axis=0, keepdims=True)
            raised = jnp.exp(scores - top)
            total = jnp.sum(raised, axis=0, keepdims=True)
            rounded = (raised * (1.0 / total)).astype(BF16)
            weights_out.ref[h * plan.parts + c] = rounded
            weights_out.flush(h * plan.parts + c)
            attended[span, lanes_of(h)] = dot(values_t, rounded).T.astype(BF16)
    own = plan.own_patches
    result = dot_nt(attended[...], chosen).astype(BF16)
    for r in range(plan.patch_ways):
        target = plan.peer(r)
        for z in range(plan.frame_ways):
            start = r * size + z * own
            send_ref[z * plan.patch_ways + target] = result[start : start + own, :]


def order_terms(plan, terms, ordered, first, count):
    share = plan.term_tiles * TILE
    for b in range(BLOCK):
        owner, inner = divmod(b, plan.term_blocks)
        start = owner * share + inner * 4 * CHUNKS + first
        ordered[start : start + count, :] = terms[pl.ds(b, count, stride=BLOCK), :]


def term_kernel(plan, prepared_ref, factors, out, outrot, terms, sems):
    copies = start_all([(prepared_ref.at[1], outrot)], sems)
    mask = diagonal_mask()
    parts = factors()
    rotation_gradient(parts[1], parts[2], mask, terms, CHUNKS)
    rotation_gradient(parts[3], parts[4], mask, terms, 2 * CHUNKS)
    wait_all(copies)
    rotation_gradient(parts[0], outrot[...], mask, terms, 0)
    ordered = out.ref.at[0]
    ordered[...] = jnp.zeros_like(ordered)
    order_terms(plan, terms, ordered, 0, 3 * CHUNKS)
    out.flush(0)


def spatial_backward_kernel(
    plan,
    adjoint_ref,
    stack,
    weights,
    blocks,
    normed,
    term,
    weight_ref,
    even_ref,
    odd_ref,
    windows,
    adjoint,
    grads,
    projected,
    terms,
    sems,
):
    copies = weight_windows(plan, weight_ref, windows, sems)
    for copy in copies:
        copy.start()
    own = plan.own_patches
    for r in range(plan.patch_ways):
        source = plan.peer(r)
        for z in range(plan.frame_ways):
            start = r * plan.patches_local + z * own
            adjoint[start : start + own, :] = adjoint_ref[z * plan.patch_ways + source]
    _, offset = plan.own_window()
    chosen = head_selection(plan, offset)
    upstream_all = dot(adjoint[...], chosen).astype(BF16)
    stack_ref, weights_ref = stack(), weights()
    for h in range(plan.items):
        queries, keys, values = [stack_ref[s, :, lanes_of(h)] for s in range(3)]
        upstream = upstream_all[:, lanes_of(h)]
        keys_t = keys.astype(F32).T.astype(BF16)
        grad_keys = None
        grad_values = None
        for c in range(plan.parts):
            span = slice(c * plan.part, (c + 1) * plan.part)
            rounded = weights_ref[h * plan.parts + c]
            probability = rounded.astype(F32)
            grad_weights = dot_nt(values, upstream[span])
            delta = jnp.sum(probability * grad_weights, axis=0, keepdims=True)
            grad_scores = (probability * (grad_weights - delta)).astype(BF16)
            value_part = dot(rounded, upstream[span])
            key_part = dot(grad_scores, queries[span])
            grad_values = value_part if grad_values is None else grad_values + value_part
            grad_keys = key_part if grad_keys is None else grad_keys + key_part
            grads[0, span, lanes_of(h)] = (dot(keys_t, grad_scores).T * SCALE).astype(BF16)
        grads[1, :, lanes_of(h)] = (grad_keys * SCALE).astype(BF16)
        grads[2, :, lanes_of(h)] = grad_values.astype(BF16)
    for s, copy in enumerate(copies):
        projected[:, s * plan.window : (s + 1) * plan.window] = dot_nt(grads[s], chosen).astype(
            BF16
        )
        copy.wait()
    rotated = dot_nt(projected[...], windows[...]).astype(BF16)
    size = plan.patches_local
    share = plan.term_tiles * TILE
    back = rotate_transposed(rotated, blocks().at[0]).astype(BF16)
    rotation_gradient(normed()[0], rotated, diagonal_mask(), terms, 0, 2 * LANES)
    ordered = term().at[0]
    order_terms(plan, terms, ordered, 3 * CHUNKS, CHUNKS)
    for r in range(plan.patch_ways):
        out_ref = (even_ref, odd_ref)[r % 2].at[r // 2]
        out_ref[0:size, :] = back[r * size : (r + 1) * size, :]
        owned = ordered[pl.ds(pl.multiple_of(plan.peer(r) * share, TILE), share), :].astype(BF16)
        for k in range(CHUNKS):
            if k < plan.term_tiles:
                tile = owned[k * TILE : (k + 1) * TILE, :]
            else:
                tile = jnp.zeros((TILE, LANES), BF16)
            out_ref[size : size + TILE, lanes_of(k)] = tile


def pair_kernel(plan, even_ref, other_ref, *out_refs):
    for s, out_ref in enumerate(out_refs):
        out_ref[...] = (even_ref[s].astype(F32) + other_ref[s].astype(F32)).astype(BF16)


def frame_column(plan, mask_ref):
    frame = lax.broadcasted_iota(jnp.int32, (plan.rows, 1), 0) // plan.own_patches
    valid = jnp.zeros((plan.rows, 1), jnp.int32)
    for f in range(plan.frames):
        valid = jnp.where(frame == f, mask_ref[f], valid)
    return valid


def collect_rows(plan, early_ref, which, target):
    return [
        (early_ref.at[z, which], target.at[pl.ds(z * plan.own_rows, plan.own_rows), :])
        for z in range(plan.frame_ways)
    ]


def top_kernel(plan, early_ref, mask_ref, weight, blocks, out, rows, sems):
    copies = start_all(collect_rows(plan, early_ref, 1, rows), sems)
    valid = frame_column(plan, mask_ref).astype(F32)
    wait_all(copies)
    top = (rows[...].astype(F32) * valid).astype(BF16)
    out.ref[0] = top
    out.flush(0)
    outrot = dot_nt(top, weight()[...]).astype(BF16)
    out.ref[1] = outrot
    out.flush(1)
    out.ref[2] = rotate_transposed(outrot, blocks().at[0]).astype(BF16)
    out.flush(2)


def head_window(h):
    low = h * HEAD_DIM // LANES * LANES
    high = -(-(h + 1) * HEAD_DIM // LANES) * LANES
    return low, high


def head_lanes(h, low, high):
    lane = low + lax.broadcasted_iota(jnp.int32, (1, high - low), 1)
    inside = (lane >= h * HEAD_DIM) & (lane < (h + 1) * HEAD_DIM)
    return jnp.where(inside, 1.0, 0.0).astype(BF16)


def temporal_kernel(plan, *refs):
    (
        early_ref,
        arrived_ref,
        mask_ref,
        outward,
        spatial_output,
        inward,
        project_ref,
        prepared,
        send_ref,
        factors,
    ) = refs[:10]
    leaving = refs[10 : 10 + plan.frame_ways]
    (
        project_weight,
        weight_sems,
        inputs,
        projected,
        weights,
        slopes,
        grads,
        piece_sems,
    ) = refs[10 + plan.frame_ways :]
    piece_copies = start_all(collect_rows(plan, early_ref, 0, inputs), piece_sems)
    weight_copies = start_all(
        [(project_ref.at[pl.ds(*span), :], project_weight.at[pl.ds(*span), :]) for span in SPANS],
        weight_sems,
    )
    own = plan.own_patches
    attended_one = factors.ref.at[3]
    for f in range(plan.frames):
        z, inner = divmod(f, plan.frames_local)
        base = z * plan.patch_ways + inner * plan.groups
        for c in range(CHUNKS):
            tile = None
            for g in range(plan.groups):
                low = c * LANES - plan.window_start(g)
                if 0 <= low < plan.window:
                    part = arrived_ref[base + g, :, low : low + LANES]
                    tile = part if tile is None else tile + part
            attended_one[f * own : (f + 1) * own, lanes_of(c)] = tile
    factors.flush(3)
    outrot_one = rotate(attended_one[...], outward().at[0]).astype(BF16)
    out_weight = spatial_output()
    wait_all(piece_copies)
    hidden = (inputs[...].astype(F32) + dot(outrot_one, out_weight[...])).astype(BF16)
    normed, inverse = normalize(hidden.astype(F32))
    normed_low = normed.astype(BF16)
    factors.ref[1] = normed_low
    factors.flush(1)
    rotated = rotate(normed_low, inward().at[0]).astype(BF16)
    total = None
    for (start, size), copy in zip(SPANS, weight_copies):
        copy.wait()
        span = slice(start, start + size)
        if start == 0:
            prepared.begin()
        part = dot(rotated[:, span], project_weight[span, :])
        total = part if total is None else total + part
    projected[...] = total.astype(BF16)

    key_valid = frame_column(plan, mask_ref) == 1
    shape = (plan.rows, plan.rows)
    key_row = lax.broadcasted_iota(jnp.int32, shape, 0)
    query_row = lax.broadcasted_iota(jnp.int32, shape, 1)
    allowed = (key_row == query_row) | (((key_row % own) == (query_row % own)) & key_valid)
    early = prepared()
    rows = plan.rows
    for h in range(HEADS):
        low, high = head_window(h)
        chosen = head_lanes(h, low, high)
        queries = projected[:, low:high] * chosen
        keys = projected[:, D + low : D + high]
        values = projected[:, 2 * D + low : 2 * D + high]
        upstream = early[2, :, low:high] * chosen
        scores = jnp.where(allowed, dot_nt(keys, queries) * SCALE, NEGATIVE)
        peak = jnp.max(scores, axis=0, keepdims=True)
        raised = jnp.exp(scores - peak)
        total = jnp.sum(raised, axis=0, keepdims=True)
        probability = raised * (1.0 / total)
        weights[h * rows : (h + 1) * rows, :] = probability.astype(BF16)
        grad_weights = dot_nt(values, upstream)
        delta = jnp.sum(probability * grad_weights, axis=0, keepdims=True)
        slope = probability * (grad_weights - delta) * SCALE
        slopes[h * rows : (h + 1) * rows, :] = slope.astype(BF16)

    for c in range(CHUNKS):
        low, high = c * LANES, (c + 1) * LANES
        first, last = low // HEAD_DIM, (high - 1) // HEAD_DIM
        span = slice(first * rows, (last + 1) * rows)
        heads = range(first, last + 1)

        def stacked(tile):
            return jnp.concatenate([tile * head_lanes(h, low, high) for h in heads], axis=0)

        def beside(ref):
            return jnp.concatenate([ref[h * rows : (h + 1) * rows, :] for h in heads], axis=1)

        factors.ref[0, :, low:high] = dot_tn(
            weights[span, :], stacked(projected[:, 2 * D + low : 2 * D + high])
        ).astype(BF16)
        grads[:, low:high] = dot_tn(
            slopes[span, :], stacked(projected[:, D + low : D + high])
        ).astype(BF16)
        grads[:, D + low : D + high] = dot(
            beside(slopes), stacked(projected[:, low:high])
        ).astype(BF16)
        grads[:, 2 * D + low : 2 * D + high] = dot(
            beside(weights), stacked(early[2, :, low:high])
        ).astype(BF16)

    factors.flush(0)
    adjoint_rotated = dot_nt(grads[...], project_weight[...]).astype(BF16)
    factors.ref[2] = adjoint_rotated
    factors.flush(2)
    adjoint_normed = rotate_transposed(adjoint_rotated, inward().at[0])
    adjoint_hidden = early[0].astype(F32) + normalize_backward(adjoint_normed, normed, inverse)
    adjoint_hidden = adjoint_hidden.astype(BF16)
    inputs[...] = adjoint_hidden
    pairs = []
    for shift, piece in enumerate(leaving):
        start = pl.multiple_of(plan.other_frame(shift) * plan.own_rows, plan.own_rows)
        pairs.append((inputs.at[pl.ds(start, plan.own_rows), :], piece))
    piece_copies = start_all(pairs, piece_sems)
    outrot_adjoint = dot_nt(adjoint_hidden, out_weight[...]).astype(BF16)
    factors.ref[4] = outrot_adjoint
    factors.flush(4)
    adjoint_attended = rotate_transposed(outrot_adjoint, outward().at[0]).astype(BF16)
    for f in range(plan.frames):
        z, inner = divmod(f, plan.frames_local)
        base = z * plan.patch_ways + inner * plan.groups
        for g in range(plan.groups):
            start = plan.window_start(g)
            send_ref[base + g] = adjoint_attended[
                f * own : (f + 1) * own, start : start + plan.window
            ]
    wait_all(piece_copies)


def final_kernel(plan, *refs):
    pieces = refs[: plan.frame_ways]
    sums = refs[plan.frame_ways : plan.frame_ways + plan.patch_ways // 2]
    video_ref, video_gradient_ref, hidden = refs[plan.frame_ways + len(sums) :]
    size = plan.patches_local
    own = plan.own_patches
    for shift, piece in enumerate(pieces):
        source = plan.other_frame(plan.frame_ways - shift)
        start = pl.multiple_of(source * own, own)
        for f in range(plan.frames_local):
            hidden[f, pl.ds(start, own), :] = piece[f * own : (f + 1) * own, :]
    each = len(sums) // plan.frames_local
    for i in range(plan.frames_local):
        f = plan.frame_of(2 * i * each)
        normed, inverse = normalize(video_ref[f].astype(F32))
        adjoint = sums[i * each][0:size, :].astype(F32)
        for part in sums[i * each + 1 : (i + 1) * each]:
            adjoint = adjoint + part[0:size, :].astype(F32)
        video_gradient_ref[f] = (
            hidden[f].astype(F32) + normalize_backward(adjoint, normed, inverse)
        ).astype(BF16)


def share_kernel(plan, *refs):
    sums, out_ref = refs[:-1], refs[-1]
    size = plan.patches_local
    added = sums[0][size:, :].astype(F32)
    for part in sums[1:]:
        added = added + part[size:, :].astype(F32)
    out_ref[...] = added.astype(BF16)


def sum_kernel(plan, *refs):
    parts, (out_ref, total, turned) = refs[: plan.frame_ways], refs[plan.frame_ways :]
    added = parts[0][...].astype(F32)
    for part in parts[1:]:
        added = added + part[...].astype(F32)
    for k in range(plan.term_tiles):
        total[k * TILE : (k + 1) * TILE, :] = added[:, lanes_of(k)]
    turned[...] = jnp.zeros_like(turned)
    for b in range(plan.term_blocks):
        base = b * 4 * CHUNKS
        for i in range(LANES // BLOCK):
            turned[base + i * CHUNKS : base + (i + 1) * CHUNKS, :] = jnp.concatenate(
                [
                    total[
                        base + t * CHUNKS : base + (t + 1) * CHUNKS, i * BLOCK : (i + 1) * BLOCK
                    ]
                    for t in range(4)
                ],
                axis=1,
            )
    out_ref[...] = turned[...].astype(BF16)


def unpack_kernel(plan, scaling, *refs):
    pieces = refs[: plan.patch_ways]
    out_refs, wide = refs[plan.patch_ways : plan.patch_ways + 4], refs[plan.patch_ways + 4]
    blocks = 4 * CHUNKS
    row = lax.broadcasted_iota(jnp.int32, (blocks, blocks), 0)
    column = lax.broadcasted_iota(jnp.int32, (blocks, blocks), 1)
    order = (row % CHUNKS) * (LANES // BLOCK) + row // CHUNKS
    chosen = jnp.where(order == column, 1.0, 0.0).astype(BF16)
    for r, piece in enumerate(pieces):
        wide[r] = piece[...].astype(F32)
        for inner in range(plan.term_blocks):
            rows = wide[r, inner * blocks : (inner + 1) * blocks, :].astype(BF16)
            turned = dot_tn(rows, chosen) * scaling
            b = plan.peer(r) * plan.term_blocks + inner
            for t, out_ref in enumerate(out_refs):
                out_ref[b] = turned[t * BLOCK : (t + 1) * BLOCK, :]


def estimate(flops, moved):
    return pl.CostEstimate(flops=int(flops), bytes_accessed=int(moved), transcendentals=0)


def per_device(
    video,
    cotangent,
    frame_mask,
    spatial_project,
    spatial_output,
    temporal_project,
    temporal_output,
    spatial_inward,
    spatial_outward,
    temporal_inward,
    temporal_outward,
):
    plan = Plan(video.shape[0], video.shape[1], lax.axis_size("frame"), lax.axis_size("patch"))
    shape = jax.ShapeDtypeStruct
    both = ("frame", "patch")
    dma = pltpu.SemaphoreType.DMA
    exchange = lambda rows, axis: lax.all_to_all(rows, axis, 0, 0, tiled=True)
    mode = lambda kind, arrays: [(kind, array) for array in arrays]

    def shifted(pieces):
        ways = plan.frame_ways
        return [pieces[0]] + [
            lax.ppermute(pieces[s], "frame", [(i, (i + s) % ways) for i in range(ways)])
            for s in range(1, ways)
        ]

    half = plan.patch_ways // 2
    part_shape = shape((plan.patches_local + TILE, D), BF16)
    item_shape = shape((plan.devices, plan.own_patches, plan.window), BF16)

    def swap(rows, distance):
        pairs = [(p, p ^ distance) for p in range(plan.patch_ways)]
        return lax.ppermute(rows, "patch", pairs)

    own, *chips = [
        lax.dynamic_index_in_dim(video, plan.frame_of(distance), 0, keepdims=False)
        for distance in range(0, plan.patch_ways, 2)
    ]
    chips = [swap(rows, 2 * s) for s, rows in enumerate(chips, 1)]
    (early,) = call(
        functools.partial(pack_kernel, plan),
        mode("l", [video, cotangent]),
        [("v", shape((plan.frame_ways, 2, plan.own_rows, D), BF16))],
        limit=16,
    )
    def diagonals(width, *stacks):
        return call(
            blocks_kernel,
            mode("v", [blocks.reshape(D, BLOCK) for blocks in stacks]),
            mode("d", [shape((1, D, width), BF16)] * len(stacks)),
            limit=60,
        )

    (spatial_inward,) = diagonals(2 * LANES, spatial_inward)
    early = exchange(early, "frame")
    chips, spatial_inward = lax.optimization_barrier((chips, spatial_inward))
    gathered = [rows for piece in [own] + chips for rows in (piece, swap(piece, 1))]

    normed, stack, weights, send = call(
        functools.partial(spatial_forward_kernel, plan),
        mode("v", gathered) + [("l", spatial_inward), ("h", spatial_project)],
        [
            ("d", shape((1, plan.patches, D), BF16)),
            ("d", shape((3, plan.patches, plan.padded), BF16)),
            ("d", shape((plan.items * plan.parts, plan.patches, plan.part), BF16)),
            ("v", item_shape),
        ],
        [
            pltpu.VMEM((D, 3 * plan.window), BF16),
            pltpu.VMEM((plan.patches, plan.padded), BF16),
            dma((3,)),
        ],
        cost=estimate(8 * plan.items * plan.patches**2 * LANES, 8e6),
    )
    send, early, *stacks = lax.optimization_barrier(
        (send, early, spatial_outward, temporal_inward, temporal_outward)
    )
    arrived = exchange(send, both)
    spatial_outward, temporal_inward, temporal_outward = diagonals(LANES, *stacks)

    (prepared,) = call(
        functools.partial(top_kernel, plan),
        [("h", early), ("s", frame_mask), ("l", temporal_output), ("l", temporal_outward)],
        [("d", shape((3, plan.rows, D), BF16))],
        [pltpu.VMEM((plan.rows, D), BF16), dma((plan.frame_ways,))],
        cost=estimate(2 * plan.rows * D * D, 4e6),
    )

    send, factors, *leaving = call(
        functools.partial(temporal_kernel, plan),
        [
            ("h", early),
            ("v", arrived),
            ("s", frame_mask),
            ("l", spatial_outward),
            ("l", spatial_output),
            ("l", temporal_inward),
            ("h", temporal_project),
            ("p", prepared),
        ],
        [("v", item_shape), ("d", shape((5, plan.rows, D), BF16))]
        + mode("h", [shape((plan.own_rows, D), BF16)] * plan.frame_ways),
        [
            pltpu.VMEM((D, 3 * D), BF16),
            dma((len(SPANS),)),
            pltpu.VMEM((plan.rows, D), BF16),
            pltpu.VMEM((plan.rows, 3 * D), BF16),
            pltpu.VMEM((HEADS * plan.rows, plan.rows), BF16),
            pltpu.VMEM((HEADS * plan.rows, plan.rows), BF16),
            pltpu.VMEM((plan.rows, 3 * D), BF16),
            dma((plan.frame_ways,)),
        ],
        cost=estimate(16 * plan.rows * D * D, 12e6),
    )
    adjoint_items = exchange(send, both)
    ordered_shape = shape((plan.patch_ways * plan.term_tiles * TILE, LANES), F32)
    (terms,) = call(
        functools.partial(term_kernel, plan),
        [("h", prepared), ("l", factors)],
        [("d", shape((1,) + ordered_shape.shape, F32))],
        [
            pltpu.VMEM((plan.rows, D), BF16),
            pltpu.VMEM((3 * CHUNKS * BLOCK, LANES), F32),
            dma((1,)),
        ],
        cost=estimate(1e9, 4e6),
    )

    adjoint_items, terms = lax.optimization_barrier((adjoint_items, terms))
    even, odd = call(
        functools.partial(spatial_backward_kernel, plan),
        [
            ("v", adjoint_items),
            ("l", stack),
            ("l", weights),
            ("l", spatial_inward),
            ("l", normed),
            ("l", terms),
            ("h", spatial_project),
        ],
        mode("v", [shape((half,) + part_shape.shape, BF16)] * 2),
        [
            pltpu.VMEM((D, 3 * plan.window), BF16),
            pltpu.VMEM((plan.patches, plan.window), BF16),
            pltpu.VMEM((3, plan.patches, plan.padded), BF16),
            pltpu.VMEM((plan.patches, 3 * plan.window), BF16),
            pltpu.VMEM((CHUNKS * BLOCK, LANES), F32),
            dma((3,)),
        ],
        limit=52,
        cost=estimate(1e10, 8e6),
    )
    other = swap(odd, 1)
    sums = call(
        functools.partial(pair_kernel, plan),
        mode("v", [even, other]),
        mode("v", [part_shape] * half),
        limit=16,
    )
    sums = [swap(part, 2 * s) if s else part for s, part in enumerate(sums)]
    sums[1], leaving = lax.optimization_barrier((sums[1], leaving))
    leaving = shifted(leaving)
    (share,) = call(
        functools.partial(share_kernel, plan),
        mode("v", sums),
        [("v", shape((TILE, D), BF16))],
        limit=16,
    )
    shares = shifted([share] * plan.frame_ways)

    (video_gradient,) = call(
        functools.partial(final_kernel, plan),
        mode("v", leaving) + mode("v", sums) + [("v", video)],
        [("v", shape(video.shape, BF16))],
        [pltpu.VMEM(video.shape, BF16)],
        limit=16,
        cost=estimate(2e9, 3e6),
    )

    shares, video_gradient = lax.optimization_barrier((shares, video_gradient))
    share_shape = shape((plan.term_tiles * TILE, LANES), BF16)
    (send,) = call(
        functools.partial(sum_kernel, plan),
        mode("v", shares),
        [("v", share_shape)],
        [pltpu.VMEM(share_shape.shape, F32)] * 2,
        limit=16,
    )
    shared = [swap(send, r) if r else send for r in range(0, plan.patch_ways, 2)]
    shared = [rows for piece in shared for rows in (piece, swap(piece, 1))]
    scaling = 1.0 / math.sqrt(plan.tokens * plan.devices)
    block_shape = shape((BLOCK, BLOCK, D // BLOCK), F32)
    tout, tin, sout, sin = [
        blocks.transpose(2, 0, 1)
        for blocks in call(
            functools.partial(unpack_kernel, plan, scaling),
            mode("v", shared),
            mode("v", [block_shape] * 4),
            [pltpu.VMEM((plan.patch_ways,) + share_shape.shape, F32)],
            limit=16,
        )
    ]
    return (video_gradient, sin, sout, tin, tout)


def solution(mesh):
    in_specs = (P("frame", "patch", None), P("frame", "patch", None)) + (P(),) * 9
    out_specs = (P("frame", "patch", None), P(), P(), P(), P())
    return jax.shard_map(
        per_device, mesh=mesh, in_specs=in_specs, out_specs=out_specs, check_vma=False
    )
```

profile of v0, /device:TPU:0, one launch (start us, length us, event | category | flops | bytes accessed | tf_op | source)
XLA Modules:
  0.0 128.8 jit_solution(1035579604288360812)
XLA Ops:
  3.6 6.3 %all-to-all-start = ((bf16[4,2,32,1152]{3,2,1,0:T(8,128)(2,1)}), bf16[4,2,32,1152]{3,2,1,0:T(8,128)(2,1)S(1)}, u32[]{:S(2)}, u32[]{:S(2)}) async-start(bf16[4,2,32,1152]{3,2,1,0:T(8,128)(2,1)} %shard_map.148), calls=%async_computation | async-start | bytes 1179648 | tf_op jit(solution)/shard_map/all_to_all | solution.py:707
  10.0 2.5 %collective-permute-start.3 = (bf16[64,1152]{1,0:T(8,128)(2,1)S(1)}, bf16[64,1152]{1,0:T(8,128)(2,1)S(1)}, u32[]{:S(2)}, u32[]{:S(2)}) collective-permute-start(bf16[64,1152]{1,0:T(8,128)(2,1)S(1)} %get-tuple-element.93), channel_id=1, source_target_pairs={{0,6},{1,7},{2,4},{3,5},{4,2},{5,3},{6,0},{7,1},{8,14},{9,15},{10,... | collective-permute-start | bytes 442376 | tf_op jit(solution)/shard_map/ppermute | solution.py:723
  14.9 2.3 %shard_map.146.refs_8_.refs_3_ = bf16[1,1152,256]{2,1,0:T(8,128)(2,1)} custom-call(f32[1152,32]{1,0:T(8,128)} %bitcast.19), custom_call_target="tpu_custom_call" | custom-call | tf_op jit(solution)/shard_map/pallas_call | solution.py:163
  17.2 2.2 %collective-permute-done.2.refs_4_ = bf16[64,1152]{1,0:T(8,128)(2,1)S(1)} collective-permute-done((bf16[64,1152]{1,0:T(8,128)(2,1)S(1)}, bf16[64,1152]{1,0:T(8,128)(2,1)S(1)}, u32[]{:S(2)}, u32[]{:S(2)}) %collective-permute-start.2) | collective-permute-done | bytes 147488 | tf_op jit(solution)/shard_map/ppermute | solution.py:723
  22.3 10.1 %shard_map.147 = (bf16[1,512,1152]{2,1,0:T(8,128)(2,1)}, bf16[3,512,512]{2,1,0:T(8,128)(2,1)}, bf16[4,512,512]{2,1,0:T(8,128)(2,1)}, bf16[32,16,384]{2,1,0:T(8,128)(2,1)}) custom-call(bf16[64,1152]{1,0:T(8,128)(2,1)} %copy-done.9, bf16[64,1152]{1,0:T(8,128)(2,1)} %copy-done.17, bf16[64,1152]{1,0:T(8,128)(2,1)} %copy-done.16, bf16[64,1152]{1,0:T(8,128)(2,1)} %copy-done.18, ...), custom_call_target="tpu_custom_call" | custom-call | flops 1073741824 | bytes 8000000 | tf_op jit(solution)/shard_map/pallas_call | solution.py:163
  32.5 5.3 %all-to-all-start.1 = ((bf16[32,16,384]{2,1,0:T(8,128)(2,1)}), bf16[32,16,384]{2,1,0:T(8,128)(2,1)S(1)}, u32[]{:S(2)}, u32[]{:S(2)}) async-start(bf16[32,16,384]{2,1,0:T(8,128)(2,1)} %get-tuple-element.55), calls=%async_computation.1 | async-start | bytes 786432 | tf_op jit(solution)/shard_map/all_to_all | solution.py:707
  41.8 2.9 %shard_map.149 = (bf16[1,1152,128]{2,1,0:T(8,128)(2,1)}, bf16[1,1152,128]{2,1,0:T(8,128)(2,1)}, bf16[1,1152,128]{2,1,0:T(8,128)(2,1)}) custom-call(f32[1152,32]{1,0:T(8,128)} %bitcast.16, f32[1152,32]{1,0:T(8,128)} %bitcast.17, f32[1152,32]{1,0:T(8,128)} %bitcast.18), custom_call_target="tpu_custom_call" | custom-call | tf_op jit(solution)/shard_map/pallas_call | solution.py:163
  44.7 4.8 %shard_map.150.refs_7_.refs_0_ = bf16[3,128,1152]{2,1,0:T(8,128)(2,1)} custom-call(bf16[4,2,32,1152]{3,2,1,0:T(8,128)(2,1)} %copy-done.7, s32[8]{0:T(128)} %refs_2_.3, bf16[1152,1152]{1,0:T(8,128)(2,1)} %refs_2_.2, bf16[1,1152,128]{2,1,0:T(8,128)(2,1)} %get-tuple-element.61.refs_3_), custom_call_target="tpu_custom_call" | custom-call | flops 339738624 | bytes 4000000 | tf_op jit(solution)/shard_map/pallas_call | solution.py:163
  51.5 14.8 %shard_map.151 = (bf16[32,16,384]{2,1,0:T(8,128)(2,1)}, bf16[5,128,1152]{2,1,0:T(8,128)(2,1)}, bf16[32,1152]{1,0:T(8,128)(2,1)}, bf16[32,1152]{1,0:T(8,128)(2,1)...) custom-call(bf16[4,2,32,1152]{3,2,1,0:T(8,128)(2,1)} %copy-done.7, bf16[32,16,384]{2,1,0:T(8,128)(2,1)} %copy-done.8, ...), custom_call_target="tpu_custom_call" | custom-call | flops 2717908992 | bytes 12000000 | tf_op jit(solution)/shard_map/pallas_call | solution.py:163
  66.3 4.6 %all-to-all-start.2 = ((bf16[32,16,384]{2,1,0:T(8,128)(2,1)}), bf16[32,16,384]{2,1,0:T(8,128)(2,1)S(1)}, u32[]{:S(2)}, u32[]{:S(2)}) async-start(bf16[32,16,384]{2,1,0:T(8,128)(2,1)} %get-tuple-element.62), calls=%async_computation.2 | async-start | bytes 786432 | tf_op jit(solution)/shard_map/all_to_all | solution.py:707
  71.0 3.2 %shard_map.152.refs_5_ = f32[1,1152,128]{2,1,0:T(8,128)} custom-call(bf16[3,128,1152]{2,1,0:T(8,128)(2,1)} %shard_map.150.refs_7_.refs_0_, bf16[5,128,1152]{2,1,0:T(8,128)(2,1)} %get-tuple-element.63.refs_1_), custom_call_target="tpu_custom_call" | custom-call | flops 1000000000 | bytes 4000000 | tf_op jit(solution)/shard_map/pallas_call | solution.py:163
  74.1 9.8 %all-to-all-done.2.refs_0_ = bf16[32,16,384]{2,1,0:T(8,128)(2,1)S(1)} async-done(((bf16[32,16,384]{2,1,0:T(8,128)(2,1)}), bf16[32,16,384]{2,1,0:T(8,128)(2,1)S(1)}, u32[]{:S(2)}, u32[]{:S(2)}) %all-to-all-start.2) | async-done | bytes 393248 | tf_op jit(solution)/shard_map/all_to_all | solution.py:707
  85.0 10.6 %shard_map.153 = (bf16[4,80,1152]{2,1,0:T(8,128)(2,1)}, bf16[4,80,1152]{2,1,0:T(8,128)(2,1)}) custom-call(bf16[32,16,384]{2,1,0:T(8,128)(2,1)S(1)} %all-to-all-done.2.refs_0_, bf16[3,512,512]{2,1,0:T(8,128)(2,1)} %get-tuple-element.65.refs_1_, bf16[4,512,512]{2,1,0:T(8,128)(2,1)} %get-tuple-element.66.refs_2_, bf16[1,1152,256]{2,1,0:T(8,128)(2,1)S(1)} %copy-done.2, ...), custom_call_target="tpu_custom_call" | custom-call | flops 10000000000 | bytes 8000000 | tf_op jit(solution)/shard_map/pallas_call | solution.py:163
  95.6 2.4 %collective-permute-done.7.refs_1_ = bf16[4,80,1152]{2,1,0:T(8,128)(2,1)S(1)} collective-permute-done((bf16[4,80,1152]{2,1,0:T(8,128)(2,1)}, bf16[4,80,1152]{2,1,0:T(8,128)(2,1)S(1)}, u32[]{:S(2)}, u32[]{:S(2)}) %collective-permute-start.7) | collective-permute-done | bytes 737312 | tf_op jit(solution)/shard_map/ppermute | solution.py:723
  100.0 1.4 %collective-permute-start.9 = (bf16[80,1152]{1,0:T(8,128)(2,1)S(1)}, bf16[80,1152]{1,0:T(8,128)(2,1)S(1)}, u32[]{:S(2)}, u32[]{:S(2)}) collective-permute-start(bf16[80,1152]{1,0:T(8,128)(2,1)S(1)} %get-tuple-element.78), channel_id=1, source_target_pairs={{0,4},{1,5},{2,6},{3,7},{4,0},{5,1},{6,2},{7,3},{8,12},{9,13},{10,... | collective-permute-start | bytes 552968 | tf_op jit(solution)/shard_map/ppermute | solution.py:723
  101.4 1.5 %collective-permute-start.10 = (bf16[80,1152]{1,0:T(8,128)(2,1)S(1)}, bf16[80,1152]{1,0:T(8,128)(2,1)S(1)}, u32[]{:S(2)}, u32[]{:S(2)}) collective-permute-start(bf16[80,1152]{1,0:T(8,128)(2,1)S(1)} %get-tuple-element.79), channel_id=1, source_target_pairs={{0,6},{1,7},{2,4},{3,5},{4,2},{5,3},{6,0},{7,1},{8,14},{9,15},{10,... | collective-permute-start | bytes 552968 | tf_op jit(solution)/shard_map/ppermute | solution.py:723
  102.9 4.0 %collective-permute-done.8.refs_1_.refs_5_ = bf16[80,1152]{1,0:T(8,128)(2,1)S(1)} collective-permute-done((bf16[80,1152]{1,0:T(8,128)(2,1)S(1)}, bf16[80,1152]{1,0:T(8,128)(2,1)S(1)}, u32[]{:S(2)}, u32[]{:S(2)}) %collective-permute-start.8) | collective-permute-done | bytes 184352 | tf_op jit(solution)/shard_map/ppermute | solution.py:723
  108.6 2.2 %collective-permute-start.16 = (bf16[32,1152]{1,0:T(8,128)(2,1)S(1)}, bf16[32,1152]{1,0:T(8,128)(2,1)S(1)}, u32[]{:S(2)}, u32[]{:S(2)}) collective-permute-start(bf16[32,1152]{1,0:T(8,128)(2,1)S(1)} %copy-done.21), channel_id=1, source_target_pairs={{0,24},{8,0},{16,8},{24,16},{1,25},{9,1},{17,9},{25,17},{2,26},{10... | collective-permute-start | bytes 221192 | tf_op jit(solution)/shard_map/ppermute | solution.py:713
  110.8 1.6 %collective-permute-start.13 = (bf16[16,1152]{1,0:T(8,128)(2,1)S(1)}, bf16[16,1152]{1,0:T(8,128)(2,1)S(1)}, u32[]{:S(2)}, u32[]{:S(2)}) collective-permute-start(bf16[16,1152]{1,0:T(8,128)(2,1)S(1)} %shard_map.155.refs_0_), channel_id=1, source_target_pairs={{0,24},{8,0},{16,8},{24,16},{1,25},{9,1},{17,9},{25,17},{2,26},{10... | collective-permute-start | bytes 110600 | tf_op jit(solution)/shard_map/ppermute | solution.py:713
  113.4 1.4 %collective-permute-start.11 = (bf16[16,1152]{1,0:T(8,128)(2,1)S(1)}, bf16[16,1152]{1,0:T(8,128)(2,1)S(1)}, u32[]{:S(2)}, u32[]{:S(2)}) collective-permute-start(bf16[16,1152]{1,0:T(8,128)(2,1)S(1)} %shard_map.155.refs_0_), channel_id=1, source_target_pairs={{0,8},{8,16},{16,24},{24,0},{1,9},{9,17},{17,25},{25,1},{2,10},{10... | collective-permute-start | bytes 110600 | tf_op jit(solution)/shard_map/ppermute | solution.py:713
  117.2 1.5 %collective-permute-done.12.refs_2_ = bf16[16,1152]{1,0:T(8,128)(2,1)S(1)} collective-permute-done((bf16[16,1152]{1,0:T(8,128)(2,1)S(1)}, bf16[16,1152]{1,0:T(8,128)(2,1)S(1)}, u32[]{:S(2)}, u32[]{:S(2)}) %collective-permute-start.12) | collective-permute-done | bytes 36896 | tf_op jit(solution)/shard_map/ppermute | solution.py:713
  119.4 1.5 %collective-permute-start.22 = (bf16[144,128]{1,0:T(8,128)(2,1)S(1)}, bf16[144,128]{1,0:T(8,128)(2,1)S(1)}, u32[]{:S(2)}, u32[]{:S(2)}) collective-permute-start(bf16[144,128]{1,0:T(8,128)(2,1)S(1)} %shard_map.157.refs_0_), channel_id=1, source_target_pairs={{0,6},{1,7},{2,4},{3,5},{4,2},{5,3},{6,0},{7,1},{8,14},{9,15},{10,... | collective-permute-start | bytes 110600 | tf_op jit(solution)/shard_map/ppermute | solution.py:723
  123.0 1.4 %collective-permute-done.22.refs_6_ = bf16[144,128]{1,0:T(8,128)(2,1)S(1)} collective-permute-done((bf16[144,128]{1,0:T(8,128)(2,1)S(1)}, bf16[144,128]{1,0:T(8,128)(2,1)S(1)}, u32[]{:S(2)}, u32[]{:S(2)}) %collective-permute-start.22) | collective-permute-done | bytes 36896 | tf_op jit(solution)/shard_map/ppermute | solution.py:723
  127.0 1.8 %shard_map.158 = (f32[32,32,36]{2,1,0:T(8,128)}, f32[32,32,36]{2,1,0:T(8,128)}, f32[32,32,36]{2,1,0:T(8,128)}, f32[32,32,36]{2,1,0:T(8,128)}) custom-call(bf16[144,128]{1,0:T(8,128)(2,1)S(1)} %shard_map.157.refs_0_, bf16[144,128]{1,0:T(8,128)(2,1)S(1)} %collective-permute-done.17.refs_1_, bf16[144,128]{1,0:T(8,128)(2,1)S(1)} %collective-permute-done.18.refs_2_, ...), custom_call_target="tpu_custom_call" | custom-call | tf_op jit(solution)/shard_map/pallas_call | solution.py:163
  (96 shorter events, 28.0 us)
Async XLA Ops:
  3.6 28.9 %all-to-all-start = ((bf16[4,2,32,1152]{3,2,1,0:T(8,128)(2,1)}), bf16[4,2,32,1152]{3,2,1,0:T(8,128)(2,1)S(1)}, u32[]{:S(2)}, u32[]{:S(2)}) async-start(bf16[4,2,32,1152]{3,2,1,0:T(8,128)(2,1)} %shard_map.148), calls=%async_computation | async-start | bytes 1179648 | tf_op jit(solution)/shard_map/all_to_all | solution.py:707
  10.0 7.2 %collective-permute-start.3 = (bf16[64,1152]{1,0:T(8,128)(2,1)S(1)}, bf16[64,1152]{1,0:T(8,128)(2,1)S(1)}, u32[]{:S(2)}, u32[]{:S(2)}) collective-permute-start(bf16[64,1152]{1,0:T(8,128)(2,1)S(1)} %get-tuple-element.93), channel_id=1, source_target_pairs={{0,6},{1,7},{2,4},{3,5},{4,2},{5,3},{6,0},{7,1},{8,14},{9,15},{10,... | collective-permute-start | bytes 442376 | tf_op jit(solution)/shard_map/ppermute | solution.py:723
  12.5 6.9 %collective-permute-start.2 = (bf16[64,1152]{1,0:T(8,128)(2,1)S(1)}, bf16[64,1152]{1,0:T(8,128)(2,1)S(1)}, u32[]{:S(2)}, u32[]{:S(2)}) collective-permute-start(bf16[64,1152]{1,0:T(8,128)(2,1)S(1)} %get-tuple-element.94), channel_id=1, source_target_pairs={{0,4},{1,5},{2,6},{3,7},{4,0},{5,1},{6,2},{7,3},{8,12},{9,13},{10,... | collective-permute-start | bytes 442376 | tf_op jit(solution)/shard_map/ppermute | solution.py:723
  13.0 6.5 %collective-permute-start.1 = (bf16[64,1152]{1,0:T(8,128)(2,1)S(1)}, bf16[64,1152]{1,0:T(8,128)(2,1)S(1)}, u32[]{:S(2)}, u32[]{:S(2)}) collective-permute-start(bf16[64,1152]{1,0:T(8,128)(2,1)S(1)} %get-tuple-element.95), channel_id=1, source_target_pairs={{0,2},{1,3},{2,0},{3,1},{4,6},{5,7},{6,4},{7,5},{8,10},{9,11},{10,... | collective-permute-start | bytes 442376 | tf_op jit(solution)/shard_map/ppermute | solution.py:723
  13.5 6.5 %collective-permute-start = (bf16[64,1152]{1,0:T(8,128)(2,1)S(1)}, bf16[64,1152]{1,0:T(8,128)(2,1)S(1)}, u32[]{:S(2)}, u32[]{:S(2)}) collective-permute-start(bf16[64,1152]{1,0:T(8,128)(2,1)S(1)} %get-tuple-element.96.refs_0_), channel_id=1, source_target_pairs={{0,1},{1,0},{2,3},{3,2},{4,5},{5,4},{6,7},{7,6},{8,9},{9,8},{10,11... | collective-permute-start | bytes 442376 | tf_op jit(solution)/shard_map/ppermute | solution.py:723
  19.5 1.4 %collective-permute-start.4 = (bf16[64,1152]{1,0:T(8,128)(2,1)S(1)}, bf16[64,1152]{1,0:T(8,128)(2,1)S(1)}, u32[]{:S(2)}, u32[]{:S(2)}) collective-permute-start(bf16[64,1152]{1,0:T(8,128)(2,1)S(1)} %collective-permute-done.1.refs_2_), channel_id=1, source_target_pairs={{0,1},{1,0},{2,3},{3,2},{4,5},{5,4},{6,7},{7,6},{8,9},{9,8},{10,11... | collective-permute-start | bytes 442376 | tf_op jit(solution)/shard_map/ppermute | solution.py:723
  19.5 1.6 %collective-permute-start.5 = (bf16[64,1152]{1,0:T(8,128)(2,1)S(1)}, bf16[64,1152]{1,0:T(8,128)(2,1)S(1)}, u32[]{:S(2)}, u32[]{:S(2)}) collective-permute-start(bf16[64,1152]{1,0:T(8,128)(2,1)S(1)} %collective-permute-done.2.refs_4_), channel_id=1, source_target_pairs={{0,1},{1,0},{2,3},{3,2},{4,5},{5,4},{6,7},{7,6},{8,9},{9,8},{10,11... | collective-permute-start | bytes 442376 | tf_op jit(solution)/shard_map/ppermute | solution.py:723
  32.5 18.3 %all-to-all-start.1 = ((bf16[32,16,384]{2,1,0:T(8,128)(2,1)}), bf16[32,16,384]{2,1,0:T(8,128)(2,1)S(1)}, u32[]{:S(2)}, u32[]{:S(2)}) async-start(bf16[32,16,384]{2,1,0:T(8,128)(2,1)} %get-tuple-element.55), calls=%async_computation.1 | async-start | bytes 786432 | tf_op jit(solution)/shard_map/all_to_all | solution.py:707
  66.3 17.6 %all-to-all-start.2 = ((bf16[32,16,384]{2,1,0:T(8,128)(2,1)}), bf16[32,16,384]{2,1,0:T(8,128)(2,1)S(1)}, u32[]{:S(2)}, u32[]{:S(2)}) async-start(bf16[32,16,384]{2,1,0:T(8,128)(2,1)} %get-tuple-element.62), calls=%async_computation.2 | async-start | bytes 786432 | tf_op jit(solution)/shard_map/all_to_all | solution.py:707
  95.6 2.5 %collective-permute-start.7 = (bf16[4,80,1152]{2,1,0:T(8,128)(2,1)}, bf16[4,80,1152]{2,1,0:T(8,128)(2,1)S(1)}, u32[]{:S(2)}, u32[]{:S(2)}) collective-permute-start(bf16[4,80,1152]{2,1,0:T(8,128)(2,1)} %get-tuple-element.70), channel_id=1, source_target_pairs={{0,1},{1,0},{2,3},{3,2},{4,5},{5,4},{6,7},{7,6},{8,9},{9,8},{10,11... | collective-permute-start | bytes 2211848 | tf_op jit(solution)/shard_map/ppermute | solution.py:723
  99.3 7.5 %collective-permute-start.8 = (bf16[80,1152]{1,0:T(8,128)(2,1)S(1)}, bf16[80,1152]{1,0:T(8,128)(2,1)S(1)}, u32[]{:S(2)}, u32[]{:S(2)}) collective-permute-start(bf16[80,1152]{1,0:T(8,128)(2,1)S(1)} %get-tuple-element.72), channel_id=1, source_target_pairs={{0,2},{1,3},{2,0},{3,1},{4,6},{5,7},{6,4},{7,5},{8,10},{9,11},{10,... | collective-permute-start | bytes 552968 | tf_op jit(solution)/shard_map/ppermute | solution.py:723
  100.0 10.8 %collective-permute-start.9 = (bf16[80,1152]{1,0:T(8,128)(2,1)S(1)}, bf16[80,1152]{1,0:T(8,128)(2,1)S(1)}, u32[]{:S(2)}, u32[]{:S(2)}) collective-permute-start(bf16[80,1152]{1,0:T(8,128)(2,1)S(1)} %get-tuple-element.78), channel_id=1, source_target_pairs={{0,4},{1,5},{2,6},{3,7},{4,0},{5,1},{6,2},{7,3},{8,12},{9,13},{10,... | collective-permute-start | bytes 552968 | tf_op jit(solution)/shard_map/ppermute | solution.py:723
  101.4 9.4 %collective-permute-start.10 = (bf16[80,1152]{1,0:T(8,128)(2,1)S(1)}, bf16[80,1152]{1,0:T(8,128)(2,1)S(1)}, u32[]{:S(2)}, u32[]{:S(2)}) collective-permute-start(bf16[80,1152]{1,0:T(8,128)(2,1)S(1)} %get-tuple-element.79), channel_id=1, source_target_pairs={{0,6},{1,7},{2,4},{3,5},{4,2},{5,3},{6,0},{7,1},{8,14},{9,15},{10,... | collective-permute-start | bytes 552968 | tf_op jit(solution)/shard_map/ppermute | solution.py:723
  106.9 6.6 %collective-permute-start.14 = (bf16[32,1152]{1,0:T(8,128)(2,1)S(1)}, bf16[32,1152]{1,0:T(8,128)(2,1)S(1)}, u32[]{:S(2)}, u32[]{:S(2)}) collective-permute-start(bf16[32,1152]{1,0:T(8,128)(2,1)S(1)} %copy-done.23), channel_id=1, source_target_pairs={{0,8},{8,16},{16,24},{24,0},{1,9},{9,17},{17,25},{25,1},{2,10},{10... | collective-permute-start | bytes 221192 | tf_op jit(solution)/shard_map/ppermute | solution.py:713
  107.9 8.1 %collective-permute-start.15 = (bf16[32,1152]{1,0:T(8,128)(2,1)S(1)}, bf16[32,1152]{1,0:T(8,128)(2,1)S(1)}, u32[]{:S(2)}, u32[]{:S(2)}) collective-permute-start(bf16[32,1152]{1,0:T(8,128)(2,1)S(1)} %copy-done.22), channel_id=1, source_target_pairs={{0,16},{8,24},{16,0},{24,8},{1,17},{9,25},{17,1},{25,9},{2,18},{10... | collective-permute-start | bytes 221192 | tf_op jit(solution)/shard_map/ppermute | solution.py:713
  108.6 7.5 %collective-permute-start.16 = (bf16[32,1152]{1,0:T(8,128)(2,1)S(1)}, bf16[32,1152]{1,0:T(8,128)(2,1)S(1)}, u32[]{:S(2)}, u32[]{:S(2)}) collective-permute-start(bf16[32,1152]{1,0:T(8,128)(2,1)S(1)} %copy-done.21), channel_id=1, source_target_pairs={{0,24},{8,0},{16,8},{24,16},{1,25},{9,1},{17,9},{25,17},{2,26},{10... | collective-permute-start | bytes 221192 | tf_op jit(solution)/shard_map/ppermute | solution.py:713
  110.8 6.4 %collective-permute-start.13 = (bf16[16,1152]{1,0:T(8,128)(2,1)S(1)}, bf16[16,1152]{1,0:T(8,128)(2,1)S(1)}, u32[]{:S(2)}, u32[]{:S(2)}) collective-permute-start(bf16[16,1152]{1,0:T(8,128)(2,1)S(1)} %shard_map.155.refs_0_), channel_id=1, source_target_pairs={{0,24},{8,0},{16,8},{24,16},{1,25},{9,1},{17,9},{25,17},{2,26},{10... | collective-permute-start | bytes 110600 | tf_op jit(solution)/shard_map/ppermute | solution.py:713
  112.4 6.3 %collective-permute-start.12 = (bf16[16,1152]{1,0:T(8,128)(2,1)S(1)}, bf16[16,1152]{1,0:T(8,128)(2,1)S(1)}, u32[]{:S(2)}, u32[]{:S(2)}) collective-permute-start(bf16[16,1152]{1,0:T(8,128)(2,1)S(1)} %shard_map.155.refs_0_), channel_id=1, source_target_pairs={{0,16},{8,24},{16,0},{24,8},{1,17},{9,25},{17,1},{25,9},{2,18},{10... | collective-permute-start | bytes 110600 | tf_op jit(solution)/shard_map/ppermute | solution.py:713
  113.4 5.8 %collective-permute-start.11 = (bf16[16,1152]{1,0:T(8,128)(2,1)S(1)}, bf16[16,1152]{1,0:T(8,128)(2,1)S(1)}, u32[]{:S(2)}, u32[]{:S(2)}) collective-permute-start(bf16[16,1152]{1,0:T(8,128)(2,1)S(1)} %shard_map.155.refs_0_), channel_id=1, source_target_pairs={{0,8},{8,16},{16,24},{24,0},{1,9},{9,17},{17,25},{25,1},{2,10},{10... | collective-permute-start | bytes 110600 | tf_op jit(solution)/shard_map/ppermute | solution.py:713
  119.4 4.9 %collective-permute-start.22 = (bf16[144,128]{1,0:T(8,128)(2,1)S(1)}, bf16[144,128]{1,0:T(8,128)(2,1)S(1)}, u32[]{:S(2)}, u32[]{:S(2)}) collective-permute-start(bf16[144,128]{1,0:T(8,128)(2,1)S(1)} %shard_map.157.refs_0_), channel_id=1, source_target_pairs={{0,6},{1,7},{2,4},{3,5},{4,2},{5,3},{6,0},{7,1},{8,14},{9,15},{10,... | collective-permute-start | bytes 110600 | tf_op jit(solution)/shard_map/ppermute | solution.py:723
  120.9 4.0 %collective-permute-start.20 = (bf16[144,128]{1,0:T(8,128)(2,1)S(1)}, bf16[144,128]{1,0:T(8,128)(2,1)S(1)}, u32[]{:S(2)}, u32[]{:S(2)}) collective-permute-start(bf16[144,128]{1,0:T(8,128)(2,1)S(1)} %shard_map.157.refs_0_), channel_id=1, source_target_pairs={{0,4},{1,5},{2,6},{3,7},{4,0},{5,1},{6,2},{7,3},{8,12},{9,13},{10,... | collective-permute-start | bytes 110600 | tf_op jit(solution)/shard_map/ppermute | solution.py:723
  121.8 4.0 %collective-permute-start.18 = (bf16[144,128]{1,0:T(8,128)(2,1)S(1)}, bf16[144,128]{1,0:T(8,128)(2,1)S(1)}, u32[]{:S(2)}, u32[]{:S(2)}) collective-permute-start(bf16[144,128]{1,0:T(8,128)(2,1)S(1)} %shard_map.157.refs_0_), channel_id=1, source_target_pairs={{0,2},{1,3},{2,0},{3,1},{4,6},{5,7},{6,4},{7,5},{8,10},{9,11},{10,... | collective-permute-start | bytes 110600 | tf_op jit(solution)/shard_map/ppermute | solution.py:723
  123.0 2.8 %collective-permute-start.17 = (bf16[144,128]{1,0:T(8,128)(2,1)S(1)}, bf16[144,128]{1,0:T(8,128)(2,1)S(1)}, u32[]{:S(2)}, u32[]{:S(2)}) collective-permute-start(bf16[144,128]{1,0:T(8,128)(2,1)S(1)} %shard_map.157.refs_0_), channel_id=1, source_target_pairs={{0,1},{1,0},{2,3},{3,2},{4,5},{5,4},{6,7},{7,6},{8,9},{9,8},{10,11... | collective-permute-start | bytes 110600 | tf_op jit(solution)/shard_map/ppermute | solution.py:723
  124.3 1.5 %collective-permute-start.23 = (bf16[144,128]{1,0:T(8,128)(2,1)S(1)}, bf16[144,128]{1,0:T(8,128)(2,1)S(1)}, u32[]{:S(2)}, u32[]{:S(2)}) collective-permute-start(bf16[144,128]{1,0:T(8,128)(2,1)S(1)} %collective-permute-done.22.refs_6_), channel_id=1, source_target_pairs={{0,1},{1,0},{2,3},{3,2},{4,5},{5,4},{6,7},{7,6},{8,9},{9,8},{10,11... | collective-permute-start | bytes 110600 | tf_op jit(solution)/shard_map/ppermute | solution.py:723
  (27 other events, 229.5 us)
where the time goes:
time: 129 us
  Pallas kernels  52.9 us (41%)
  starting transfers between devices  35 us (27%)
  waiting for transfers between devices  28.7 us (22%)
  local copies, waits for them, and re-layouts  11.3 us (9%)
    pallas_call x13, Pallas kernels, call(): pl.pallas_call(body, out_shape=tuple((out for _, out in outs)), in_specs=...  52.9 us
    all_to_all x3, starting transfers between devices, per_device(): exchange = lambda rows, axis: lax.all_to_all(rows, axis, 0, 0, tiled=True)  16.3 us
    ppermute x18, waiting for transfers between devices, swap(): return lax.ppermute(rows, 'patch', pairs)  14 us
    ppermute x18, starting transfers between devices, swap(): return lax.ppermute(rows, 'patch', pairs)  11.3 us
    all_to_all x3, waiting for transfers between devices, per_device(): exchange = lambda rows, axis: lax.all_to_all(rows, axis, 0, 0, tiled=True)  11.1 us
    ppermute x6, starting transfers between devices, shifted(): lax.ppermute(pieces[s], 'frame', [(i, (i + s) % ways) for i in range(ways)])  7.39 us
    unnamed x49, local copies, waits for them, and re-layouts  7.22 us
    optimization_barrier x3, local copies, waits for them, and re-layouts, per_device(): lax.optimization_barrier((send, early, spatial_outward, temporal_inward,...  3.98 us
  transfers between devices with their start and end apart: 27, of which 18 were waited for; matrix products, arithmetic and copies ran while one was open for 4% of the time, Pallas kernels for 19%

commit v1 on v0

--- a/solution.py
+++ b/solution.py
@@ -63,43 +63,25 @@
     return slice(chunk * LANES, (chunk + 1) * LANES)
 
 
-def diagonal_spans(blocks_ref):
-    width = blocks_ref.shape[1]
-    return [(low, min(width, D - low)) for low in range(0, D, width)]
-
-
 def rotate(rows, blocks_ref):
     return jnp.concatenate(
-        [
-            dot(rows[:, low : low + size], blocks_ref[low : low + size, 0:size])
-            for low, size in diagonal_spans(blocks_ref)
-        ],
-        axis=1,
+        [dot(rows[:, lanes_of(c)], blocks_ref[lanes_of(c), :]) for c in range(CHUNKS)], axis=1
     )
 
 
 def rotate_transposed(rows, blocks_ref):
     return jnp.concatenate(
-        [
-            dot_nt(rows[:, low : low + size], blocks_ref[low : low + size, 0:size])
-            for low, size in diagonal_spans(blocks_ref)
-        ],
-        axis=1,
-    )
-
-
-def rotation_gradient(left, right, mask, term_ref, base, width=LANES):
-    for low in range(0, D, width):
-        span = slice(low, min(low + width, D))
-        product = dot_tn(left[:, span], right[:, span])
-        for inner in range(0, span.stop - low, LANES):
-            tile = slice(inner, inner + LANES)
-            full = jnp.where(mask, product[tile, tile], 0.0)
-            packed = full[0:BLOCK]
-            for i in range(1, LANES // BLOCK):
-                packed = packed + full[i * BLOCK : (i + 1) * BLOCK]
-            start = (base + (low + inner) // LANES) * BLOCK
-            term_ref[start : start + BLOCK, :] = packed
+        [dot_nt(rows[:, lanes_of(c)], blocks_ref[lanes_of(c), :]) for c in range(CHUNKS)], axis=1
+    )
+
+
+def rotation_gradient(left, right, mask, term_ref, base):
+    for c in range(CHUNKS):
+        full = jnp.where(mask, dot_tn(left[:, lanes_of(c)], right[:, lanes_of(c)]), 0.0)
+        packed = full[0:BLOCK]
+        for i in range(1, LANES // BLOCK):
+            packed = packed + full[i * BLOCK : (i + 1) * BLOCK]
+        term_ref[(base + c) * BLOCK : (base + c + 1) * BLOCK, :] = packed
 
 
 class Arriving:
@@ -263,13 +245,9 @@
 def blocks_kernel(*refs):
     mask = diagonal_mask()
     for blocks_ref, out in zip(refs[: len(refs) // 2], refs[len(refs) // 2 :]):
-        width = out.ref.shape[2]
         for c in range(CHUNKS):
             tiled = jnp.concatenate([blocks_ref[lanes_of(c), :]] * (LANES // BLOCK), axis=1)
-            tile = jnp.where(mask, tiled, 0.0).astype(BF16)
-            for k in range(width // LANES):
-                here = c % (width // LANES) == k
-                out.ref[0, lanes_of(c), lanes_of(k)] = tile if here else jnp.zeros_like(tile)
+            out.ref[0, lanes_of(c), :] = jnp.where(mask, tiled, 0.0).astype(BF16)
         out.flush(0)
 
 
@@ -281,11 +259,13 @@
         normed_out,
         stack_out,
         weights_out,
+        inverse_out,
+        attended_out,
         send_ref,
         windows,
-        attended,
         sems,
     ) = refs[plan.patch_ways :]
+    attended = attended_out.ref.at[0]
     copies = weight_windows(plan, weight_ref, windows, sems)
     for copy in copies:
         copy.start()
@@ -313,11 +293,14 @@
             scores = dot_nt(keys, queries[span]) * SCALE
             top = jnp.max(scores, axis=0, keepdims=True)
             raised = jnp.exp(scores - top)
-            total = jnp.sum(raised, axis=0, keepdims=True)
-            rounded = (raised * (1.0 / total)).astype(BF16)
+            inverse = 1.0 / jnp.sum(raised, axis=0, keepdims=True)
+            rounded = raised.astype(BF16)
             weights_out.ref[h * plan.parts + c] = rounded
             weights_out.flush(h * plan.parts + c)
-            attended[span, lanes_of(h)] = dot(values_t, rounded).T.astype(BF16)
+            inverse_out.ref[h * plan.parts + c] = jnp.broadcast_to(inverse, (8, plan.part))
+            attended[span, lanes_of(h)] = (dot(values_t, rounded) * inverse).T.astype(BF16)
+    inverse_out.flush(*range(plan.items * plan.parts))
+    attended_out.flush(0)
     own = plan.own_patches
     result = dot_nt(attended[...], chosen).astype(BF16)
     for r in range(plan.patch_ways):
@@ -351,8 +334,10 @@
 
 def spatial_backward_kernel(
     plan,
-    adjoint_ref,
+    adjoint_items,
     stack,
+    inverses,
+    attended,
     weights,
     blocks,
     normed,
@@ -371,6 +356,7 @@
     for copy in copies:
         copy.start()
     own = plan.own_patches
+    adjoint_ref = adjoint_items()
     for r in range(plan.patch_ways):
         source = plan.peer(r)
         for z in range(plan.frame_ways):
@@ -379,7 +365,8 @@
     _, offset = plan.own_window()
     chosen = head_selection(plan, offset)
     upstream_all = dot(adjoint[...], chosen).astype(BF16)
-    stack_ref, weights_ref = stack(), weights()
+    stack_ref, inverse_ref, attended_ref = stack(), inverses(), attended()
+    weights_ref = weights()
     for h in range(plan.items):
         queries, keys, values = [stack_ref[s, :, lanes_of(h)] for s in range(3)]
         upstream = upstream_all[:, lanes_of(h)]
@@ -389,11 +376,14 @@
         for c in range(plan.parts):
             span = slice(c * plan.part, (c + 1) * plan.part)
             rounded = weights_ref[h * plan.parts + c]
-            probability = rounded.astype(F32)
-            grad_weights = dot_nt(values, upstream[span])
-            delta = jnp.sum(probability * grad_weights, axis=0, keepdims=True)
-            grad_scores = (probability * (grad_weights - delta)).astype(BF16)
-            value_part = dot(rounded, upstream[span])
+            inverse = inverse_ref[h * plan.parts + c]
+            wide = upstream[span].astype(F32)
+            scaled = (wide * inverse.T[:, 0:1]).astype(BF16)
+            overlap = (wide * attended_ref[0, span, lanes_of(h)].astype(F32)).T
+            delta = jnp.sum(overlap, axis=0, keepdims=True) * inverse[0:1]
+            grad_weights = dot_nt(values, scaled)
+            grad_scores = (rounded.astype(F32) * (grad_weights - delta)).astype(BF16)
+            value_part = dot(rounded, scaled)
             key_part = dot(grad_scores, queries[span])
             grad_values = value_part if grad_values is None else grad_values + value_part
             grad_keys = key_part if grad_keys is None else grad_keys + key_part
@@ -409,7 +399,7 @@
     size = plan.patches_local
     share = plan.term_tiles * TILE
     back = rotate_transposed(rotated, blocks().at[0]).astype(BF16)
-    rotation_gradient(normed()[0], rotated, diagonal_mask(), terms, 0, 2 * LANES)
+    rotation_gradient(normed()[0], rotated, diagonal_mask(), terms, 0)
     ordered = term().at[0]
     order_terms(plan, terms, ordered, 3 * CHUNKS, CHUNKS)
     for r in range(plan.patch_ways):
@@ -473,7 +463,7 @@
 def temporal_kernel(plan, *refs):
     (
         early_ref,
-        arrived_ref,
+        arrived,
         mask_ref,
         outward,
         spatial_output,
@@ -499,8 +489,10 @@
         [(project_ref.at[pl.ds(*span), :], project_weight.at[pl.ds(*span), :]) for span in SPANS],
         weight_sems,
     )
+    prepared.begin()
     own = plan.own_patches
     attended_one = factors.ref.at[3]
+    arrived_ref = arrived()
     for f in range(plan.frames):
         z, inner = divmod(f, plan.frames_local)
         base = z * plan.patch_ways + inner * plan.groups
@@ -526,8 +518,6 @@
     for (start, size), copy in zip(SPANS, weight_copies):
         copy.wait()
         span = slice(start, start + size)
-        if start == 0:
-            prepared.begin()
         part = dot(rotated[:, span], project_weight[span, :])
         total = part if total is None else total + part
     projected[...] = total.astype(BF16)
@@ -731,33 +721,34 @@
         functools.partial(pack_kernel, plan),
         mode("l", [video, cotangent]),
         [("v", shape((plan.frame_ways, 2, plan.own_rows, D), BF16))],
-        limit=16,
-    )
-    def diagonals(width, *stacks):
+        limit=62,
+    )
+    def diagonals(*stacks):
         return call(
             blocks_kernel,
             mode("v", [blocks.reshape(D, BLOCK) for blocks in stacks]),
-            mode("d", [shape((1, D, width), BF16)] * len(stacks)),
-            limit=60,
+            mode("d", [shape((1, D, LANES), BF16)] * len(stacks)),
+            limit=16,
         )
 
-    (spatial_inward,) = diagonals(2 * LANES, spatial_inward)
+    (spatial_inward,) = diagonals(spatial_inward)
     early = exchange(early, "frame")
     chips, spatial_inward = lax.optimization_barrier((chips, spatial_inward))
     gathered = [rows for piece in [own] + chips for rows in (piece, swap(piece, 1))]
 
-    normed, stack, weights, send = call(
+    normed, stack, weights, inverses, attended, send = call(
         functools.partial(spatial_forward_kernel, plan),
         mode("v", gathered) + [("l", spatial_inward), ("h", spatial_project)],
         [
             ("d", shape((1, plan.patches, D), BF16)),
             ("d", shape((3, plan.patches, plan.padded), BF16)),
             ("d", shape((plan.items * plan.parts, plan.patches, plan.part), BF16)),
+            ("d", shape((plan.items * plan.parts, 8, plan.part), F32)),
+            ("d", shape((1, plan.patches, plan.padded), BF16)),
             ("v", item_shape),
         ],
         [
             pltpu.VMEM((D, 3 * plan.window), BF16),
-            pltpu.VMEM((plan.patches, plan.padded), BF16),
             dma((3,)),
         ],
         cost=estimate(8 * plan.items * plan.patches**2 * LANES, 8e6),
@@ -766,7 +757,7 @@
         (send, early, spatial_outward, temporal_inward, temporal_outward)
     )
     arrived = exchange(send, both)
-    spatial_outward, temporal_inward, temporal_outward = diagonals(LANES, *stacks)
+    spatial_outward, temporal_inward, temporal_outward = diagonals(*stacks)
 
     (prepared,) = call(
         functools.partial(top_kernel, plan),
@@ -780,7 +771,7 @@
         functools.partial(temporal_kernel, plan),
         [
             ("h", early),
-            ("v", arrived),
+            ("l", arrived),
             ("s", frame_mask),
             ("l", spatial_outward),
             ("l", spatial_output),
@@ -820,8 +811,10 @@
     even, odd = call(
         functools.partial(spatial_backward_kernel, plan),
         [
-            ("v", adjoint_items),
+            ("l", adjoint_items),
             ("l", stack),
+            ("l", inverses),
+            ("l", attended),
             ("l", weights),
             ("l", spatial_inward),
             ("l", normed),

time: 129 us -> 128 us (level)
  waiting for transfers between devices: 28.7 us -> 32.5 us
  Pallas kernels: 52.9 us -> 50.4 us
  starting transfers between devices: 35 us -> 33.3 us
  local copies, waits for them, and re-layouts: 11.3 us -> 9.81 us
    pallas_call x13, Pallas kernels: 52.9 us -> 50.4 us  [call(): pl.pallas_call(body, out_shape=tuple((out for _, out in outs)), in_specs=...]
    ppermute x18, waiting for transfers between devices: 14 us -> 16.1 us  [swap(): return lax.ppermute(rows, 'patch', pairs)]
    all_to_all x3, starting transfers between devices: 16.3 us -> 14.6 us  [per_device(): exchange = lambda rows, axis: lax.all_to_all(rows, axis, 0, 0, tiled=True)]
    all_to_all x3, waiting for transfers between devices: 11.1 us -> 12.7 us  [per_device(): exchange = lambda rows, axis: lax.all_to_all(rows, axis, 0, 0, tiled=True)]
  transfers between devices with their start and end apart: 27 -> 27, of which waited for: 18 -> 18; matrix products, arithmetic and copies ran while one was open for 4% -> 3% of each run, Pallas kernels for 19% -> 17%
where the time goes in v1:
time: 128 us; the launch traced here: 127 us
  Pallas kernels  50.4 us (39%)
  starting transfers between devices  33.3 us (26%)
  waiting for transfers between devices  32.5 us (25%)
  local copies, waits for them, and re-layouts  9.81 us (8%)
    pallas_call x13, Pallas kernels, call(): pl.pallas_call(body, out_shape=tuple((out for _, out in outs)), in_specs=...  50.4 us
    ppermute x18, waiting for transfers between devices, swap(): return lax.ppermute(rows, 'patch', pairs)  16.1 us
    all_to_all x3, starting transfers between devices, per_device(): exchange = lambda rows, axis: lax.all_to_all(rows, axis, 0, 0, tiled=True)  14.6 us
    all_to_all x3, waiting for transfers between devices, per_device(): exchange = lambda rows, axis: lax.all_to_all(rows, axis, 0, 0, tiled=True)  12.7 us
    ppermute x18, starting transfers between devices, swap(): return lax.ppermute(rows, 'patch', pairs)  11.3 us
    ppermute x6, starting transfers between devices, shifted(): lax.ppermute(pieces[s], 'frame', [(i, (i + s) % ways) for i in range(ways)])  7.39 us
    unnamed x49, local copies, waits for them, and re-layouts  7 us
    ppermute x6, waiting for transfers between devices, shifted(): lax.ppermute(pieces[s], 'frame', [(i, (i + s) % ways) for i in range(ways)])  3.67 us
  transfers between devices with their start and end apart: 27, of which 18 were waited for; matrix products, arithmetic and copies ran while one was open for 3% of the time, Pallas kernels for 17%

profile of v1, /device:TPU:0, one launch (start us, length us, event | category | flops | bytes accessed | tf_op | source)
XLA Modules:
  0.0 126.9 jit_solution(1933516583397280361)
XLA Ops:
  0.7 2.0 %shard_map.148 = bf16[4,2,32,1152]{3,2,1,0:T(8,128)(2,1)} custom-call(bf16[2,64,1152]{2,1,0:T(8,128)(2,1)} %refs_8_.3, bf16[2,64,1152]{2,1,0:T(8,128)(2,1)} %refs_1_.2), custom_call_target="tpu_custom_call" | custom-call | tf_op jit(solution)/shard_map/pallas_call | solution.py:145
  2.7 6.3 %all-to-all-start = ((bf16[4,2,32,1152]{3,2,1,0:T(8,128)(2,1)}), bf16[4,2,32,1152]{3,2,1,0:T(8,128)(2,1)S(1)}, u32[]{:S(2)}, u32[]{:S(2)}) async-start(bf16[4,2,32,1152]{3,2,1,0:T(8,128)(2,1)} %shard_map.148), calls=%async_computation | async-start | bytes 1179648 | tf_op jit(solution)/shard_map/all_to_all | solution.py:697
  9.1 2.5 %collective-permute-start.3 = (bf16[64,1152]{1,0:T(8,128)(2,1)S(1)}, bf16[64,1152]{1,0:T(8,128)(2,1)S(1)}, u32[]{:S(2)}, u32[]{:S(2)}) collective-permute-start(bf16[64,1152]{1,0:T(8,128)(2,1)S(1)} %get-tuple-element.97), channel_id=1, source_target_pairs={{0,6},{1,7},{2,4},{3,5},{4,2},{5,3},{6,0},{7,1},{8,14},{9,15},{10,... | collective-permute-start | bytes 442376 | tf_op jit(solution)/shard_map/ppermute | solution.py:713
  14.3 1.7 %collective-permute-done.3.refs_6_ = bf16[64,1152]{1,0:T(8,128)(2,1)S(1)} collective-permute-done((bf16[64,1152]{1,0:T(8,128)(2,1)S(1)}, bf16[64,1152]{1,0:T(8,128)(2,1)S(1)}, u32[]{:S(2)}, u32[]{:S(2)}) %collective-permute-start.3) | collective-permute-done | bytes 147488 | tf_op jit(solution)/shard_map/ppermute | solution.py:713
  16.1 2.6 %collective-permute-done.2.refs_4_ = bf16[64,1152]{1,0:T(8,128)(2,1)} collective-permute-done((bf16[64,1152]{1,0:T(8,128)(2,1)S(1)}, bf16[64,1152]{1,0:T(8,128)(2,1)}, u32[]{:S(2)}, u32[]{:S(2)}) %collective-permute-start.2) | collective-permute-done | bytes 147488 | tf_op jit(solution)/shard_map/ppermute | solution.py:713
  21.9 10.4 %shard_map.147 = (bf16[1,512,1152]{2,1,0:T(8,128)(2,1)}, bf16[3,512,512]{2,1,0:T(8,128)(2,1)}, bf16[4,512,512]{2,1,0:T(8,128)(2,1)}, f32[4,8,512]{2,1,0:T(8,128)...) custom-call(bf16[64,1152]{1,0:T(8,128)(2,1)} %copy-done.13, bf16[64,1152]{1,0:T(8,128)(2,1)} %collective-permute-done.refs_1_, ...), custom_call_target="tpu_custom_call" | custom-call | flops 1073741824 | bytes 8000000 | tf_op jit(solution)/shard_map/pallas_call | solution.py:145
  32.3 5.2 %all-to-all-start.1 = ((bf16[32,16,384]{2,1,0:T(8,128)(2,1)}), bf16[32,16,384]{2,1,0:T(8,128)(2,1)S(1)}, u32[]{:S(2)}, u32[]{:S(2)}) async-start(bf16[32,16,384]{2,1,0:T(8,128)(2,1)} %get-tuple-element.57), calls=%async_computation.1 | async-start | bytes 786432 | tf_op jit(solution)/shard_map/all_to_all | solution.py:697
  38.7 1.6 %copy.19 = f32[36,32,32]{2,1,0:T(8,128)S(1)} copy(f32[36,32,32]{0,2,1:T(8,128)} %param.21) | data formatting | bytes 294912 | tf_op jit(solution)/shard_map/optimization_barrier | solution.py:756
  42.9 4.8 %shard_map.150.refs_7_.refs_0_ = bf16[3,128,1152]{2,1,0:T(8,128)(2,1)} custom-call(bf16[4,2,32,1152]{3,2,1,0:T(8,128)(2,1)} %copy-done.11, s32[8]{0:T(128)} %refs_2_.3, bf16[1152,1152]{1,0:T(8,128)(2,1)} %refs_2_.2, bf16[1,1152,128]{2,1,0:T(8,128)(2,1)} %copy-done.6), custom_call_target="tpu_custom_call" | custom-call | flops 339738624 | bytes 4000000 | tf_op jit(solution)/shard_map/pallas_call | solution.py:145
  47.7 2.8 %all-to-all-done.1.refs_1_ = bf16[32,16,384]{2,1,0:T(8,128)(2,1)S(1)} async-done(((bf16[32,16,384]{2,1,0:T(8,128)(2,1)}), bf16[32,16,384]{2,1,0:T(8,128)(2,1)S(1)}, u32[]{:S(2)}, u32[]{:S(2)}) %all-to-all-start.1) | async-done | bytes 393248 | tf_op jit(solution)/shard_map/all_to_all | solution.py:697
  51.3 14.4 %shard_map.151 = (bf16[32,16,384]{2,1,0:T(8,128)(2,1)}, bf16[5,128,1152]{2,1,0:T(8,128)(2,1)}, bf16[32,1152]{1,0:T(8,128)(2,1)}, bf16[32,1152]{1,0:T(8,128)(2,1)...) custom-call(bf16[4,2,32,1152]{3,2,1,0:T(8,128)(2,1)} %copy-done.11, bf16[32,16,384]{2,1,0:T(8,128)(2,1)} %copy-done.12, ...), custom_call_target="tpu_custom_call" | custom-call | flops 2717908992 | bytes 12000000 | tf_op jit(solution)/shard_map/pallas_call | solution.py:145
  65.8 3.1 %all-to-all-start.2 = ((bf16[32,16,384]{2,1,0:T(8,128)(2,1)}), bf16[32,16,384]{2,1,0:T(8,128)(2,1)S(1)}, u32[]{:S(2)}, u32[]{:S(2)}) async-start(bf16[32,16,384]{2,1,0:T(8,128)(2,1)} %get-tuple-element.64), calls=%async_computation.2 | async-start | bytes 786432 | tf_op jit(solution)/shard_map/all_to_all | solution.py:697
  68.9 3.1 %shard_map.152.refs_7_ = f32[1,1152,128]{2,1,0:T(8,128)} custom-call(bf16[3,128,1152]{2,1,0:T(8,128)(2,1)} %shard_map.150.refs_7_.refs_0_, bf16[5,128,1152]{2,1,0:T(8,128)(2,1)} %get-tuple-element.65.refs_1_), custom_call_target="tpu_custom_call" | custom-call | flops 1000000000 | bytes 4000000 | tf_op jit(solution)/shard_map/pallas_call | solution.py:145
  72.0 9.8 %all-to-all-done.2.refs_0_ = bf16[32,16,384]{2,1,0:T(8,128)(2,1)S(1)} async-done(((bf16[32,16,384]{2,1,0:T(8,128)(2,1)}), bf16[32,16,384]{2,1,0:T(8,128)(2,1)S(1)}, u32[]{:S(2)}, u32[]{:S(2)}) %all-to-all-start.2) | async-done | bytes 393248 | tf_op jit(solution)/shard_map/all_to_all | solution.py:697
  82.9 10.8 %shard_map.153 = (bf16[4,80,1152]{2,1,0:T(8,128)(2,1)}, bf16[4,80,1152]{2,1,0:T(8,128)(2,1)}) custom-call(bf16[32,16,384]{2,1,0:T(8,128)(2,1)S(1)} %all-to-all-done.2.refs_0_, bf16[3,512,512]{2,1,0:T(8,128)(2,1)} %get-tuple-element.67.refs_1_, f32[4,8,512]{2,1,0:T(8,128)S(1)} %copy-done.9, bf16[1,512,512]{2,1,0:T(8,128)(2,1)S(1)} %copy-done.7, ...), custom_call_target="tpu_custom_call" | custom-call | flops 10000000000 | bytes 8000000 | tf_op jit(solution)/shard_map/pallas_call | solution.py:145
  93.8 2.4 %collective-permute-done.7.refs_1_ = bf16[4,80,1152]{2,1,0:T(8,128)(2,1)S(1)} collective-permute-done((bf16[4,80,1152]{2,1,0:T(8,128)(2,1)}, bf16[4,80,1152]{2,1,0:T(8,128)(2,1)S(1)}, u32[]{:S(2)}, u32[]{:S(2)}) %collective-permute-start.7) | collective-permute-done | bytes 737312 | tf_op jit(solution)/shard_map/ppermute | solution.py:713
  99.5 1.5 %collective-permute-start.10 = (bf16[80,1152]{1,0:T(8,128)(2,1)S(1)}, bf16[80,1152]{1,0:T(8,128)(2,1)S(1)}, u32[]{:S(2)}, u32[]{:S(2)}) collective-permute-start(bf16[80,1152]{1,0:T(8,128)(2,1)S(1)} %get-tuple-element.83), channel_id=1, source_target_pairs={{0,6},{1,7},{2,4},{3,5},{4,2},{5,3},{6,0},{7,1},{8,14},{9,15},{10,... | collective-permute-start | bytes 552968 | tf_op jit(solution)/shard_map/ppermute | solution.py:713
  101.0 4.0 %collective-permute-done.8.refs_1_.refs_5_ = bf16[80,1152]{1,0:T(8,128)(2,1)S(1)} collective-permute-done((bf16[80,1152]{1,0:T(8,128)(2,1)S(1)}, bf16[80,1152]{1,0:T(8,128)(2,1)S(1)}, u32[]{:S(2)}, u32[]{:S(2)}) %collective-permute-start.8) | collective-permute-done | bytes 184352 | tf_op jit(solution)/shard_map/ppermute | solution.py:713
  106.7 2.2 %collective-permute-start.16 = (bf16[32,1152]{1,0:T(8,128)(2,1)S(1)}, bf16[32,1152]{1,0:T(8,128)(2,1)S(1)}, u32[]{:S(2)}, u32[]{:S(2)}) collective-permute-start(bf16[32,1152]{1,0:T(8,128)(2,1)S(1)} %copy-done.21), channel_id=1, source_target_pairs={{0,24},{8,0},{16,8},{24,16},{1,25},{9,1},{17,9},{25,17},{2,26},{10... | collective-permute-start | bytes 221192 | tf_op jit(solution)/shard_map/ppermute | solution.py:703
  108.9 1.6 %collective-permute-start.13 = (bf16[16,1152]{1,0:T(8,128)(2,1)S(1)}, bf16[16,1152]{1,0:T(8,128)(2,1)S(1)}, u32[]{:S(2)}, u32[]{:S(2)}) collective-permute-start(bf16[16,1152]{1,0:T(8,128)(2,1)S(1)} %shard_map.155.refs_0_), channel_id=1, source_target_pairs={{0,24},{8,0},{16,8},{24,16},{1,25},{9,1},{17,9},{25,17},{2,26},{10... | collective-permute-start | bytes 110600 | tf_op jit(solution)/shard_map/ppermute | solution.py:703
  111.6 1.4 %collective-permute-start.11 = (bf16[16,1152]{1,0:T(8,128)(2,1)S(1)}, bf16[16,1152]{1,0:T(8,128)(2,1)S(1)}, u32[]{:S(2)}, u32[]{:S(2)}) collective-permute-start(bf16[16,1152]{1,0:T(8,128)(2,1)S(1)} %shard_map.155.refs_0_), channel_id=1, source_target_pairs={{0,8},{8,16},{16,24},{24,0},{1,9},{9,17},{17,25},{25,1},{2,10},{10... | collective-permute-start | bytes 110600 | tf_op jit(solution)/shard_map/ppermute | solution.py:703
  115.4 1.5 %collective-permute-done.12.refs_2_ = bf16[16,1152]{1,0:T(8,128)(2,1)S(1)} collective-permute-done((bf16[16,1152]{1,0:T(8,128)(2,1)S(1)}, bf16[16,1152]{1,0:T(8,128)(2,1)S(1)}, u32[]{:S(2)}, u32[]{:S(2)}) %collective-permute-start.12) | collective-permute-done | bytes 36896 | tf_op jit(solution)/shard_map/ppermute | solution.py:703
  117.5 1.5 %collective-permute-start.22 = (bf16[144,128]{1,0:T(8,128)(2,1)S(1)}, bf16[144,128]{1,0:T(8,128)(2,1)S(1)}, u32[]{:S(2)}, u32[]{:S(2)}) collective-permute-start(bf16[144,128]{1,0:T(8,128)(2,1)S(1)} %shard_map.157.refs_0_), channel_id=1, source_target_pairs={{0,6},{1,7},{2,4},{3,5},{4,2},{5,3},{6,0},{7,1},{8,14},{9,15},{10,... | collective-permute-start | bytes 110600 | tf_op jit(solution)/shard_map/ppermute | solution.py:713
  125.1 1.8 %shard_map.158 = (f32[32,32,36]{2,1,0:T(8,128)}, f32[32,32,36]{2,1,0:T(8,128)}, f32[32,32,36]{2,1,0:T(8,128)}, f32[32,32,36]{2,1,0:T(8,128)}) custom-call(bf16[144,128]{1,0:T(8,128)(2,1)S(1)} %shard_map.157.refs_0_, bf16[144,128]{1,0:T(8,128)(2,1)S(1)} %collective-permute-done.17.refs_1_, bf16[144,128]{1,0:T(8,128)(2,1)S(1)} %collective-permute-done.18.refs_2_, ...), custom_call_target="tpu_custom_call" | custom-call | tf_op jit(solution)/shard_map/pallas_call | solution.py:145
  (96 shorter events, 26.9 us)
Async XLA Ops:
  2.7 29.6 %all-to-all-start = ((bf16[4,2,32,1152]{3,2,1,0:T(8,128)(2,1)}), bf16[4,2,32,1152]{3,2,1,0:T(8,128)(2,1)S(1)}, u32[]{:S(2)}, u32[]{:S(2)}) async-start(bf16[4,2,32,1152]{3,2,1,0:T(8,128)(2,1)} %shard_map.148), calls=%async_computation | async-start | bytes 1179648 | tf_op jit(solution)/shard_map/all_to_all | solution.py:697
  9.1 7.0 %collective-permute-start.3 = (bf16[64,1152]{1,0:T(8,128)(2,1)S(1)}, bf16[64,1152]{1,0:T(8,128)(2,1)S(1)}, u32[]{:S(2)}, u32[]{:S(2)}) collective-permute-start(bf16[64,1152]{1,0:T(8,128)(2,1)S(1)} %get-tuple-element.97), channel_id=1, source_target_pairs={{0,6},{1,7},{2,4},{3,5},{4,2},{5,3},{6,0},{7,1},{8,14},{9,15},{10,... | collective-permute-start | bytes 442376 | tf_op jit(solution)/shard_map/ppermute | solution.py:713
  11.6 7.0 %collective-permute-start.2 = (bf16[64,1152]{1,0:T(8,128)(2,1)S(1)}, bf16[64,1152]{1,0:T(8,128)(2,1)}, u32[]{:S(2)}, u32[]{:S(2)}) collective-permute-start(bf16[64,1152]{1,0:T(8,128)(2,1)S(1)} %get-tuple-element.98), channel_id=1, source_target_pairs={{0,4},{1,5},{2,6},{3,7},{4,0},{5,1},{6,2},{7,3},{8,12},{9,13},{10,... | collective-permute-start | bytes 442376 | tf_op jit(solution)/shard_map/ppermute | solution.py:713
  12.1 6.6 %collective-permute-start.1 = (bf16[64,1152]{1,0:T(8,128)(2,1)S(1)}, bf16[64,1152]{1,0:T(8,128)(2,1)}, u32[]{:S(2)}, u32[]{:S(2)}) collective-permute-start(bf16[64,1152]{1,0:T(8,128)(2,1)S(1)} %get-tuple-element.99), channel_id=1, source_target_pairs={{0,2},{1,3},{2,0},{3,1},{4,6},{5,7},{6,4},{7,5},{8,10},{9,11},{10,... | collective-permute-start | bytes 442376 | tf_op jit(solution)/shard_map/ppermute | solution.py:713
  12.6 6.6 %collective-permute-start = (bf16[64,1152]{1,0:T(8,128)(2,1)S(1)}, bf16[64,1152]{1,0:T(8,128)(2,1)}, u32[]{:S(2)}, u32[]{:S(2)}) collective-permute-start(bf16[64,1152]{1,0:T(8,128)(2,1)S(1)} %get-tuple-element.100.refs_0_), channel_id=1, source_target_pairs={{0,1},{1,0},{2,3},{3,2},{4,5},{5,4},{6,7},{7,6},{8,9},{9,8},{10,11... | collective-permute-start | bytes 442376 | tf_op jit(solution)/shard_map/ppermute | solution.py:713
  18.7 1.6 %collective-permute-start.4 = (bf16[64,1152]{1,0:T(8,128)(2,1)}, bf16[64,1152]{1,0:T(8,128)(2,1)S(1)}, u32[]{:S(2)}, u32[]{:S(2)}) collective-permute-start(bf16[64,1152]{1,0:T(8,128)(2,1)} %collective-permute-done.1.refs_2_), channel_id=1, source_target_pairs={{0,1},{1,0},{2,3},{3,2},{4,5},{5,4},{6,7},{7,6},{8,9},{9,8},{10,11... | collective-permute-start | bytes 442376 | tf_op jit(solution)/shard_map/ppermute | solution.py:713
  18.7 1.9 %collective-permute-start.5 = (bf16[64,1152]{1,0:T(8,128)(2,1)}, bf16[64,1152]{1,0:T(8,128)(2,1)S(1)}, u32[]{:S(2)}, u32[]{:S(2)}) collective-permute-start(bf16[64,1152]{1,0:T(8,128)(2,1)} %collective-permute-done.2.refs_4_), channel_id=1, source_target_pairs={{0,1},{1,0},{2,3},{3,2},{4,5},{5,4},{6,7},{7,6},{8,9},{9,8},{10,11... | collective-permute-start | bytes 442376 | tf_op jit(solution)/shard_map/ppermute | solution.py:713
  32.3 18.2 %all-to-all-start.1 = ((bf16[32,16,384]{2,1,0:T(8,128)(2,1)}), bf16[32,16,384]{2,1,0:T(8,128)(2,1)S(1)}, u32[]{:S(2)}, u32[]{:S(2)}) async-start(bf16[32,16,384]{2,1,0:T(8,128)(2,1)} %get-tuple-element.57), calls=%async_computation.1 | async-start | bytes 786432 | tf_op jit(solution)/shard_map/all_to_all | solution.py:697
  65.8 16.0 %all-to-all-start.2 = ((bf16[32,16,384]{2,1,0:T(8,128)(2,1)}), bf16[32,16,384]{2,1,0:T(8,128)(2,1)S(1)}, u32[]{:S(2)}, u32[]{:S(2)}) async-start(bf16[32,16,384]{2,1,0:T(8,128)(2,1)} %get-tuple-element.64), calls=%async_computation.2 | async-start | bytes 786432 | tf_op jit(solution)/shard_map/all_to_all | solution.py:697
  93.7 2.5 %collective-permute-start.7 = (bf16[4,80,1152]{2,1,0:T(8,128)(2,1)}, bf16[4,80,1152]{2,1,0:T(8,128)(2,1)S(1)}, u32[]{:S(2)}, u32[]{:S(2)}) collective-permute-start(bf16[4,80,1152]{2,1,0:T(8,128)(2,1)} %get-tuple-element.74), channel_id=1, source_target_pairs={{0,1},{1,0},{2,3},{3,2},{4,5},{5,4},{6,7},{7,6},{8,9},{9,8},{10,11... | collective-permute-start | bytes 2211848 | tf_op jit(solution)/shard_map/ppermute | solution.py:713
  97.5 7.5 %collective-permute-start.8 = (bf16[80,1152]{1,0:T(8,128)(2,1)S(1)}, bf16[80,1152]{1,0:T(8,128)(2,1)S(1)}, u32[]{:S(2)}, u32[]{:S(2)}) collective-permute-start(bf16[80,1152]{1,0:T(8,128)(2,1)S(1)} %get-tuple-element.76), channel_id=1, source_target_pairs={{0,2},{1,3},{2,0},{3,1},{4,6},{5,7},{6,4},{7,5},{8,10},{9,11},{10,... | collective-permute-start | bytes 552968 | tf_op jit(solution)/shard_map/ppermute | solution.py:713
  98.1 10.8 %collective-permute-start.9 = (bf16[80,1152]{1,0:T(8,128)(2,1)S(1)}, bf16[80,1152]{1,0:T(8,128)(2,1)S(1)}, u32[]{:S(2)}, u32[]{:S(2)}) collective-permute-start(bf16[80,1152]{1,0:T(8,128)(2,1)S(1)} %get-tuple-element.82), channel_id=1, source_target_pairs={{0,4},{1,5},{2,6},{3,7},{4,0},{5,1},{6,2},{7,3},{8,12},{9,13},{10,... | collective-permute-start | bytes 552968 | tf_op jit(solution)/shard_map/ppermute | solution.py:713
  99.5 9.4 %collective-permute-start.10 = (bf16[80,1152]{1,0:T(8,128)(2,1)S(1)}, bf16[80,1152]{1,0:T(8,128)(2,1)S(1)}, u32[]{:S(2)}, u32[]{:S(2)}) collective-permute-start(bf16[80,1152]{1,0:T(8,128)(2,1)S(1)} %get-tuple-element.83), channel_id=1, source_target_pairs={{0,6},{1,7},{2,4},{3,5},{4,2},{5,3},{6,0},{7,1},{8,14},{9,15},{10,... | collective-permute-start | bytes 552968 | tf_op jit(solution)/shard_map/ppermute | solution.py:713
  105.0 6.6 %collective-permute-start.14 = (bf16[32,1152]{1,0:T(8,128)(2,1)S(1)}, bf16[32,1152]{1,0:T(8,128)(2,1)S(1)}, u32[]{:S(2)}, u32[]{:S(2)}) collective-permute-start(bf16[32,1152]{1,0:T(8,128)(2,1)S(1)} %copy-done.23), channel_id=1, source_target_pairs={{0,8},{8,16},{16,24},{24,0},{1,9},{9,17},{17,25},{25,1},{2,10},{10... | collective-permute-start | bytes 221192 | tf_op jit(solution)/shard_map/ppermute | solution.py:703
  106.0 8.1 %collective-permute-start.15 = (bf16[32,1152]{1,0:T(8,128)(2,1)S(1)}, bf16[32,1152]{1,0:T(8,128)(2,1)S(1)}, u32[]{:S(2)}, u32[]{:S(2)}) collective-permute-start(bf16[32,1152]{1,0:T(8,128)(2,1)S(1)} %copy-done.22), channel_id=1, source_target_pairs={{0,16},{8,24},{16,0},{24,8},{1,17},{9,25},{17,1},{25,9},{2,18},{10... | collective-permute-start | bytes 221192 | tf_op jit(solution)/shard_map/ppermute | solution.py:703
  106.7 7.5 %collective-permute-start.16 = (bf16[32,1152]{1,0:T(8,128)(2,1)S(1)}, bf16[32,1152]{1,0:T(8,128)(2,1)S(1)}, u32[]{:S(2)}, u32[]{:S(2)}) collective-permute-start(bf16[32,1152]{1,0:T(8,128)(2,1)S(1)} %copy-done.21), channel_id=1, source_target_pairs={{0,24},{8,0},{16,8},{24,16},{1,25},{9,1},{17,9},{25,17},{2,26},{10... | collective-permute-start | bytes 221192 | tf_op jit(solution)/shard_map/ppermute | solution.py:703
  108.9 6.4 %collective-permute-start.13 = (bf16[16,1152]{1,0:T(8,128)(2,1)S(1)}, bf16[16,1152]{1,0:T(8,128)(2,1)S(1)}, u32[]{:S(2)}, u32[]{:S(2)}) collective-permute-start(bf16[16,1152]{1,0:T(8,128)(2,1)S(1)} %shard_map.155.refs_0_), channel_id=1, source_target_pairs={{0,24},{8,0},{16,8},{24,16},{1,25},{9,1},{17,9},{25,17},{2,26},{10... | collective-permute-start | bytes 110600 | tf_op jit(solution)/shard_map/ppermute | solution.py:703
  110.5 6.3 %collective-permute-start.12 = (bf16[16,1152]{1,0:T(8,128)(2,1)S(1)}, bf16[16,1152]{1,0:T(8,128)(2,1)S(1)}, u32[]{:S(2)}, u32[]{:S(2)}) collective-permute-start(bf16[16,1152]{1,0:T(8,128)(2,1)S(1)} %shard_map.155.refs_0_), channel_id=1, source_target_pairs={{0,16},{8,24},{16,0},{24,8},{1,17},{9,25},{17,1},{25,9},{2,18},{10... | collective-permute-start | bytes 110600 | tf_op jit(solution)/shard_map/ppermute | solution.py:703
  111.6 5.8 %collective-permute-start.11 = (bf16[16,1152]{1,0:T(8,128)(2,1)S(1)}, bf16[16,1152]{1,0:T(8,128)(2,1)S(1)}, u32[]{:S(2)}, u32[]{:S(2)}) collective-permute-start(bf16[16,1152]{1,0:T(8,128)(2,1)S(1)} %shard_map.155.refs_0_), channel_id=1, source_target_pairs={{0,8},{8,16},{16,24},{24,0},{1,9},{9,17},{17,25},{25,1},{2,10},{10... | collective-permute-start | bytes 110600 | tf_op jit(solution)/shard_map/ppermute | solution.py:703
  117.5 4.9 %collective-permute-start.22 = (bf16[144,128]{1,0:T(8,128)(2,1)S(1)}, bf16[144,128]{1,0:T(8,128)(2,1)S(1)}, u32[]{:S(2)}, u32[]{:S(2)}) collective-permute-start(bf16[144,128]{1,0:T(8,128)(2,1)S(1)} %shard_map.157.refs_0_), channel_id=1, source_target_pairs={{0,6},{1,7},{2,4},{3,5},{4,2},{5,3},{6,0},{7,1},{8,14},{9,15},{10,... | collective-permute-start | bytes 110600 | tf_op jit(solution)/shard_map/ppermute | solution.py:713
  119.0 4.0 %collective-permute-start.20 = (bf16[144,128]{1,0:T(8,128)(2,1)S(1)}, bf16[144,128]{1,0:T(8,128)(2,1)S(1)}, u32[]{:S(2)}, u32[]{:S(2)}) collective-permute-start(bf16[144,128]{1,0:T(8,128)(2,1)S(1)} %shard_map.157.refs_0_), channel_id=1, source_target_pairs={{0,4},{1,5},{2,6},{3,7},{4,0},{5,1},{6,2},{7,3},{8,12},{9,13},{10,... | collective-permute-start | bytes 110600 | tf_op jit(solution)/shard_map/ppermute | solution.py:713
  120.0 4.0 %collective-permute-start.18 = (bf16[144,128]{1,0:T(8,128)(2,1)S(1)}, bf16[144,128]{1,0:T(8,128)(2,1)S(1)}, u32[]{:S(2)}, u32[]{:S(2)}) collective-permute-start(bf16[144,128]{1,0:T(8,128)(2,1)S(1)} %shard_map.157.refs_0_), channel_id=1, source_target_pairs={{0,2},{1,3},{2,0},{3,1},{4,6},{5,7},{6,4},{7,5},{8,10},{9,11},{10,... | collective-permute-start | bytes 110600 | tf_op jit(solution)/shard_map/ppermute | solution.py:713
  121.1 2.8 %collective-permute-start.17 = (bf16[144,128]{1,0:T(8,128)(2,1)S(1)}, bf16[144,128]{1,0:T(8,128)(2,1)S(1)}, u32[]{:S(2)}, u32[]{:S(2)}) collective-permute-start(bf16[144,128]{1,0:T(8,128)(2,1)S(1)} %shard_map.157.refs_0_), channel_id=1, source_target_pairs={{0,1},{1,0},{2,3},{3,2},{4,5},{5,4},{6,7},{7,6},{8,9},{9,8},{10,11... | collective-permute-start | bytes 110600 | tf_op jit(solution)/shard_map/ppermute | solution.py:713
  122.5 1.5 %collective-permute-start.23 = (bf16[144,128]{1,0:T(8,128)(2,1)S(1)}, bf16[144,128]{1,0:T(8,128)(2,1)S(1)}, u32[]{:S(2)}, u32[]{:S(2)}) collective-permute-start(bf16[144,128]{1,0:T(8,128)(2,1)S(1)} %collective-permute-done.22.refs_6_), channel_id=1, source_target_pairs={{0,1},{1,0},{2,3},{3,2},{4,5},{5,4},{6,7},{7,6},{8,9},{9,8},{10,11... | collective-permute-start | bytes 110600 | tf_op jit(solution)/shard_map/ppermute | solution.py:713
  (27 other events, 259.7 us)

commit v2 on v1

--- a/solution.py
+++ b/solution.py
@@ -259,13 +259,11 @@
         normed_out,
         stack_out,
         weights_out,
-        inverse_out,
-        attended_out,
         send_ref,
         windows,
+        attended,
         sems,
     ) = refs[plan.patch_ways :]
-    attended = attended_out.ref.at[0]
     copies = weight_windows(plan, weight_ref, windows, sems)
     for copy in copies:
         copy.start()
@@ -273,8 +271,9 @@
     chosen = head_selection(plan, offset)
     size = plan.patches_local
     for r, piece in enumerate(pieces):
+        rows = piece()
         for i in range(0, size, BLOCK):
-            normed = normalize(piece[i : i + BLOCK, :].astype(F32))[0].astype(BF16)
+            normed = normalize(rows[i : i + BLOCK, :].astype(F32))[0].astype(BF16)
             normed_out.ref[0, r * size + i : r * size + i + BLOCK, :] = normed
     normed_out.flush(0)
     rotated = rotate(normed_out.ref[0], blocks().at[0]).astype(BF16)
@@ -293,14 +292,11 @@
             scores = dot_nt(keys, queries[span]) * SCALE
             top = jnp.max(scores, axis=0, keepdims=True)
             raised = jnp.exp(scores - top)
-            inverse = 1.0 / jnp.sum(raised, axis=0, keepdims=True)
-            rounded = raised.astype(BF16)
+            total = jnp.sum(raised, axis=0, keepdims=True)
+            rounded = (raised * (1.0 / total)).astype(BF16)
             weights_out.ref[h * plan.parts + c] = rounded
             weights_out.flush(h * plan.parts + c)
-            inverse_out.ref[h * plan.parts + c] = jnp.broadcast_to(inverse, (8, plan.part))
-            attended[span, lanes_of(h)] = (dot(values_t, rounded) * inverse).T.astype(BF16)
-    inverse_out.flush(*range(plan.items * plan.parts))
-    attended_out.flush(0)
+            attended[span, lanes_of(h)] = dot(values_t, rounded).T.astype(BF16)
     own = plan.own_patches
     result = dot_nt(attended[...], chosen).astype(BF16)
     for r in range(plan.patch_ways):
@@ -336,15 +332,13 @@
     plan,
     adjoint_items,
     stack,
-    inverses,
-    attended,
     weights,
     blocks,
     normed,
     term,
     weight_ref,
-    even_ref,
-    odd_ref,
+    even_out,
+    odd_out,
     windows,
     adjoint,
     grads,
@@ -365,8 +359,7 @@
     _, offset = plan.own_window()
     chosen = head_selection(plan, offset)
     upstream_all = dot(adjoint[...], chosen).astype(BF16)
-    stack_ref, inverse_ref, attended_ref = stack(), inverses(), attended()
-    weights_ref = weights()
+    stack_ref, weights_ref = stack(), weights()
     for h in range(plan.items):
         queries, keys, values = [stack_ref[s, :, lanes_of(h)] for s in range(3)]
         upstream = upstream_all[:, lanes_of(h)]
@@ -376,14 +369,11 @@
         for c in range(plan.parts):
             span = slice(c * plan.part, (c + 1) * plan.part)
             rounded = weights_ref[h * plan.parts + c]
-            inverse = inverse_ref[h * plan.parts + c]
-            wide = upstream[span].astype(F32)
-            scaled = (wide * inverse.T[:, 0:1]).astype(BF16)
-            overlap = (wide * attended_ref[0, span, lanes_of(h)].astype(F32)).T
-            delta = jnp.sum(overlap, axis=0, keepdims=True) * inverse[0:1]
-            grad_weights = dot_nt(values, scaled)
-            grad_scores = (rounded.astype(F32) * (grad_weights - delta)).astype(BF16)
-            value_part = dot(rounded, scaled)
+            probability = rounded.astype(F32)
+            grad_weights = dot_nt(values, upstream[span])
+            delta = jnp.sum(probability * grad_weights, axis=0, keepdims=True)
+            grad_scores = (probability * (grad_weights - delta)).astype(BF16)
+            value_part = dot(rounded, upstream[span])
             key_part = dot(grad_scores, queries[span])
             grad_values = value_part if grad_values is None else grad_values + value_part
             grad_keys = key_part if grad_keys is None else grad_keys + key_part
@@ -398,12 +388,13 @@
     rotated = dot_nt(projected[...], windows[...]).astype(BF16)
     size = plan.patches_local
     share = plan.term_tiles * TILE
-    back = rotate_transposed(rotated, blocks().at[0]).astype(BF16)
     rotation_gradient(normed()[0], rotated, diagonal_mask(), terms, 0)
     ordered = term().at[0]
     order_terms(plan, terms, ordered, 3 * CHUNKS, CHUNKS)
-    for r in range(plan.patch_ways):
-        out_ref = (even_ref, odd_ref)[r % 2].at[r // 2]
+    back = rotate_transposed(rotated, blocks().at[0]).astype(BF16)
+    for r in list(range(1, plan.patch_ways, 2)) + list(range(0, plan.patch_ways, 2)):
+        out = (even_out, odd_out)[r % 2]
+        out_ref = out.ref.at[r // 2]
         out_ref[0:size, :] = back[r * size : (r + 1) * size, :]
         owned = ordered[pl.ds(pl.multiple_of(plan.peer(r) * share, TILE), share), :].astype(BF16)
         for k in range(CHUNKS):
@@ -412,6 +403,7 @@
             else:
                 tile = jnp.zeros((TILE, LANES), BF16)
             out_ref[size : size + TILE, lanes_of(k)] = tile
+        out.flush(r // 2)
 
 
 def pair_kernel(plan, even_ref, other_ref, *out_refs):
@@ -489,7 +481,6 @@
         [(project_ref.at[pl.ds(*span), :], project_weight.at[pl.ds(*span), :]) for span in SPANS],
         weight_sems,
     )
-    prepared.begin()
     own = plan.own_patches
     attended_one = factors.ref.at[3]
     arrived_ref = arrived()
@@ -518,6 +509,8 @@
     for (start, size), copy in zip(SPANS, weight_copies):
         copy.wait()
         span = slice(start, start + size)
+        if start == 0:
+            prepared.begin()
         part = dot(rotated[:, span], project_weight[span, :])
         total = part if total is None else total + part
     projected[...] = total.astype(BF16)
@@ -736,19 +729,18 @@
     chips, spatial_inward = lax.optimization_barrier((chips, spatial_inward))
     gathered = [rows for piece in [own] + chips for rows in (piece, swap(piece, 1))]
 
-    normed, stack, weights, inverses, attended, send = call(
+    normed, stack, weights, send = call(
         functools.partial(spatial_forward_kernel, plan),
-        mode("v", gathered) + [("l", spatial_inward), ("h", spatial_project)],
+        mode("l", gathered) + [("l", spatial_inward), ("h", spatial_project)],
         [
             ("d", shape((1, plan.patches, D), BF16)),
             ("d", shape((3, plan.patches, plan.padded), BF16)),
             ("d", shape((plan.items * plan.parts, plan.patches, plan.part), BF16)),
-            ("d", shape((plan.items * plan.parts, 8, plan.part), F32)),
-            ("d", shape((1, plan.patches, plan.padded), BF16)),
             ("v", item_shape),
         ],
         [
             pltpu.VMEM((D, 3 * plan.window), BF16),
+            pltpu.VMEM((plan.patches, plan.padded), BF16),
             dma((3,)),
         ],
         cost=estimate(8 * plan.items * plan.patches**2 * LANES, 8e6),
@@ -813,15 +805,13 @@
         [
             ("l", adjoint_items),
             ("l", stack),
-            ("l", inverses),
-            ("l", attended),
             ("l", weights),
             ("l", spatial_inward),
             ("l", normed),
             ("l", terms),
             ("h", spatial_project),
         ],
-        mode("v", [shape((half,) + part_shape.shape, BF16)] * 2),
+        mode("d", [shape((half,) + part_shape.shape, BF16)] * 2),
         [
             pltpu.VMEM((D, 3 * plan.window), BF16),
             pltpu.VMEM((plan.patches, plan.window), BF16),

time: 128 us -> 125 us (0.977)
    unnamed x49 -> x45, local copies, waits for them, and re-layouts: 7 us -> 5.84 us
  transfers between devices with their start and end apart: 27 -> 27, of which waited for: 18 -> 18; matrix products, arithmetic and copies ran while one was open for 3% -> 3% of each run, Pallas kernels for 17% -> 16%
where the time goes in v2:
time: 125 us
  Pallas kernels  49.5 us (40%)
  starting transfers between devices  33.1 us (26%)
  waiting for transfers between devices  32.5 us (26%)
  local copies, waits for them, and re-layouts  8.65 us (7%)
    pallas_call x13, Pallas kernels, call(): pl.pallas_call(body, out_shape=tuple((out for _, out in outs)), in_specs=...  49.5 us
    ppermute x18, waiting for transfers between devices, swap(): return lax.ppermute(rows, 'patch', pairs)  16.1 us
    all_to_all x3, starting transfers between devices, per_device(): exchange = lambda rows, axis: lax.all_to_all(rows, axis, 0, 0, tiled=True)  14.4 us
    all_to_all x3, waiting for transfers between devices, per_device(): exchange = lambda rows, axis: lax.all_to_all(rows, axis, 0, 0, tiled=True)  12.7 us
    ppermute x18, starting transfers between devices, swap(): return lax.ppermute(rows, 'patch', pairs)  11.3 us
    ppermute x6, starting transfers between devices, shifted(): lax.ppermute(pieces[s], 'frame', [(i, (i + s) % ways) for i in range(ways)])  7.39 us
    unnamed x45, local copies, waits for them, and re-layouts  5.84 us
    ppermute x6, waiting for transfers between devices, shifted(): lax.ppermute(pieces[s], 'frame', [(i, (i + s) % ways) for i in range(ways)])  3.68 us
  transfers between devices with their start and end apart: 27, of which 18 were waited for; matrix products, arithmetic and copies ran while one was open for 3% of the time, Pallas kernels for 16%

profile of v2, /device:TPU:0, one launch (start us, length us, event | category | flops | bytes accessed | tf_op | source)
XLA Modules:
  0.0 124.6 jit_solution(51316042066741958)
XLA Ops:
  0.7 2.0 %shard_map.148 = bf16[4,2,32,1152]{3,2,1,0:T(8,128)(2,1)} custom-call(bf16[2,64,1152]{2,1,0:T(8,128)(2,1)} %refs_8_.1, bf16[2,64,1152]{2,1,0:T(8,128)(2,1)} %refs_1_.2), custom_call_target="tpu_custom_call" | custom-call | tf_op jit(solution)/shard_map/pallas_call | solution.py:145
  2.7 6.3 %all-to-all-start = ((bf16[4,2,32,1152]{3,2,1,0:T(8,128)(2,1)}), bf16[4,2,32,1152]{3,2,1,0:T(8,128)(2,1)S(1)}, u32[]{:S(2)}, u32[]{:S(2)}) async-start(bf16[4,2,32,1152]{3,2,1,0:T(8,128)(2,1)} %shard_map.148), calls=%async_computation | async-start | bytes 1179648 | tf_op jit(solution)/shard_map/all_to_all | solution.py:690
  9.1 2.5 %collective-permute-start.3 = (bf16[64,1152]{1,0:T(8,128)(2,1)S(1)}, bf16[64,1152]{1,0:T(8,128)(2,1)S(1)}, u32[]{:S(2)}, u32[]{:S(2)}) collective-permute-start(bf16[64,1152]{1,0:T(8,128)(2,1)S(1)} %get-tuple-element.93), channel_id=1, source_target_pairs={{0,6},{1,7},{2,4},{3,5},{4,2},{5,3},{6,0},{7,1},{8,14},{9,15},{10,... | collective-permute-start | bytes 442376 | tf_op jit(solution)/shard_map/ppermute | solution.py:706
  14.3 1.7 %collective-permute-done.3.refs_6_ = bf16[64,1152]{1,0:T(8,128)(2,1)S(1)} collective-permute-done((bf16[64,1152]{1,0:T(8,128)(2,1)S(1)}, bf16[64,1152]{1,0:T(8,128)(2,1)S(1)}, u32[]{:S(2)}, u32[]{:S(2)}) %collective-permute-start.3) | collective-permute-done | bytes 147488 | tf_op jit(solution)/shard_map/ppermute | solution.py:706
  16.1 2.4 %collective-permute-done.2.refs_4_ = bf16[64,1152]{1,0:T(8,128)(2,1)S(1)} collective-permute-done((bf16[64,1152]{1,0:T(8,128)(2,1)S(1)}, bf16[64,1152]{1,0:T(8,128)(2,1)S(1)}, u32[]{:S(2)}, u32[]{:S(2)}) %collective-permute-start.2) | collective-permute-done | bytes 147488 | tf_op jit(solution)/shard_map/ppermute | solution.py:706
  21.8 9.7 %shard_map.147 = (bf16[1,512,1152]{2,1,0:T(8,128)(2,1)}, bf16[3,512,512]{2,1,0:T(8,128)(2,1)}, bf16[4,512,512]{2,1,0:T(8,128)(2,1)}, bf16[32,16,384]{2,1,0:T(8,128)(2,1)}) custom-call(bf16[64,1152]{1,0:T(8,128)(2,1)} %copy-done.10, bf16[64,1152]{1,0:T(8,128)(2,1)} %collective-permute-done.refs_1_, bf16[64,1152]{1,0:T(8,128)(2,1)} %collective-permute-done.1.refs_2_, ...), custom_call_target="tpu_custom_call" | custom-call | flops 1073741824 | bytes 8000000 | tf_op jit(solution)/shard_map/pallas_call | solution.py:145
  31.6 5.1 %all-to-all-start.1 = ((bf16[32,16,384]{2,1,0:T(8,128)(2,1)}), bf16[32,16,384]{2,1,0:T(8,128)(2,1)S(1)}, u32[]{:S(2)}, u32[]{:S(2)}) async-start(bf16[32,16,384]{2,1,0:T(8,128)(2,1)} %get-tuple-element.55), calls=%async_computation.1 | async-start | bytes 786432 | tf_op jit(solution)/shard_map/all_to_all | solution.py:690
  37.8 1.6 %copy.19 = f32[36,32,32]{2,1,0:T(8,128)S(1)} copy(f32[36,32,32]{0,2,1:T(8,128)} %param.21) | data formatting | bytes 294912 | tf_op jit(solution)/shard_map/optimization_barrier | solution.py:748
  42.0 4.8 %shard_map.150.refs_7_.refs_0_ = bf16[3,128,1152]{2,1,0:T(8,128)(2,1)} custom-call(bf16[4,2,32,1152]{3,2,1,0:T(8,128)(2,1)} %copy-done.8, s32[8]{0:T(128)} %refs_2_.3, bf16[1152,1152]{1,0:T(8,128)(2,1)} %refs_2_.2, bf16[1,1152,128]{2,1,0:T(8,128)(2,1)} %copy-done.5), custom_call_target="tpu_custom_call" | custom-call | flops 339738624 | bytes 4000000 | tf_op jit(solution)/shard_map/pallas_call | solution.py:145
  46.8 2.8 %all-to-all-done.1.refs_1_ = bf16[32,16,384]{2,1,0:T(8,128)(2,1)S(1)} async-done(((bf16[32,16,384]{2,1,0:T(8,128)(2,1)}), bf16[32,16,384]{2,1,0:T(8,128)(2,1)S(1)}, u32[]{:S(2)}, u32[]{:S(2)}) %all-to-all-start.1) | async-done | bytes 393248 | tf_op jit(solution)/shard_map/all_to_all | solution.py:690
  50.4 14.4 %shard_map.151 = (bf16[32,16,384]{2,1,0:T(8,128)(2,1)}, bf16[5,128,1152]{2,1,0:T(8,128)(2,1)}, bf16[32,1152]{1,0:T(8,128)(2,1)}, bf16[32,1152]{1,0:T(8,128)(2,1)...) custom-call(bf16[4,2,32,1152]{3,2,1,0:T(8,128)(2,1)} %copy-done.8, bf16[32,16,384]{2,1,0:T(8,128)(2,1)} %copy-done.9, ...), custom_call_target="tpu_custom_call" | custom-call | flops 2717908992 | bytes 12000000 | tf_op jit(solution)/shard_map/pallas_call | solution.py:145
  64.8 3.1 %all-to-all-start.2 = ((bf16[32,16,384]{2,1,0:T(8,128)(2,1)}), bf16[32,16,384]{2,1,0:T(8,128)(2,1)S(1)}, u32[]{:S(2)}, u32[]{:S(2)}) async-start(bf16[32,16,384]{2,1,0:T(8,128)(2,1)} %get-tuple-element.62), calls=%async_computation.2 | async-start | bytes 786432 | tf_op jit(solution)/shard_map/all_to_all | solution.py:690
  67.9 3.1 %shard_map.152.refs_5_ = f32[1,1152,128]{2,1,0:T(8,128)} custom-call(bf16[3,128,1152]{2,1,0:T(8,128)(2,1)} %shard_map.150.refs_7_.refs_0_, bf16[5,128,1152]{2,1,0:T(8,128)(2,1)} %get-tuple-element.63.refs_1_), custom_call_target="tpu_custom_call" | custom-call | flops 1000000000 | bytes 4000000 | tf_op jit(solution)/shard_map/pallas_call | solution.py:145
  71.0 9.8 %all-to-all-done.2.refs_0_ = bf16[32,16,384]{2,1,0:T(8,128)(2,1)S(1)} async-done(((bf16[32,16,384]{2,1,0:T(8,128)(2,1)}), bf16[32,16,384]{2,1,0:T(8,128)(2,1)S(1)}, u32[]{:S(2)}, u32[]{:S(2)}) %all-to-all-start.2) | async-done | bytes 393248 | tf_op jit(solution)/shard_map/all_to_all | solution.py:690
  81.9 10.5 %shard_map.153 = (bf16[4,80,1152]{2,1,0:T(8,128)(2,1)S(1)}, bf16[4,80,1152]{2,1,0:T(8,128)(2,1)}) custom-call(bf16[32,16,384]{2,1,0:T(8,128)(2,1)S(1)} %all-to-all-done.2.refs_0_, bf16[3,512,512]{2,1,0:T(8,128)(2,1)} %get-tuple-element.65.refs_1_, bf16[4,512,512]{2,1,0:T(8,128)(2,1)} %get-tuple-element.66.refs_2_, bf16[1,1152,128]{2,1,0:T(8,128)(2,1)S(1)} %copy-done.2, ...), custom_call_target="tpu_custom_call" | custom-call | flops 10000000000 | bytes 8000000 | tf_op jit(solution)/shard_map/pallas_call | solution.py:145
  92.5 2.4 %collective-permute-done.7.refs_1_ = bf16[4,80,1152]{2,1,0:T(8,128)(2,1)S(1)} collective-permute-done((bf16[4,80,1152]{2,1,0:T(8,128)(2,1)}, bf16[4,80,1152]{2,1,0:T(8,128)(2,1)S(1)}, u32[]{:S(2)}, u32[]{:S(2)}) %collective-permute-start.7) | collective-permute-done | bytes 737312 | tf_op jit(solution)/shard_map/ppermute | solution.py:706
  97.2 1.5 %collective-permute-start.10 = (bf16[80,1152]{1,0:T(8,128)(2,1)S(1)}, bf16[80,1152]{1,0:T(8,128)(2,1)S(1)}, u32[]{:S(2)}, u32[]{:S(2)}) collective-permute-start(bf16[80,1152]{1,0:T(8,128)(2,1)S(1)} %get-tuple-element.79), channel_id=1, source_target_pairs={{0,6},{1,7},{2,4},{3,5},{4,2},{5,3},{6,0},{7,1},{8,14},{9,15},{10,... | collective-permute-start | bytes 552968 | tf_op jit(solution)/shard_map/ppermute | solution.py:706
  98.7 4.0 %collective-permute-done.8.refs_1_.refs_5_ = bf16[80,1152]{1,0:T(8,128)(2,1)S(1)} collective-permute-done((bf16[80,1152]{1,0:T(8,128)(2,1)S(1)}, bf16[80,1152]{1,0:T(8,128)(2,1)S(1)}, u32[]{:S(2)}, u32[]{:S(2)}) %collective-permute-start.8) | collective-permute-done | bytes 184352 | tf_op jit(solution)/shard_map/ppermute | solution.py:706
  104.3 2.2 %collective-permute-start.16 = (bf16[32,1152]{1,0:T(8,128)(2,1)S(1)}, bf16[32,1152]{1,0:T(8,128)(2,1)S(1)}, u32[]{:S(2)}, u32[]{:S(2)}) collective-permute-start(bf16[32,1152]{1,0:T(8,128)(2,1)S(1)} %copy-done.19), channel_id=1, source_target_pairs={{0,24},{8,0},{16,8},{24,16},{1,25},{9,1},{17,9},{25,17},{2,26},{10... | collective-permute-start | bytes 221192 | tf_op jit(solution)/shard_map/ppermute | solution.py:696
  106.6 1.6 %collective-permute-start.13 = (bf16[16,1152]{1,0:T(8,128)(2,1)S(1)}, bf16[16,1152]{1,0:T(8,128)(2,1)S(1)}, u32[]{:S(2)}, u32[]{:S(2)}) collective-permute-start(bf16[16,1152]{1,0:T(8,128)(2,1)S(1)} %shard_map.155.refs_0_), channel_id=1, source_target_pairs={{0,24},{8,0},{16,8},{24,16},{1,25},{9,1},{17,9},{25,17},{2,26},{10... | collective-permute-start | bytes 110600 | tf_op jit(solution)/shard_map/ppermute | solution.py:696
  109.2 1.4 %collective-permute-start.11 = (bf16[16,1152]{1,0:T(8,128)(2,1)S(1)}, bf16[16,1152]{1,0:T(8,128)(2,1)S(1)}, u32[]{:S(2)}, u32[]{:S(2)}) collective-permute-start(bf16[16,1152]{1,0:T(8,128)(2,1)S(1)} %shard_map.155.refs_0_), channel_id=1, source_target_pairs={{0,8},{8,16},{16,24},{24,0},{1,9},{9,17},{17,25},{25,1},{2,10},{10... | collective-permute-start | bytes 110600 | tf_op jit(solution)/shard_map/ppermute | solution.py:696
  113.0 1.5 %collective-permute-done.12.refs_2_ = bf16[16,1152]{1,0:T(8,128)(2,1)S(1)} collective-permute-done((bf16[16,1152]{1,0:T(8,128)(2,1)S(1)}, bf16[16,1152]{1,0:T(8,128)(2,1)S(1)}, u32[]{:S(2)}, u32[]{:S(2)}) %collective-permute-start.12) | collective-permute-done | bytes 36896 | tf_op jit(solution)/shard_map/ppermute | solution.py:696
  115.2 1.5 %collective-permute-start.22 = (bf16[144,128]{1,0:T(8,128)(2,1)S(1)}, bf16[144,128]{1,0:T(8,128)(2,1)S(1)}, u32[]{:S(2)}, u32[]{:S(2)}) collective-permute-start(bf16[144,128]{1,0:T(8,128)(2,1)S(1)} %shard_map.157.refs_0_), channel_id=1, source_target_pairs={{0,6},{1,7},{2,4},{3,5},{4,2},{5,3},{6,0},{7,1},{8,14},{9,15},{10,... | collective-permute-start | bytes 110600 | tf_op jit(solution)/shard_map/ppermute | solution.py:706
  122.8 1.8 %shard_map.158 = (f32[32,32,36]{2,1,0:T(8,128)}, f32[32,32,36]{2,1,0:T(8,128)}, f32[32,32,36]{2,1,0:T(8,128)}, f32[32,32,36]{2,1,0:T(8,128)}) custom-call(bf16[144,128]{1,0:T(8,128)(2,1)S(1)} %shard_map.157.refs_0_, bf16[144,128]{1,0:T(8,128)(2,1)S(1)} %collective-permute-done.17.refs_1_, bf16[144,128]{1,0:T(8,128)(2,1)S(1)} %collective-permute-done.18.refs_2_, ...), custom_call_target="tpu_custom_call" | custom-call | tf_op jit(solution)/shard_map/pallas_call | solution.py:145
  (92 shorter events, 25.9 us)
Async XLA Ops:
  2.7 28.9 %all-to-all-start = ((bf16[4,2,32,1152]{3,2,1,0:T(8,128)(2,1)}), bf16[4,2,32,1152]{3,2,1,0:T(8,128)(2,1)S(1)}, u32[]{:S(2)}, u32[]{:S(2)}) async-start(bf16[4,2,32,1152]{3,2,1,0:T(8,128)(2,1)} %shard_map.148), calls=%async_computation | async-start | bytes 1179648 | tf_op jit(solution)/shard_map/all_to_all | solution.py:690
  9.1 7.0 %collective-permute-start.3 = (bf16[64,1152]{1,0:T(8,128)(2,1)S(1)}, bf16[64,1152]{1,0:T(8,128)(2,1)S(1)}, u32[]{:S(2)}, u32[]{:S(2)}) collective-permute-start(bf16[64,1152]{1,0:T(8,128)(2,1)S(1)} %get-tuple-element.93), channel_id=1, source_target_pairs={{0,6},{1,7},{2,4},{3,5},{4,2},{5,3},{6,0},{7,1},{8,14},{9,15},{10,... | collective-permute-start | bytes 442376 | tf_op jit(solution)/shard_map/ppermute | solution.py:706
  11.6 6.9 %collective-permute-start.2 = (bf16[64,1152]{1,0:T(8,128)(2,1)S(1)}, bf16[64,1152]{1,0:T(8,128)(2,1)S(1)}, u32[]{:S(2)}, u32[]{:S(2)}) collective-permute-start(bf16[64,1152]{1,0:T(8,128)(2,1)S(1)} %get-tuple-element.94), channel_id=1, source_target_pairs={{0,4},{1,5},{2,6},{3,7},{4,0},{5,1},{6,2},{7,3},{8,12},{9,13},{10,... | collective-permute-start | bytes 442376 | tf_op jit(solution)/shard_map/ppermute | solution.py:706
  12.1 6.6 %collective-permute-start.1 = (bf16[64,1152]{1,0:T(8,128)(2,1)S(1)}, bf16[64,1152]{1,0:T(8,128)(2,1)}, u32[]{:S(2)}, u32[]{:S(2)}) collective-permute-start(bf16[64,1152]{1,0:T(8,128)(2,1)S(1)} %get-tuple-element.95), channel_id=1, source_target_pairs={{0,2},{1,3},{2,0},{3,1},{4,6},{5,7},{6,4},{7,5},{8,10},{9,11},{10,... | collective-permute-start | bytes 442376 | tf_op jit(solution)/shard_map/ppermute | solution.py:706
  12.6 6.6 %collective-permute-start = (bf16[64,1152]{1,0:T(8,128)(2,1)S(1)}, bf16[64,1152]{1,0:T(8,128)(2,1)}, u32[]{:S(2)}, u32[]{:S(2)}) collective-permute-start(bf16[64,1152]{1,0:T(8,128)(2,1)S(1)} %get-tuple-element.96.refs_0_), channel_id=1, source_target_pairs={{0,1},{1,0},{2,3},{3,2},{4,5},{5,4},{6,7},{7,6},{8,9},{9,8},{10,11... | collective-permute-start | bytes 442376 | tf_op jit(solution)/shard_map/ppermute | solution.py:706
  18.7 1.8 %collective-permute-start.4 = (bf16[64,1152]{1,0:T(8,128)(2,1)}, bf16[64,1152]{1,0:T(8,128)(2,1)S(1)}, u32[]{:S(2)}, u32[]{:S(2)}) collective-permute-start(bf16[64,1152]{1,0:T(8,128)(2,1)} %collective-permute-done.1.refs_2_), channel_id=1, source_target_pairs={{0,1},{1,0},{2,3},{3,2},{4,5},{5,4},{6,7},{7,6},{8,9},{9,8},{10,11... | collective-permute-start | bytes 442376 | tf_op jit(solution)/shard_map/ppermute | solution.py:706
  18.7 1.8 %collective-permute-start.5 = (bf16[64,1152]{1,0:T(8,128)(2,1)S(1)}, bf16[64,1152]{1,0:T(8,128)(2,1)S(1)}, u32[]{:S(2)}, u32[]{:S(2)}) collective-permute-start(bf16[64,1152]{1,0:T(8,128)(2,1)S(1)} %collective-permute-done.2.refs_4_), channel_id=1, source_target_pairs={{0,1},{1,0},{2,3},{3,2},{4,5},{5,4},{6,7},{7,6},{8,9},{9,8},{10,11... | collective-permute-start | bytes 442376 | tf_op jit(solution)/shard_map/ppermute | solution.py:706
  31.6 18.1 %all-to-all-start.1 = ((bf16[32,16,384]{2,1,0:T(8,128)(2,1)}), bf16[32,16,384]{2,1,0:T(8,128)(2,1)S(1)}, u32[]{:S(2)}, u32[]{:S(2)}) async-start(bf16[32,16,384]{2,1,0:T(8,128)(2,1)} %get-tuple-element.55), calls=%async_computation.1 | async-start | bytes 786432 | tf_op jit(solution)/shard_map/all_to_all | solution.py:690
  64.8 16.0 %all-to-all-start.2 = ((bf16[32,16,384]{2,1,0:T(8,128)(2,1)}), bf16[32,16,384]{2,1,0:T(8,128)(2,1)S(1)}, u32[]{:S(2)}, u32[]{:S(2)}) async-start(bf16[32,16,384]{2,1,0:T(8,128)(2,1)} %get-tuple-element.62), calls=%async_computation.2 | async-start | bytes 786432 | tf_op jit(solution)/shard_map/all_to_all | solution.py:690
  92.4 2.5 %collective-permute-start.7 = (bf16[4,80,1152]{2,1,0:T(8,128)(2,1)}, bf16[4,80,1152]{2,1,0:T(8,128)(2,1)S(1)}, u32[]{:S(2)}, u32[]{:S(2)}) collective-permute-start(bf16[4,80,1152]{2,1,0:T(8,128)(2,1)} %get-tuple-element.70), channel_id=1, source_target_pairs={{0,1},{1,0},{2,3},{3,2},{4,5},{5,4},{6,7},{7,6},{8,9},{9,8},{10,11... | collective-permute-start | bytes 2211848 | tf_op jit(solution)/shard_map/ppermute | solution.py:706
  95.1 7.5 %collective-permute-start.8 = (bf16[80,1152]{1,0:T(8,128)(2,1)S(1)}, bf16[80,1152]{1,0:T(8,128)(2,1)S(1)}, u32[]{:S(2)}, u32[]{:S(2)}) collective-permute-start(bf16[80,1152]{1,0:T(8,128)(2,1)S(1)} %get-tuple-element.72), channel_id=1, source_target_pairs={{0,2},{1,3},{2,0},{3,1},{4,6},{5,7},{6,4},{7,5},{8,10},{9,11},{10,... | collective-permute-start | bytes 552968 | tf_op jit(solution)/shard_map/ppermute | solution.py:706
  95.8 10.8 %collective-permute-start.9 = (bf16[80,1152]{1,0:T(8,128)(2,1)S(1)}, bf16[80,1152]{1,0:T(8,128)(2,1)S(1)}, u32[]{:S(2)}, u32[]{:S(2)}) collective-permute-start(bf16[80,1152]{1,0:T(8,128)(2,1)S(1)} %get-tuple-element.78), channel_id=1, source_target_pairs={{0,4},{1,5},{2,6},{3,7},{4,0},{5,1},{6,2},{7,3},{8,12},{9,13},{10,... | collective-permute-start | bytes 552968 | tf_op jit(solution)/shard_map/ppermute | solution.py:706
  97.2 9.4 %collective-permute-start.10 = (bf16[80,1152]{1,0:T(8,128)(2,1)S(1)}, bf16[80,1152]{1,0:T(8,128)(2,1)S(1)}, u32[]{:S(2)}, u32[]{:S(2)}) collective-permute-start(bf16[80,1152]{1,0:T(8,128)(2,1)S(1)} %get-tuple-element.79), channel_id=1, source_target_pairs={{0,6},{1,7},{2,4},{3,5},{4,2},{5,3},{6,0},{7,1},{8,14},{9,15},{10,... | collective-permute-start | bytes 552968 | tf_op jit(solution)/shard_map/ppermute | solution.py:706
  102.7 6.6 %collective-permute-start.14 = (bf16[32,1152]{1,0:T(8,128)(2,1)S(1)}, bf16[32,1152]{1,0:T(8,128)(2,1)S(1)}, u32[]{:S(2)}, u32[]{:S(2)}) collective-permute-start(bf16[32,1152]{1,0:T(8,128)(2,1)S(1)} %copy-done.21), channel_id=1, source_target_pairs={{0,8},{8,16},{16,24},{24,0},{1,9},{9,17},{17,25},{25,1},{2,10},{10... | collective-permute-start | bytes 221192 | tf_op jit(solution)/shard_map/ppermute | solution.py:696
  103.7 8.1 %collective-permute-start.15 = (bf16[32,1152]{1,0:T(8,128)(2,1)S(1)}, bf16[32,1152]{1,0:T(8,128)(2,1)S(1)}, u32[]{:S(2)}, u32[]{:S(2)}) collective-permute-start(bf16[32,1152]{1,0:T(8,128)(2,1)S(1)} %copy-done.20), channel_id=1, source_target_pairs={{0,16},{8,24},{16,0},{24,8},{1,17},{9,25},{17,1},{25,9},{2,18},{10... | collective-permute-start | bytes 221192 | tf_op jit(solution)/shard_map/ppermute | solution.py:696
  104.3 7.5 %collective-permute-start.16 = (bf16[32,1152]{1,0:T(8,128)(2,1)S(1)}, bf16[32,1152]{1,0:T(8,128)(2,1)S(1)}, u32[]{:S(2)}, u32[]{:S(2)}) collective-permute-start(bf16[32,1152]{1,0:T(8,128)(2,1)S(1)} %copy-done.19), channel_id=1, source_target_pairs={{0,24},{8,0},{16,8},{24,16},{1,25},{9,1},{17,9},{25,17},{2,26},{10... | collective-permute-start | bytes 221192 | tf_op jit(solution)/shard_map/ppermute | solution.py:696
  106.6 6.4 %collective-permute-start.13 = (bf16[16,1152]{1,0:T(8,128)(2,1)S(1)}, bf16[16,1152]{1,0:T(8,128)(2,1)S(1)}, u32[]{:S(2)}, u32[]{:S(2)}) collective-permute-start(bf16[16,1152]{1,0:T(8,128)(2,1)S(1)} %shard_map.155.refs_0_), channel_id=1, source_target_pairs={{0,24},{8,0},{16,8},{24,16},{1,25},{9,1},{17,9},{25,17},{2,26},{10... | collective-permute-start | bytes 110600 | tf_op jit(solution)/shard_map/ppermute | solution.py:696
  108.2 6.3 %collective-permute-start.12 = (bf16[16,1152]{1,0:T(8,128)(2,1)S(1)}, bf16[16,1152]{1,0:T(8,128)(2,1)S(1)}, u32[]{:S(2)}, u32[]{:S(2)}) collective-permute-start(bf16[16,1152]{1,0:T(8,128)(2,1)S(1)} %shard_map.155.refs_0_), channel_id=1, source_target_pairs={{0,16},{8,24},{16,0},{24,8},{1,17},{9,25},{17,1},{25,9},{2,18},{10... | collective-permute-start | bytes 110600 | tf_op jit(solution)/shard_map/ppermute | solution.py:696
  109.2 5.8 %collective-permute-start.11 = (bf16[16,1152]{1,0:T(8,128)(2,1)S(1)}, bf16[16,1152]{1,0:T(8,128)(2,1)S(1)}, u32[]{:S(2)}, u32[]{:S(2)}) collective-permute-start(bf16[16,1152]{1,0:T(8,128)(2,1)S(1)} %shard_map.155.refs_0_), channel_id=1, source_target_pairs={{0,8},{8,16},{16,24},{24,0},{1,9},{9,17},{17,25},{25,1},{2,10},{10... | collective-permute-start | bytes 110600 | tf_op jit(solution)/shard_map/ppermute | solution.py:696
  115.2 4.9 %collective-permute-start.22 = (bf16[144,128]{1,0:T(8,128)(2,1)S(1)}, bf16[144,128]{1,0:T(8,128)(2,1)S(1)}, u32[]{:S(2)}, u32[]{:S(2)}) collective-permute-start(bf16[144,128]{1,0:T(8,128)(2,1)S(1)} %shard_map.157.refs_0_), channel_id=1, source_target_pairs={{0,6},{1,7},{2,4},{3,5},{4,2},{5,3},{6,0},{7,1},{8,14},{9,15},{10,... | collective-permute-start | bytes 110600 | tf_op jit(solution)/shard_map/ppermute | solution.py:706
  116.7 4.0 %collective-permute-start.20 = (bf16[144,128]{1,0:T(8,128)(2,1)S(1)}, bf16[144,128]{1,0:T(8,128)(2,1)S(1)}, u32[]{:S(2)}, u32[]{:S(2)}) collective-permute-start(bf16[144,128]{1,0:T(8,128)(2,1)S(1)} %shard_map.157.refs_0_), channel_id=1, source_target_pairs={{0,4},{1,5},{2,6},{3,7},{4,0},{5,1},{6,2},{7,3},{8,12},{9,13},{10,... | collective-permute-start | bytes 110600 | tf_op jit(solution)/shard_map/ppermute | solution.py:706
  117.6 4.0 %collective-permute-start.18 = (bf16[144,128]{1,0:T(8,128)(2,1)S(1)}, bf16[144,128]{1,0:T(8,128)(2,1)S(1)}, u32[]{:S(2)}, u32[]{:S(2)}) collective-permute-start(bf16[144,128]{1,0:T(8,128)(2,1)S(1)} %shard_map.157.refs_0_), channel_id=1, source_target_pairs={{0,2},{1,3},{2,0},{3,1},{4,6},{5,7},{6,4},{7,5},{8,10},{9,11},{10,... | collective-permute-start | bytes 110600 | tf_op jit(solution)/shard_map/ppermute | solution.py:706
  118.7 2.8 %collective-permute-start.17 = (bf16[144,128]{1,0:T(8,128)(2,1)S(1)}, bf16[144,128]{1,0:T(8,128)(2,1)S(1)}, u32[]{:S(2)}, u32[]{:S(2)}) collective-permute-start(bf16[144,128]{1,0:T(8,128)(2,1)S(1)} %shard_map.157.refs_0_), channel_id=1, source_target_pairs={{0,1},{1,0},{2,3},{3,2},{4,5},{5,4},{6,7},{7,6},{8,9},{9,8},{10,11... | collective-permute-start | bytes 110600 | tf_op jit(solution)/shard_map/ppermute | solution.py:706
  120.1 1.5 %collective-permute-start.23 = (bf16[144,128]{1,0:T(8,128)(2,1)S(1)}, bf16[144,128]{1,0:T(8,128)(2,1)S(1)}, u32[]{:S(2)}, u32[]{:S(2)}) collective-permute-start(bf16[144,128]{1,0:T(8,128)(2,1)S(1)} %collective-permute-done.22.refs_6_), channel_id=1, source_target_pairs={{0,1},{1,0},{2,3},{3,2},{4,5},{5,4},{6,7},{7,6},{8,9},{9,8},{10,11... | collective-permute-start | bytes 110600 | tf_op jit(solution)/shard_map/ppermute | solution.py:706
  (25 other events, 221.0 us)

commit v3 on v2

--- a/solution.py
+++ b/solution.py
@@ -110,6 +110,12 @@
             copy = pltpu.make_async_copy(self.ref.at[i], self.target.at[i], self.sems.at[i])
             copy.start()
             self.started.append(copy)
+
+    def flush_span(self, start, size, i):
+        span = pl.ds(start, size)
+        copy = pltpu.make_async_copy(self.ref.at[span], self.target.at[span], self.sems.at[i])
+        copy.start()
+        self.started.append(copy)
 
     def finish(self):
         for copy in self.started:
@@ -314,7 +320,19 @@
         ordered[start : start + count, :] = terms[pl.ds(b, count, stride=BLOCK), :]
 
 
-def term_kernel(plan, prepared_ref, factors, out, outrot, terms, sems):
+def store_terms(plan, ordered, distance, out_ref):
+    share = plan.term_tiles * TILE
+    start = pl.multiple_of(plan.peer(distance) * share, TILE)
+    owned = ordered[pl.ds(start, share), :].astype(BF16)
+    for k in range(CHUNKS):
+        if k < plan.term_tiles:
+            tile = owned[k * TILE : (k + 1) * TILE, :]
+        else:
+            tile = jnp.zeros((TILE, LANES), BF16)
+        out_ref[:, lanes_of(k)] = tile
+
+
+def term_kernel(plan, prepared_ref, factors, even_out, odd_out, outrot, terms, ordered, sems):
     copies = start_all([(prepared_ref.at[1], outrot)], sems)
     mask = diagonal_mask()
     parts = factors()
@@ -322,20 +340,21 @@
     rotation_gradient(parts[3], parts[4], mask, terms, 2 * CHUNKS)
     wait_all(copies)
     rotation_gradient(parts[0], outrot[...], mask, terms, 0)
-    ordered = out.ref.at[0]
     ordered[...] = jnp.zeros_like(ordered)
     order_terms(plan, terms, ordered, 0, 3 * CHUNKS)
-    out.flush(0)
+    for r in range(plan.patch_ways):
+        out = (even_out, odd_out)[r % 2]
+        store_terms(plan, ordered, r, out.ref.at[r // 2])
+        out.flush(r // 2)
 
 
 def spatial_backward_kernel(
     plan,
-    adjoint_items,
+    adjoint_ref,
     stack,
     weights,
     blocks,
     normed,
-    term,
     weight_ref,
     even_out,
     odd_out,
@@ -344,13 +363,13 @@
     grads,
     projected,
     terms,
+    ordered,
     sems,
 ):
     copies = weight_windows(plan, weight_ref, windows, sems)
     for copy in copies:
         copy.start()
     own = plan.own_patches
-    adjoint_ref = adjoint_items()
     for r in range(plan.patch_ways):
         source = plan.peer(r)
         for z in range(plan.frame_ways):
@@ -387,28 +406,25 @@
         copy.wait()
     rotated = dot_nt(projected[...], windows[...]).astype(BF16)
     size = plan.patches_local
-    share = plan.term_tiles * TILE
     rotation_gradient(normed()[0], rotated, diagonal_mask(), terms, 0)
-    ordered = term().at[0]
+    ordered[...] = jnp.zeros_like(ordered)
     order_terms(plan, terms, ordered, 3 * CHUNKS, CHUNKS)
     back = rotate_transposed(rotated, blocks().at[0]).astype(BF16)
     for r in list(range(1, plan.patch_ways, 2)) + list(range(0, plan.patch_ways, 2)):
         out = (even_out, odd_out)[r % 2]
         out_ref = out.ref.at[r // 2]
         out_ref[0:size, :] = back[r * size : (r + 1) * size, :]
-        owned = ordered[pl.ds(pl.multiple_of(plan.peer(r) * share, TILE), share), :].astype(BF16)
-        for k in range(CHUNKS):
-            if k < plan.term_tiles:
-                tile = owned[k * TILE : (k + 1) * TILE, :]
-            else:
-                tile = jnp.zeros((TILE, LANES), BF16)
-            out_ref[size : size + TILE, lanes_of(k)] = tile
+        store_terms(plan, ordered, r, out_ref.at[size : size + TILE])
         out.flush(r // 2)
 
 
-def pair_kernel(plan, even_ref, other_ref, *out_refs):
+def pair_kernel(plan, even_ref, other_ref, even_term_ref, other_term_ref, *out_refs):
+    size = plan.patches_local
     for s, out_ref in enumerate(out_refs):
-        out_ref[...] = (even_ref[s].astype(F32) + other_ref[s].astype(F32)).astype(BF16)
+        added = even_ref[s].astype(F32) + other_ref[s].astype(F32)
+        early = even_term_ref[s].astype(F32) + other_term_ref[s].astype(F32)
+        out_ref[0:size, :] = added[0:size].astype(BF16)
+        out_ref[size:, :] = (added[size:] + early).astype(BF16)
 
 
 def frame_column(plan, mask_ref):
@@ -650,7 +666,7 @@
 
 def unpack_kernel(plan, scaling, *refs):
     pieces = refs[: plan.patch_ways]
-    out_refs, wide = refs[plan.patch_ways : plan.patch_ways + 4], refs[plan.patch_ways + 4]
+    outs, wide = refs[plan.patch_ways : plan.patch_ways + 4], refs[plan.patch_ways + 4]
     blocks = 4 * CHUNKS
     row = lax.broadcasted_iota(jnp.int32, (blocks, blocks), 0)
     column = lax.broadcasted_iota(jnp.int32, (blocks, blocks), 1)
@@ -662,8 +678,10 @@
             rows = wide[r, inner * blocks : (inner + 1) * blocks, :].astype(BF16)
             turned = dot_tn(rows, chosen) * scaling
             b = plan.peer(r) * plan.term_blocks + inner
-            for t, out_ref in enumerate(out_refs):
-                out_ref[b] = turned[t * BLOCK : (t + 1) * BLOCK, :]
+            for t, out in enumerate(outs):
+                out.ref[b] = turned[t * BLOCK : (t + 1) * BLOCK, :]
+        for out in outs:
+            out.flush_span(plan.peer(r) * plan.term_blocks, plan.term_blocks, r)
 
 
 def estimate(flops, moved):
@@ -786,29 +804,30 @@
         cost=estimate(16 * plan.rows * D * D, 12e6),
     )
     adjoint_items = exchange(send, both)
-    ordered_shape = shape((plan.patch_ways * plan.term_tiles * TILE, LANES), F32)
-    (terms,) = call(
+    ordered_scratch = pltpu.VMEM((plan.patch_ways * plan.term_tiles * TILE, LANES), F32)
+    even_terms, odd_terms = call(
         functools.partial(term_kernel, plan),
         [("h", prepared), ("l", factors)],
-        [("d", shape((1,) + ordered_shape.shape, F32))],
+        mode("d", [shape((half, TILE, D), BF16)] * 2),
         [
             pltpu.VMEM((plan.rows, D), BF16),
             pltpu.VMEM((3 * CHUNKS * BLOCK, LANES), F32),
+            ordered_scratch,
             dma((1,)),
         ],
         cost=estimate(1e9, 4e6),
     )
-
-    adjoint_items, terms = lax.optimization_barrier((adjoint_items, terms))
+    adjoint_items, even_terms, other_terms = lax.optimization_barrier(
+        (adjoint_items, even_terms, swap(odd_terms, 1))
+    )
     even, odd = call(
         functools.partial(spatial_backward_kernel, plan),
         [
-            ("l", adjoint_items),
+            ("v", adjoint_items),
             ("l", stack),
             ("l", weights),
             ("l", spatial_inward),
             ("l", normed),
-            ("l", terms),
             ("h", spatial_project),
         ],
         mode("d", [shape((half,) + part_shape.shape, BF16)] * 2),
@@ -818,6 +837,7 @@
             pltpu.VMEM((3, plan.patches, plan.padded), BF16),
             pltpu.VMEM((plan.patches, 3 * plan.window), BF16),
             pltpu.VMEM((CHUNKS * BLOCK, LANES), F32),
+            ordered_scratch,
             dma((3,)),
         ],
         limit=52,
@@ -826,7 +846,7 @@
     other = swap(odd, 1)
     sums = call(
         functools.partial(pair_kernel, plan),
-        mode("v", [even, other]),
+        mode("v", [even, other, even_terms, other_terms]),
         mode("v", [part_shape] * half),
         limit=16,
     )
@@ -868,7 +888,7 @@
         for blocks in call(
             functools.partial(unpack_kernel, plan, scaling),
             mode("v", shared),
-            mode("v", [block_shape] * 4),
+            mode("d", [block_shape] * 4),
             [pltpu.VMEM((plan.patch_ways,) + share_shape.shape, F32)],
             limit=16,
         )

time: 125 us -> 125 us (level)
    all_to_all x3, waiting for transfers between devices: 12.7 us -> 11.1 us  [per_device(): exchange = lambda rows, axis: lax.all_to_all(rows, axis, 0, 0, tiled=True)]
    ppermute x18 -> x19, waiting for transfers between devices: 16.1 us -> 17.7 us  [swap(): return lax.ppermute(rows, 'patch', pairs)]
    ppermute x18 -> x19, starting transfers between devices: 11.3 us -> 11.4 us  [swap(): return lax.ppermute(rows, 'patch', pairs)]
  transfers between devices with their start and end apart: 27 -> 28, of which waited for: 18 -> 19; matrix products, arithmetic and copies ran while one was open for 3% -> 3% of each run, Pallas kernels for 16% -> 16%
where the time goes in v3:
time: 125 us; the launch traced here: 124 us
  Pallas kernels  50.1 us (40%)
  starting transfers between devices  33.2 us (27%)
  waiting for transfers between devices  32.5 us (26%)
  local copies, waits for them, and re-layouts  7.57 us (6%)
    pallas_call x13, Pallas kernels, call(): pl.pallas_call(body, out_shape=tuple((out for _, out in outs)), in_specs=...  50.1 us
    ppermute x19, waiting for transfers between devices, swap(): return lax.ppermute(rows, 'patch', pairs)  17.7 us
    all_to_all x3, starting transfers between devices, per_device(): exchange = lambda rows, axis: lax.all_to_all(rows, axis, 0, 0, tiled=True)  14.5 us
    ppermute x19, starting transfers between devices, swap(): return lax.ppermute(rows, 'patch', pairs)  11.4 us
    all_to_all x3, waiting for transfers between devices, per_device(): exchange = lambda rows, axis: lax.all_to_all(rows, axis, 0, 0, tiled=True)  11.1 us
    ppermute x6, starting transfers between devices, shifted(): lax.ppermute(pieces[s], 'frame', [(i, (i + s) % ways) for i in range(ways)])  7.39 us
    unnamed x45, local copies, waits for them, and re-layouts  4.76 us
    ppermute x6, waiting for transfers between devices, shifted(): lax.ppermute(pieces[s], 'frame', [(i, (i + s) % ways) for i in range(ways)])  3.68 us
  transfers between devices with their start and end apart: 28, of which 19 were waited for; matrix products, arithmetic and copies ran while one was open for 3% of the time, Pallas kernels for 16%

profile of v3, /device:TPU:0, one launch (start us, length us, event | category | flops | bytes accessed | tf_op | source)
XLA Modules:
  0.0 124.4 jit_solution(3570862039853376753)
XLA Ops:
  0.7 2.0 %shard_map.148 = bf16[4,2,32,1152]{3,2,1,0:T(8,128)(2,1)} custom-call(bf16[2,64,1152]{2,1,0:T(8,128)(2,1)} %refs_8_.1, bf16[2,64,1152]{2,1,0:T(8,128)(2,1)} %refs_1_.2), custom_call_target="tpu_custom_call" | custom-call | tf_op jit(solution)/shard_map/pallas_call | solution.py:151
  2.7 6.3 %all-to-all-start = ((bf16[4,2,32,1152]{3,2,1,0:T(8,128)(2,1)}), bf16[4,2,32,1152]{3,2,1,0:T(8,128)(2,1)S(1)}, u32[]{:S(2)}, u32[]{:S(2)}) async-start(bf16[4,2,32,1152]{3,2,1,0:T(8,128)(2,1)} %shard_map.148), calls=%async_computation | async-start | bytes 1179648 | tf_op jit(solution)/shard_map/all_to_all | solution.py:708
  9.1 2.5 %collective-permute-start.3 = (bf16[64,1152]{1,0:T(8,128)(2,1)S(1)}, bf16[64,1152]{1,0:T(8,128)(2,1)S(1)}, u32[]{:S(2)}, u32[]{:S(2)}) collective-permute-start(bf16[64,1152]{1,0:T(8,128)(2,1)S(1)} %get-tuple-element.99), channel_id=1, source_target_pairs={{0,6},{1,7},{2,4},{3,5},{4,2},{5,3},{6,0},{7,1},{8,14},{9,15},{10,... | collective-permute-start | bytes 442376 | tf_op jit(solution)/shard_map/ppermute | solution.py:724
  14.3 1.7 %collective-permute-done.3.refs_6_ = bf16[64,1152]{1,0:T(8,128)(2,1)S(1)} collective-permute-done((bf16[64,1152]{1,0:T(8,128)(2,1)S(1)}, bf16[64,1152]{1,0:T(8,128)(2,1)S(1)}, u32[]{:S(2)}, u32[]{:S(2)}) %collective-permute-start.3) | collective-permute-done | bytes 147488 | tf_op jit(solution)/shard_map/ppermute | solution.py:724
  16.1 2.4 %collective-permute-done.2.refs_4_ = bf16[64,1152]{1,0:T(8,128)(2,1)S(1)} collective-permute-done((bf16[64,1152]{1,0:T(8,128)(2,1)S(1)}, bf16[64,1152]{1,0:T(8,128)(2,1)S(1)}, u32[]{:S(2)}, u32[]{:S(2)}) %collective-permute-start.2) | collective-permute-done | bytes 147488 | tf_op jit(solution)/shard_map/ppermute | solution.py:724
  21.8 9.7 %shard_map.147 = (bf16[1,512,1152]{2,1,0:T(8,128)(2,1)}, bf16[3,512,512]{2,1,0:T(8,128)(2,1)}, bf16[4,512,512]{2,1,0:T(8,128)(2,1)}, bf16[32,16,384]{2,1,0:T(8,128)(2,1)}) custom-call(bf16[64,1152]{1,0:T(8,128)(2,1)} %copy-done.10, bf16[64,1152]{1,0:T(8,128)(2,1)} %collective-permute-done.refs_1_, bf16[64,1152]{1,0:T(8,128)(2,1)} %collective-permute-done.1.refs_2_, ...), custom_call_target="tpu_custom_call" | custom-call | flops 1073741824 | bytes 8000000 | tf_op jit(solution)/shard_map/pallas_call | solution.py:151
  31.5 5.1 %all-to-all-start.1 = ((bf16[32,16,384]{2,1,0:T(8,128)(2,1)}), bf16[32,16,384]{2,1,0:T(8,128)(2,1)S(1)}, u32[]{:S(2)}, u32[]{:S(2)}) async-start(bf16[32,16,384]{2,1,0:T(8,128)(2,1)} %get-tuple-element.58), calls=%async_computation.1 | async-start | bytes 786432 | tf_op jit(solution)/shard_map/all_to_all | solution.py:708
  37.8 1.6 %copy.19 = f32[36,32,32]{2,1,0:T(8,128)S(1)} copy(f32[36,32,32]{0,2,1:T(8,128)} %param.21) | data formatting | bytes 294912 | tf_op jit(solution)/shard_map/optimization_barrier | solution.py:766
  42.0 4.8 %shard_map.150.refs_7_.refs_0_ = bf16[3,128,1152]{2,1,0:T(8,128)(2,1)} custom-call(bf16[4,2,32,1152]{3,2,1,0:T(8,128)(2,1)} %copy-done.8, s32[8]{0:T(128)} %refs_2_.3, bf16[1152,1152]{1,0:T(8,128)(2,1)} %refs_2_.2, bf16[1,1152,128]{2,1,0:T(8,128)(2,1)} %copy-done.5), custom_call_target="tpu_custom_call" | custom-call | flops 339738624 | bytes 4000000 | tf_op jit(solution)/shard_map/pallas_call | solution.py:151
  46.8 2.8 %all-to-all-done.1.refs_1_ = bf16[32,16,384]{2,1,0:T(8,128)(2,1)S(1)} async-done(((bf16[32,16,384]{2,1,0:T(8,128)(2,1)}), bf16[32,16,384]{2,1,0:T(8,128)(2,1)S(1)}, u32[]{:S(2)}, u32[]{:S(2)}) %all-to-all-start.1) | async-done | bytes 393248 | tf_op jit(solution)/shard_map/all_to_all | solution.py:708
  50.3 14.4 %shard_map.151 = (bf16[32,16,384]{2,1,0:T(8,128)(2,1)}, bf16[5,128,1152]{2,1,0:T(8,128)(2,1)}, bf16[32,1152]{1,0:T(8,128)(2,1)}, bf16[32,1152]{1,0:T(8,128)(2,1)...) custom-call(bf16[4,2,32,1152]{3,2,1,0:T(8,128)(2,1)} %copy-done.8, bf16[32,16,384]{2,1,0:T(8,128)(2,1)} %copy-done.9, ...), custom_call_target="tpu_custom_call" | custom-call | flops 2717908992 | bytes 12000000 | tf_op jit(solution)/shard_map/pallas_call | solution.py:151
  64.8 3.1 %all-to-all-start.2 = ((bf16[32,16,384]{2,1,0:T(8,128)(2,1)}), bf16[32,16,384]{2,1,0:T(8,128)(2,1)S(1)}, u32[]{:S(2)}, u32[]{:S(2)}) async-start(bf16[32,16,384]{2,1,0:T(8,128)(2,1)} %get-tuple-element.65), calls=%async_computation.2 | async-start | bytes 786432 | tf_op jit(solution)/shard_map/all_to_all | solution.py:708
  67.9 3.0 %shard_map.152 = (bf16[4,16,1152]{2,1,0:T(8,128)(2,1)}, bf16[4,16,1152]{2,1,0:T(8,128)(2,1)}) custom-call(bf16[3,128,1152]{2,1,0:T(8,128)(2,1)} %shard_map.150.refs_7_.refs_0_, bf16[5,128,1152]{2,1,0:T(8,128)(2,1)} %get-tuple-element.66.refs_1_), custom_call_target="tpu_custom_call" | custom-call | flops 1000000000 | bytes 4000000 | tf_op jit(solution)/shard_map/pallas_call | solution.py:151
  71.0 1.5 %collective-permute-done.7.refs_3_ = bf16[4,16,1152]{2,1,0:T(8,128)(2,1)S(1)} collective-permute-done((bf16[4,16,1152]{2,1,0:T(8,128)(2,1)}, bf16[4,16,1152]{2,1,0:T(8,128)(2,1)S(1)}, u32[]{:S(2)}, u32[]{:S(2)}) %collective-permute-start.7) | collective-permute-done | bytes 147488 | tf_op jit(solution)/shard_map/ppermute | solution.py:724
  72.5 8.3 %all-to-all-done.2.refs_0_ = bf16[32,16,384]{2,1,0:T(8,128)(2,1)S(1)} async-done(((bf16[32,16,384]{2,1,0:T(8,128)(2,1)}), bf16[32,16,384]{2,1,0:T(8,128)(2,1)S(1)}, u32[]{:S(2)}, u32[]{:S(2)}) %all-to-all-start.2) | async-done | bytes 393248 | tf_op jit(solution)/shard_map/all_to_all | solution.py:708
  80.9 10.3 %shard_map.153 = (bf16[4,80,1152]{2,1,0:T(8,128)(2,1)S(1)}, bf16[4,80,1152]{2,1,0:T(8,128)(2,1)}) custom-call(bf16[32,16,384]{2,1,0:T(8,128)(2,1)S(1)} %all-to-all-done.2.refs_0_, bf16[3,512,512]{2,1,0:T(8,128)(2,1)} %get-tuple-element.70.refs_1_, bf16[4,512,512]{2,1,0:T(8,128)(2,1)} %get-tuple-element.71.refs_2_, bf16[1,1152,128]{2,1,0:T(8,128)(2,1)S(1)} %copy-done.2, ...), custom_call_target="tpu_custom_call" | custom-call | flops 10000000000 | bytes 8000000 | tf_op jit(solution)/shard_map/pallas_call | solution.py:151
  91.3 2.4 %collective-permute-done.8.refs_1_ = bf16[4,80,1152]{2,1,0:T(8,128)(2,1)S(1)} collective-permute-done((bf16[4,80,1152]{2,1,0:T(8,128)(2,1)}, bf16[4,80,1152]{2,1,0:T(8,128)(2,1)S(1)}, u32[]{:S(2)}, u32[]{:S(2)}) %collective-permute-start.8) | collective-permute-done | bytes 737312 | tf_op jit(solution)/shard_map/ppermute | solution.py:724
  95.9 1.5 %collective-permute-start.11 = (bf16[80,1152]{1,0:T(8,128)(2,1)S(1)}, bf16[80,1152]{1,0:T(8,128)(2,1)S(1)}, u32[]{:S(2)}, u32[]{:S(2)}) collective-permute-start(bf16[80,1152]{1,0:T(8,128)(2,1)S(1)} %get-tuple-element.85), channel_id=1, source_target_pairs={{0,6},{1,7},{2,4},{3,5},{4,2},{5,3},{6,0},{7,1},{8,14},{9,15},{10,... | collective-permute-start | bytes 552968 | tf_op jit(solution)/shard_map/ppermute | solution.py:724
  97.5 4.0 %collective-permute-done.9.refs_1_.refs_5_ = bf16[80,1152]{1,0:T(8,128)(2,1)S(1)} collective-permute-done((bf16[80,1152]{1,0:T(8,128)(2,1)S(1)}, bf16[80,1152]{1,0:T(8,128)(2,1)S(1)}, u32[]{:S(2)}, u32[]{:S(2)}) %collective-permute-start.9) | collective-permute-done | bytes 184352 | tf_op jit(solution)/shard_map/ppermute | solution.py:724
  103.1 2.2 %collective-permute-start.17 = (bf16[32,1152]{1,0:T(8,128)(2,1)S(1)}, bf16[32,1152]{1,0:T(8,128)(2,1)S(1)}, u32[]{:S(2)}, u32[]{:S(2)}) collective-permute-start(bf16[32,1152]{1,0:T(8,128)(2,1)S(1)} %copy-done.19), channel_id=1, source_target_pairs={{0,24},{8,0},{16,8},{24,16},{1,25},{9,1},{17,9},{25,17},{2,26},{10... | collective-permute-start | bytes 221192 | tf_op jit(solution)/shard_map/ppermute | solution.py:714
  105.4 1.6 %collective-permute-start.14 = (bf16[16,1152]{1,0:T(8,128)(2,1)S(1)}, bf16[16,1152]{1,0:T(8,128)(2,1)S(1)}, u32[]{:S(2)}, u32[]{:S(2)}) collective-permute-start(bf16[16,1152]{1,0:T(8,128)(2,1)S(1)} %shard_map.155.refs_0_), channel_id=1, source_target_pairs={{0,24},{8,0},{16,8},{24,16},{1,25},{9,1},{17,9},{25,17},{2,26},{10... | collective-permute-start | bytes 110600 | tf_op jit(solution)/shard_map/ppermute | solution.py:714
  111.8 1.5 %collective-permute-done.13.refs_2_ = bf16[16,1152]{1,0:T(8,128)(2,1)S(1)} collective-permute-done((bf16[16,1152]{1,0:T(8,128)(2,1)S(1)}, bf16[16,1152]{1,0:T(8,128)(2,1)S(1)}, u32[]{:S(2)}, u32[]{:S(2)}) %collective-permute-start.13) | collective-permute-done | bytes 36896 | tf_op jit(solution)/shard_map/ppermute | solution.py:714
  114.0 1.5 %collective-permute-start.23 = (bf16[144,128]{1,0:T(8,128)(2,1)S(1)}, bf16[144,128]{1,0:T(8,128)(2,1)S(1)}, u32[]{:S(2)}, u32[]{:S(2)}) collective-permute-start(bf16[144,128]{1,0:T(8,128)(2,1)S(1)} %shard_map.157.refs_0_), channel_id=1, source_target_pairs={{0,6},{1,7},{2,4},{3,5},{4,2},{5,3},{6,0},{7,1},{8,14},{9,15},{10,... | collective-permute-start | bytes 110600 | tf_op jit(solution)/shard_map/ppermute | solution.py:724
  121.6 2.7 %shard_map.158 = (f32[32,32,36]{2,1,0:T(8,128)}, f32[32,32,36]{2,1,0:T(8,128)}, f32[32,32,36]{2,1,0:T(8,128)}, f32[32,32,36]{2,1,0:T(8,128)}) custom-call(bf16[144,128]{1,0:T(8,128)(2,1)S(1)} %shard_map.157.refs_0_, bf16[144,128]{1,0:T(8,128)(2,1)S(1)} %collective-permute-done.18.refs_1_, bf16[144,128]{1,0:T(8,128)(2,1)S(1)} %collective-permute-done.19.refs_2_, ...), custom_call_target="tpu_custom_call" | custom-call | tf_op jit(solution)/shard_map/pallas_call | solution.py:151
  (94 shorter events, 26.3 us)
Async XLA Ops:
  2.7 28.8 %all-to-all-start = ((bf16[4,2,32,1152]{3,2,1,0:T(8,128)(2,1)}), bf16[4,2,32,1152]{3,2,1,0:T(8,128)(2,1)S(1)}, u32[]{:S(2)}, u32[]{:S(2)}) async-start(bf16[4,2,32,1152]{3,2,1,0:T(8,128)(2,1)} %shard_map.148), calls=%async_computation | async-start | bytes 1179648 | tf_op jit(solution)/shard_map/all_to_all | solution.py:708
  9.1 7.0 %collective-permute-start.3 = (bf16[64,1152]{1,0:T(8,128)(2,1)S(1)}, bf16[64,1152]{1,0:T(8,128)(2,1)S(1)}, u32[]{:S(2)}, u32[]{:S(2)}) collective-permute-start(bf16[64,1152]{1,0:T(8,128)(2,1)S(1)} %get-tuple-element.99), channel_id=1, source_target_pairs={{0,6},{1,7},{2,4},{3,5},{4,2},{5,3},{6,0},{7,1},{8,14},{9,15},{10,... | collective-permute-start | bytes 442376 | tf_op jit(solution)/shard_map/ppermute | solution.py:724
  11.6 6.9 %collective-permute-start.2 = (bf16[64,1152]{1,0:T(8,128)(2,1)S(1)}, bf16[64,1152]{1,0:T(8,128)(2,1)S(1)}, u32[]{:S(2)}, u32[]{:S(2)}) collective-permute-start(bf16[64,1152]{1,0:T(8,128)(2,1)S(1)} %get-tuple-element.100), channel_id=1, source_target_pairs={{0,4},{1,5},{2,6},{3,7},{4,0},{5,1},{6,2},{7,3},{8,12},{9,13},{10,... | collective-permute-start | bytes 442376 | tf_op jit(solution)/shard_map/ppermute | solution.py:724
  12.1 6.6 %collective-permute-start.1 = (bf16[64,1152]{1,0:T(8,128)(2,1)S(1)}, bf16[64,1152]{1,0:T(8,128)(2,1)}, u32[]{:S(2)}, u32[]{:S(2)}) collective-permute-start(bf16[64,1152]{1,0:T(8,128)(2,1)S(1)} %get-tuple-element.101), channel_id=1, source_target_pairs={{0,2},{1,3},{2,0},{3,1},{4,6},{5,7},{6,4},{7,5},{8,10},{9,11},{10,... | collective-permute-start | bytes 442376 | tf_op jit(solution)/shard_map/ppermute | solution.py:724
  12.6 6.6 %collective-permute-start = (bf16[64,1152]{1,0:T(8,128)(2,1)S(1)}, bf16[64,1152]{1,0:T(8,128)(2,1)}, u32[]{:S(2)}, u32[]{:S(2)}) collective-permute-start(bf16[64,1152]{1,0:T(8,128)(2,1)S(1)} %get-tuple-element.102.refs_0_), channel_id=1, source_target_pairs={{0,1},{1,0},{2,3},{3,2},{4,5},{5,4},{6,7},{7,6},{8,9},{9,8},{10,11... | collective-permute-start | bytes 442376 | tf_op jit(solution)/shard_map/ppermute | solution.py:724
  18.7 1.8 %collective-permute-start.4 = (bf16[64,1152]{1,0:T(8,128)(2,1)}, bf16[64,1152]{1,0:T(8,128)(2,1)S(1)}, u32[]{:S(2)}, u32[]{:S(2)}) collective-permute-start(bf16[64,1152]{1,0:T(8,128)(2,1)} %collective-permute-done.1.refs_2_), channel_id=1, source_target_pairs={{0,1},{1,0},{2,3},{3,2},{4,5},{5,4},{6,7},{7,6},{8,9},{9,8},{10,11... | collective-permute-start | bytes 442376 | tf_op jit(solution)/shard_map/ppermute | solution.py:724
  18.7 1.8 %collective-permute-start.5 = (bf16[64,1152]{1,0:T(8,128)(2,1)S(1)}, bf16[64,1152]{1,0:T(8,128)(2,1)S(1)}, u32[]{:S(2)}, u32[]{:S(2)}) collective-permute-start(bf16[64,1152]{1,0:T(8,128)(2,1)S(1)} %collective-permute-done.2.refs_4_), channel_id=1, source_target_pairs={{0,1},{1,0},{2,3},{3,2},{4,5},{5,4},{6,7},{7,6},{8,9},{9,8},{10,11... | collective-permute-start | bytes 442376 | tf_op jit(solution)/shard_map/ppermute | solution.py:724
  31.5 18.1 %all-to-all-start.1 = ((bf16[32,16,384]{2,1,0:T(8,128)(2,1)}), bf16[32,16,384]{2,1,0:T(8,128)(2,1)S(1)}, u32[]{:S(2)}, u32[]{:S(2)}) async-start(bf16[32,16,384]{2,1,0:T(8,128)(2,1)} %get-tuple-element.58), calls=%async_computation.1 | async-start | bytes 786432 | tf_op jit(solution)/shard_map/all_to_all | solution.py:708
  64.8 16.0 %all-to-all-start.2 = ((bf16[32,16,384]{2,1,0:T(8,128)(2,1)}), bf16[32,16,384]{2,1,0:T(8,128)(2,1)S(1)}, u32[]{:S(2)}, u32[]{:S(2)}) async-start(bf16[32,16,384]{2,1,0:T(8,128)(2,1)} %get-tuple-element.65), calls=%async_computation.2 | async-start | bytes 786432 | tf_op jit(solution)/shard_map/all_to_all | solution.py:708
  70.9 1.6 %collective-permute-start.7 = (bf16[4,16,1152]{2,1,0:T(8,128)(2,1)}, bf16[4,16,1152]{2,1,0:T(8,128)(2,1)S(1)}, u32[]{:S(2)}, u32[]{:S(2)}) collective-permute-start(bf16[4,16,1152]{2,1,0:T(8,128)(2,1)} %get-tuple-element.68), channel_id=1, source_target_pairs={{0,1},{1,0},{2,3},{3,2},{4,5},{5,4},{6,7},{7,6},{8,9},{9,8},{10,11... | collective-permute-start | bytes 442376 | tf_op jit(solution)/shard_map/ppermute | solution.py:724
  91.2 2.5 %collective-permute-start.8 = (bf16[4,80,1152]{2,1,0:T(8,128)(2,1)}, bf16[4,80,1152]{2,1,0:T(8,128)(2,1)S(1)}, u32[]{:S(2)}, u32[]{:S(2)}) collective-permute-start(bf16[4,80,1152]{2,1,0:T(8,128)(2,1)} %get-tuple-element.74), channel_id=1, source_target_pairs={{0,1},{1,0},{2,3},{3,2},{4,5},{5,4},{6,7},{7,6},{8,9},{9,8},{10,11... | collective-permute-start | bytes 2211848 | tf_op jit(solution)/shard_map/ppermute | solution.py:724
  93.9 7.5 %collective-permute-start.9 = (bf16[80,1152]{1,0:T(8,128)(2,1)S(1)}, bf16[80,1152]{1,0:T(8,128)(2,1)S(1)}, u32[]{:S(2)}, u32[]{:S(2)}) collective-permute-start(bf16[80,1152]{1,0:T(8,128)(2,1)S(1)} %get-tuple-element.78), channel_id=1, source_target_pairs={{0,2},{1,3},{2,0},{3,1},{4,6},{5,7},{6,4},{7,5},{8,10},{9,11},{10,... | collective-permute-start | bytes 552968 | tf_op jit(solution)/shard_map/ppermute | solution.py:724
  94.6 10.8 %collective-permute-start.10 = (bf16[80,1152]{1,0:T(8,128)(2,1)S(1)}, bf16[80,1152]{1,0:T(8,128)(2,1)S(1)}, u32[]{:S(2)}, u32[]{:S(2)}) collective-permute-start(bf16[80,1152]{1,0:T(8,128)(2,1)S(1)} %get-tuple-element.84), channel_id=1, source_target_pairs={{0,4},{1,5},{2,6},{3,7},{4,0},{5,1},{6,2},{7,3},{8,12},{9,13},{10,... | collective-permute-start | bytes 552968 | tf_op jit(solution)/shard_map/ppermute | solution.py:724
  95.9 9.4 %collective-permute-start.11 = (bf16[80,1152]{1,0:T(8,128)(2,1)S(1)}, bf16[80,1152]{1,0:T(8,128)(2,1)S(1)}, u32[]{:S(2)}, u32[]{:S(2)}) collective-permute-start(bf16[80,1152]{1,0:T(8,128)(2,1)S(1)} %get-tuple-element.85), channel_id=1, source_target_pairs={{0,6},{1,7},{2,4},{3,5},{4,2},{5,3},{6,0},{7,1},{8,14},{9,15},{10,... | collective-permute-start | bytes 552968 | tf_op jit(solution)/shard_map/ppermute | solution.py:724
  101.5 6.6 %collective-permute-start.15 = (bf16[32,1152]{1,0:T(8,128)(2,1)S(1)}, bf16[32,1152]{1,0:T(8,128)(2,1)S(1)}, u32[]{:S(2)}, u32[]{:S(2)}) collective-permute-start(bf16[32,1152]{1,0:T(8,128)(2,1)S(1)} %copy-done.21), channel_id=1, source_target_pairs={{0,8},{8,16},{16,24},{24,0},{1,9},{9,17},{17,25},{25,1},{2,10},{10... | collective-permute-start | bytes 221192 | tf_op jit(solution)/shard_map/ppermute | solution.py:714
  102.5 8.1 %collective-permute-start.16 = (bf16[32,1152]{1,0:T(8,128)(2,1)S(1)}, bf16[32,1152]{1,0:T(8,128)(2,1)S(1)}, u32[]{:S(2)}, u32[]{:S(2)}) collective-permute-start(bf16[32,1152]{1,0:T(8,128)(2,1)S(1)} %copy-done.20), channel_id=1, source_target_pairs={{0,16},{8,24},{16,0},{24,8},{1,17},{9,25},{17,1},{25,9},{2,18},{10... | collective-permute-start | bytes 221192 | tf_op jit(solution)/shard_map/ppermute | solution.py:714
  103.1 7.5 %collective-permute-start.17 = (bf16[32,1152]{1,0:T(8,128)(2,1)S(1)}, bf16[32,1152]{1,0:T(8,128)(2,1)S(1)}, u32[]{:S(2)}, u32[]{:S(2)}) collective-permute-start(bf16[32,1152]{1,0:T(8,128)(2,1)S(1)} %copy-done.19), channel_id=1, source_target_pairs={{0,24},{8,0},{16,8},{24,16},{1,25},{9,1},{17,9},{25,17},{2,26},{10... | collective-permute-start | bytes 221192 | tf_op jit(solution)/shard_map/ppermute | solution.py:714
  105.4 6.4 %collective-permute-start.14 = (bf16[16,1152]{1,0:T(8,128)(2,1)S(1)}, bf16[16,1152]{1,0:T(8,128)(2,1)S(1)}, u32[]{:S(2)}, u32[]{:S(2)}) collective-permute-start(bf16[16,1152]{1,0:T(8,128)(2,1)S(1)} %shard_map.155.refs_0_), channel_id=1, source_target_pairs={{0,24},{8,0},{16,8},{24,16},{1,25},{9,1},{17,9},{25,17},{2,26},{10... | collective-permute-start | bytes 110600 | tf_op jit(solution)/shard_map/ppermute | solution.py:714
  107.0 6.3 %collective-permute-start.13 = (bf16[16,1152]{1,0:T(8,128)(2,1)S(1)}, bf16[16,1152]{1,0:T(8,128)(2,1)S(1)}, u32[]{:S(2)}, u32[]{:S(2)}) collective-permute-start(bf16[16,1152]{1,0:T(8,128)(2,1)S(1)} %shard_map.155.refs_0_), channel_id=1, source_target_pairs={{0,16},{8,24},{16,0},{24,8},{1,17},{9,25},{17,1},{25,9},{2,18},{10... | collective-permute-start | bytes 110600 | tf_op jit(solution)/shard_map/ppermute | solution.py:714
  108.0 5.8 %collective-permute-start.12 = (bf16[16,1152]{1,0:T(8,128)(2,1)S(1)}, bf16[16,1152]{1,0:T(8,128)(2,1)S(1)}, u32[]{:S(2)}, u32[]{:S(2)}) collective-permute-start(bf16[16,1152]{1,0:T(8,128)(2,1)S(1)} %shard_map.155.refs_0_), channel_id=1, source_target_pairs={{0,8},{8,16},{16,24},{24,0},{1,9},{9,17},{17,25},{25,1},{2,10},{10... | collective-permute-start | bytes 110600 | tf_op jit(solution)/shard_map/ppermute | solution.py:714
  114.0 4.9 %collective-permute-start.23 = (bf16[144,128]{1,0:T(8,128)(2,1)S(1)}, bf16[144,128]{1,0:T(8,128)(2,1)S(1)}, u32[]{:S(2)}, u32[]{:S(2)}) collective-permute-start(bf16[144,128]{1,0:T(8,128)(2,1)S(1)} %shard_map.157.refs_0_), channel_id=1, source_target_pairs={{0,6},{1,7},{2,4},{3,5},{4,2},{5,3},{6,0},{7,1},{8,14},{9,15},{10,... | collective-permute-start | bytes 110600 | tf_op jit(solution)/shard_map/ppermute | solution.py:724
  115.4 4.0 %collective-permute-start.21 = (bf16[144,128]{1,0:T(8,128)(2,1)S(1)}, bf16[144,128]{1,0:T(8,128)(2,1)S(1)}, u32[]{:S(2)}, u32[]{:S(2)}) collective-permute-start(bf16[144,128]{1,0:T(8,128)(2,1)S(1)} %shard_map.157.refs_0_), channel_id=1, source_target_pairs={{0,4},{1,5},{2,6},{3,7},{4,0},{5,1},{6,2},{7,3},{8,12},{9,13},{10,... | collective-permute-start | bytes 110600 | tf_op jit(solution)/shard_map/ppermute | solution.py:724
  116.4 4.0 %collective-permute-start.19 = (bf16[144,128]{1,0:T(8,128)(2,1)S(1)}, bf16[144,128]{1,0:T(8,128)(2,1)S(1)}, u32[]{:S(2)}, u32[]{:S(2)}) collective-permute-start(bf16[144,128]{1,0:T(8,128)(2,1)S(1)} %shard_map.157.refs_0_), channel_id=1, source_target_pairs={{0,2},{1,3},{2,0},{3,1},{4,6},{5,7},{6,4},{7,5},{8,10},{9,11},{10,... | collective-permute-start | bytes 110600 | tf_op jit(solution)/shard_map/ppermute | solution.py:724
  117.5 2.8 %collective-permute-start.18 = (bf16[144,128]{1,0:T(8,128)(2,1)S(1)}, bf16[144,128]{1,0:T(8,128)(2,1)S(1)}, u32[]{:S(2)}, u32[]{:S(2)}) collective-permute-start(bf16[144,128]{1,0:T(8,128)(2,1)S(1)} %shard_map.157.refs_0_), channel_id=1, source_target_pairs={{0,1},{1,0},{2,3},{3,2},{4,5},{5,4},{6,7},{7,6},{8,9},{9,8},{10,11... | collective-permute-start | bytes 110600 | tf_op jit(solution)/shard_map/ppermute | solution.py:724
  (26 other events, 233.7 us)

commit v4 on v3

--- a/solution.py
+++ b/solution.py
@@ -110,12 +110,6 @@
             copy = pltpu.make_async_copy(self.ref.at[i], self.target.at[i], self.sems.at[i])
             copy.start()
             self.started.append(copy)
-
-    def flush_span(self, start, size, i):
-        span = pl.ds(start, size)
-        copy = pltpu.make_async_copy(self.ref.at[span], self.target.at[span], self.sems.at[i])
-        copy.start()
-        self.started.append(copy)
 
     def finish(self):
         for copy in self.started:
@@ -666,7 +660,7 @@
 
 def unpack_kernel(plan, scaling, *refs):
     pieces = refs[: plan.patch_ways]
-    outs, wide = refs[plan.patch_ways : plan.patch_ways + 4], refs[plan.patch_ways + 4]
+    out_refs, wide = refs[plan.patch_ways : plan.patch_ways + 4], refs[plan.patch_ways + 4]
     blocks = 4 * CHUNKS
     row = lax.broadcasted_iota(jnp.int32, (blocks, blocks), 0)
     column = lax.broadcasted_iota(jnp.int32, (blocks, blocks), 1)
@@ -678,10 +672,8 @@
             rows = wide[r, inner * blocks : (inner + 1) * blocks, :].astype(BF16)
             turned = dot_tn(rows, chosen) * scaling
             b = plan.peer(r) * plan.term_blocks + inner
-            for t, out in enumerate(outs):
-                out.ref[b] = turned[t * BLOCK : (t + 1) * BLOCK, :]
-        for out in outs:
-            out.flush_span(plan.peer(r) * plan.term_blocks, plan.term_blocks, r)
+            for t, out_ref in enumerate(out_refs):
+                out_ref[b] = turned[t * BLOCK : (t + 1) * BLOCK, :]
 
 
 def estimate(flops, moved):
@@ -888,7 +880,7 @@
         for blocks in call(
             functools.partial(unpack_kernel, plan, scaling),
             mode("v", shared),
-            mode("d", [block_shape] * 4),
+            mode("v", [block_shape] * 4),
             [pltpu.VMEM((plan.patch_ways,) + share_shape.shape, F32)],
             limit=16,
         )

time: 125 us -> 124 us (level)
  no operation moved by 1% of the time
where the time goes in v4:
time: 124 us; the launch traced here: 123 us
  Pallas kernels  49.2 us (40%)
  starting transfers between devices  33.2 us (27%)
  waiting for transfers between devices  32.5 us (26%)
  local copies, waits for them, and re-layouts  7.57 us (6%)
    pallas_call x13, Pallas kernels, call(): pl.pallas_call(body, out_shape=tuple((out for _, out in outs)), in_specs=...  49.2 us
    ppermute x19, waiting for transfers between devices, swap(): return lax.ppermute(rows, 'patch', pairs)  17.7 us
    all_to_all x3, starting transfers between devices, per_device(): exchange = lambda rows, axis: lax.all_to_all(rows, axis, 0, 0, tiled=True)  14.5 us
    ppermute x19, starting transfers between devices, swap(): return lax.ppermute(rows, 'patch', pairs)  11.4 us
    all_to_all x3, waiting for transfers between devices, per_device(): exchange = lambda rows, axis: lax.all_to_all(rows, axis, 0, 0, tiled=True)  11.1 us
    ppermute x6, starting transfers between devices, shifted(): lax.ppermute(pieces[s], 'frame', [(i, (i + s) % ways) for i in range(ways)])  7.39 us
    unnamed x45, local copies, waits for them, and re-layouts  4.76 us
    ppermute x6, waiting for transfers between devices, shifted(): lax.ppermute(pieces[s], 'frame', [(i, (i + s) % ways) for i in range(ways)])  3.68 us
  transfers between devices with their start and end apart: 28, of which 19 were waited for; matrix products, arithmetic and copies ran while one was open for 3% of the time, Pallas kernels for 16%

profile of v4, /device:TPU:0, one launch (start us, length us, event | category | flops | bytes accessed | tf_op | source)
XLA Modules:
  0.0 123.4 jit_solution(2364745364827331311)
XLA Ops:
  0.7 2.0 %shard_map.148 = bf16[4,2,32,1152]{3,2,1,0:T(8,128)(2,1)} custom-call(bf16[2,64,1152]{2,1,0:T(8,128)(2,1)} %refs_8_.1, bf16[2,64,1152]{2,1,0:T(8,128)(2,1)} %refs_1_.2), custom_call_target="tpu_custom_call" | custom-call | tf_op jit(solution)/shard_map/pallas_call | solution.py:145
  2.7 6.3 %all-to-all-start = ((bf16[4,2,32,1152]{3,2,1,0:T(8,128)(2,1)}), bf16[4,2,32,1152]{3,2,1,0:T(8,128)(2,1)S(1)}, u32[]{:S(2)}, u32[]{:S(2)}) async-start(bf16[4,2,32,1152]{3,2,1,0:T(8,128)(2,1)} %shard_map.148), calls=%async_computation | async-start | bytes 1179648 | tf_op jit(solution)/shard_map/all_to_all | solution.py:700
  9.1 2.5 %collective-permute-start.3 = (bf16[64,1152]{1,0:T(8,128)(2,1)S(1)}, bf16[64,1152]{1,0:T(8,128)(2,1)S(1)}, u32[]{:S(2)}, u32[]{:S(2)}) collective-permute-start(bf16[64,1152]{1,0:T(8,128)(2,1)S(1)} %get-tuple-element.99), channel_id=1, source_target_pairs={{0,6},{1,7},{2,4},{3,5},{4,2},{5,3},{6,0},{7,1},{8,14},{9,15},{10,... | collective-permute-start | bytes 442376 | tf_op jit(solution)/shard_map/ppermute | solution.py:716
  14.3 1.7 %collective-permute-done.3.refs_6_ = bf16[64,1152]{1,0:T(8,128)(2,1)S(1)} collective-permute-done((bf16[64,1152]{1,0:T(8,128)(2,1)S(1)}, bf16[64,1152]{1,0:T(8,128)(2,1)S(1)}, u32[]{:S(2)}, u32[]{:S(2)}) %collective-permute-start.3) | collective-permute-done | bytes 147488 | tf_op jit(solution)/shard_map/ppermute | solution.py:716
  16.1 2.4 %collective-permute-done.2.refs_4_ = bf16[64,1152]{1,0:T(8,128)(2,1)S(1)} collective-permute-done((bf16[64,1152]{1,0:T(8,128)(2,1)S(1)}, bf16[64,1152]{1,0:T(8,128)(2,1)S(1)}, u32[]{:S(2)}, u32[]{:S(2)}) %collective-permute-start.2) | collective-permute-done | bytes 147488 | tf_op jit(solution)/shard_map/ppermute | solution.py:716
  21.8 9.7 %shard_map.147 = (bf16[1,512,1152]{2,1,0:T(8,128)(2,1)}, bf16[3,512,512]{2,1,0:T(8,128)(2,1)}, bf16[4,512,512]{2,1,0:T(8,128)(2,1)}, bf16[32,16,384]{2,1,0:T(8,128)(2,1)}) custom-call(bf16[64,1152]{1,0:T(8,128)(2,1)} %copy-done.10, bf16[64,1152]{1,0:T(8,128)(2,1)} %collective-permute-done.refs_1_, bf16[64,1152]{1,0:T(8,128)(2,1)} %collective-permute-done.1.refs_2_, ...), custom_call_target="tpu_custom_call" | custom-call | flops 1073741824 | bytes 8000000 | tf_op jit(solution)/shard_map/pallas_call | solution.py:145
  31.5 5.1 %all-to-all-start.1 = ((bf16[32,16,384]{2,1,0:T(8,128)(2,1)}), bf16[32,16,384]{2,1,0:T(8,128)(2,1)S(1)}, u32[]{:S(2)}, u32[]{:S(2)}) async-start(bf16[32,16,384]{2,1,0:T(8,128)(2,1)} %get-tuple-element.58), calls=%async_computation.1 | async-start | bytes 786432 | tf_op jit(solution)/shard_map/all_to_all | solution.py:700
  37.8 1.6 %copy.19 = f32[36,32,32]{2,1,0:T(8,128)S(1)} copy(f32[36,32,32]{0,2,1:T(8,128)} %param.21) | data formatting | bytes 294912 | tf_op jit(solution)/shard_map/optimization_barrier | solution.py:758
  42.0 4.8 %shard_map.150.refs_7_.refs_0_ = bf16[3,128,1152]{2,1,0:T(8,128)(2,1)} custom-call(bf16[4,2,32,1152]{3,2,1,0:T(8,128)(2,1)} %copy-done.8, s32[8]{0:T(128)} %refs_2_.3, bf16[1152,1152]{1,0:T(8,128)(2,1)} %refs_2_.2, bf16[1,1152,128]{2,1,0:T(8,128)(2,1)} %copy-done.5), custom_call_target="tpu_custom_call" | custom-call | flops 339738624 | bytes 4000000 | tf_op jit(solution)/shard_map/pallas_call | solution.py:145
  46.8 2.8 %all-to-all-done.1.refs_1_ = bf16[32,16,384]{2,1,0:T(8,128)(2,1)S(1)} async-done(((bf16[32,16,384]{2,1,0:T(8,128)(2,1)}), bf16[32,16,384]{2,1,0:T(8,128)(2,1)S(1)}, u32[]{:S(2)}, u32[]{:S(2)}) %all-to-all-start.1) | async-done | bytes 393248 | tf_op jit(solution)/shard_map/all_to_all | solution.py:700
  50.3 14.4 %shard_map.151 = (bf16[32,16,384]{2,1,0:T(8,128)(2,1)}, bf16[5,128,1152]{2,1,0:T(8,128)(2,1)}, bf16[32,1152]{1,0:T(8,128)(2,1)}, bf16[32,1152]{1,0:T(8,128)(2,1)...) custom-call(bf16[4,2,32,1152]{3,2,1,0:T(8,128)(2,1)} %copy-done.8, bf16[32,16,384]{2,1,0:T(8,128)(2,1)} %copy-done.9, ...), custom_call_target="tpu_custom_call" | custom-call | flops 2717908992 | bytes 12000000 | tf_op jit(solution)/shard_map/pallas_call | solution.py:145
  64.8 3.1 %all-to-all-start.2 = ((bf16[32,16,384]{2,1,0:T(8,128)(2,1)}), bf16[32,16,384]{2,1,0:T(8,128)(2,1)S(1)}, u32[]{:S(2)}, u32[]{:S(2)}) async-start(bf16[32,16,384]{2,1,0:T(8,128)(2,1)} %get-tuple-element.65), calls=%async_computation.2 | async-start | bytes 786432 | tf_op jit(solution)/shard_map/all_to_all | solution.py:700
  67.9 3.0 %shard_map.152 = (bf16[4,16,1152]{2,1,0:T(8,128)(2,1)}, bf16[4,16,1152]{2,1,0:T(8,128)(2,1)}) custom-call(bf16[3,128,1152]{2,1,0:T(8,128)(2,1)} %shard_map.150.refs_7_.refs_0_, bf16[5,128,1152]{2,1,0:T(8,128)(2,1)} %get-tuple-element.66.refs_1_), custom_call_target="tpu_custom_call" | custom-call | flops 1000000000 | bytes 4000000 | tf_op jit(solution)/shard_map/pallas_call | solution.py:145
  71.0 1.5 %collective-permute-done.7.refs_3_ = bf16[4,16,1152]{2,1,0:T(8,128)(2,1)S(1)} collective-permute-done((bf16[4,16,1152]{2,1,0:T(8,128)(2,1)}, bf16[4,16,1152]{2,1,0:T(8,128)(2,1)S(1)}, u32[]{:S(2)}, u32[]{:S(2)}) %collective-permute-start.7) | collective-permute-done | bytes 147488 | tf_op jit(solution)/shard_map/ppermute | solution.py:716
  72.5 8.3 %all-to-all-done.2.refs_0_ = bf16[32,16,384]{2,1,0:T(8,128)(2,1)S(1)} async-done(((bf16[32,16,384]{2,1,0:T(8,128)(2,1)}), bf16[32,16,384]{2,1,0:T(8,128)(2,1)S(1)}, u32[]{:S(2)}, u32[]{:S(2)}) %all-to-all-start.2) | async-done | bytes 393248 | tf_op jit(solution)/shard_map/all_to_all | solution.py:700
  80.9 10.3 %shard_map.153 = (bf16[4,80,1152]{2,1,0:T(8,128)(2,1)S(1)}, bf16[4,80,1152]{2,1,0:T(8,128)(2,1)}) custom-call(bf16[32,16,384]{2,1,0:T(8,128)(2,1)S(1)} %all-to-all-done.2.refs_0_, bf16[3,512,512]{2,1,0:T(8,128)(2,1)} %get-tuple-element.70.refs_1_, bf16[4,512,512]{2,1,0:T(8,128)(2,1)} %get-tuple-element.71.refs_2_, bf16[1,1152,128]{2,1,0:T(8,128)(2,1)S(1)} %copy-done.2, ...), custom_call_target="tpu_custom_call" | custom-call | flops 10000000000 | bytes 8000000 | tf_op jit(solution)/shard_map/pallas_call | solution.py:145
  91.3 2.4 %collective-permute-done.8.refs_1_ = bf16[4,80,1152]{2,1,0:T(8,128)(2,1)S(1)} collective-permute-done((bf16[4,80,1152]{2,1,0:T(8,128)(2,1)}, bf16[4,80,1152]{2,1,0:T(8,128)(2,1)S(1)}, u32[]{:S(2)}, u32[]{:S(2)}) %collective-permute-start.8) | collective-permute-done | bytes 737312 | tf_op jit(solution)/shard_map/ppermute | solution.py:716
  95.9 1.5 %collective-permute-start.11 = (bf16[80,1152]{1,0:T(8,128)(2,1)S(1)}, bf16[80,1152]{1,0:T(8,128)(2,1)S(1)}, u32[]{:S(2)}, u32[]{:S(2)}) collective-permute-start(bf16[80,1152]{1,0:T(8,128)(2,1)S(1)} %get-tuple-element.85), channel_id=1, source_target_pairs={{0,6},{1,7},{2,4},{3,5},{4,2},{5,3},{6,0},{7,1},{8,14},{9,15},{10,... | collective-permute-start | bytes 552968 | tf_op jit(solution)/shard_map/ppermute | solution.py:716
  97.5 4.0 %collective-permute-done.9.refs_1_.refs_5_ = bf16[80,1152]{1,0:T(8,128)(2,1)S(1)} collective-permute-done((bf16[80,1152]{1,0:T(8,128)(2,1)S(1)}, bf16[80,1152]{1,0:T(8,128)(2,1)S(1)}, u32[]{:S(2)}, u32[]{:S(2)}) %collective-permute-start.9) | collective-permute-done | bytes 184352 | tf_op jit(solution)/shard_map/ppermute | solution.py:716
  103.1 2.2 %collective-permute-start.17 = (bf16[32,1152]{1,0:T(8,128)(2,1)S(1)}, bf16[32,1152]{1,0:T(8,128)(2,1)S(1)}, u32[]{:S(2)}, u32[]{:S(2)}) collective-permute-start(bf16[32,1152]{1,0:T(8,128)(2,1)S(1)} %copy-done.19), channel_id=1, source_target_pairs={{0,24},{8,0},{16,8},{24,16},{1,25},{9,1},{17,9},{25,17},{2,26},{10... | collective-permute-start | bytes 221192 | tf_op jit(solution)/shard_map/ppermute | solution.py:706
  105.4 1.6 %collective-permute-start.14 = (bf16[16,1152]{1,0:T(8,128)(2,1)S(1)}, bf16[16,1152]{1,0:T(8,128)(2,1)S(1)}, u32[]{:S(2)}, u32[]{:S(2)}) collective-permute-start(bf16[16,1152]{1,0:T(8,128)(2,1)S(1)} %shard_map.155.refs_0_), channel_id=1, source_target_pairs={{0,24},{8,0},{16,8},{24,16},{1,25},{9,1},{17,9},{25,17},{2,26},{10... | collective-permute-start | bytes 110600 | tf_op jit(solution)/shard_map/ppermute | solution.py:706
  111.8 1.5 %collective-permute-done.13.refs_2_ = bf16[16,1152]{1,0:T(8,128)(2,1)S(1)} collective-permute-done((bf16[16,1152]{1,0:T(8,128)(2,1)S(1)}, bf16[16,1152]{1,0:T(8,128)(2,1)S(1)}, u32[]{:S(2)}, u32[]{:S(2)}) %collective-permute-start.13) | collective-permute-done | bytes 36896 | tf_op jit(solution)/shard_map/ppermute | solution.py:706
  114.0 1.5 %collective-permute-start.23 = (bf16[144,128]{1,0:T(8,128)(2,1)S(1)}, bf16[144,128]{1,0:T(8,128)(2,1)S(1)}, u32[]{:S(2)}, u32[]{:S(2)}) collective-permute-start(bf16[144,128]{1,0:T(8,128)(2,1)S(1)} %shard_map.157.refs_0_), channel_id=1, source_target_pairs={{0,6},{1,7},{2,4},{3,5},{4,2},{5,3},{6,0},{7,1},{8,14},{9,15},{10,... | collective-permute-start | bytes 110600 | tf_op jit(solution)/shard_map/ppermute | solution.py:716
  121.6 1.8 %shard_map.158 = (f32[32,32,36]{2,1,0:T(8,128)}, f32[32,32,36]{2,1,0:T(8,128)}, f32[32,32,36]{2,1,0:T(8,128)}, f32[32,32,36]{2,1,0:T(8,128)}) custom-call(bf16[144,128]{1,0:T(8,128)(2,1)S(1)} %shard_map.157.refs_0_, bf16[144,128]{1,0:T(8,128)(2,1)S(1)} %collective-permute-done.18.refs_1_, bf16[144,128]{1,0:T(8,128)(2,1)S(1)} %collective-permute-done.19.refs_2_, ...), custom_call_target="tpu_custom_call" | custom-call | tf_op jit(solution)/shard_map/pallas_call | solution.py:145
  (94 shorter events, 26.3 us)
Async XLA Ops:
  2.7 28.8 %all-to-all-start = ((bf16[4,2,32,1152]{3,2,1,0:T(8,128)(2,1)}), bf16[4,2,32,1152]{3,2,1,0:T(8,128)(2,1)S(1)}, u32[]{:S(2)}, u32[]{:S(2)}) async-start(bf16[4,2,32,1152]{3,2,1,0:T(8,128)(2,1)} %shard_map.148), calls=%async_computation | async-start | bytes 1179648 | tf_op jit(solution)/shard_map/all_to_all | solution.py:700
  9.1 7.0 %collective-permute-start.3 = (bf16[64,1152]{1,0:T(8,128)(2,1)S(1)}, bf16[64,1152]{1,0:T(8,128)(2,1)S(1)}, u32[]{:S(2)}, u32[]{:S(2)}) collective-permute-start(bf16[64,1152]{1,0:T(8,128)(2,1)S(1)} %get-tuple-element.99), channel_id=1, source_target_pairs={{0,6},{1,7},{2,4},{3,5},{4,2},{5,3},{6,0},{7,1},{8,14},{9,15},{10,... | collective-permute-start | bytes 442376 | tf_op jit(solution)/shard_map/ppermute | solution.py:716
  11.6 6.9 %collective-permute-start.2 = (bf16[64,1152]{1,0:T(8,128)(2,1)S(1)}, bf16[64,1152]{1,0:T(8,128)(2,1)S(1)}, u32[]{:S(2)}, u32[]{:S(2)}) collective-permute-start(bf16[64,1152]{1,0:T(8,128)(2,1)S(1)} %get-tuple-element.100), channel_id=1, source_target_pairs={{0,4},{1,5},{2,6},{3,7},{4,0},{5,1},{6,2},{7,3},{8,12},{9,13},{10,... | collective-permute-start | bytes 442376 | tf_op jit(solution)/shard_map/ppermute | solution.py:716
  12.1 6.6 %collective-permute-start.1 = (bf16[64,1152]{1,0:T(8,128)(2,1)S(1)}, bf16[64,1152]{1,0:T(8,128)(2,1)}, u32[]{:S(2)}, u32[]{:S(2)}) collective-permute-start(bf16[64,1152]{1,0:T(8,128)(2,1)S(1)} %get-tuple-element.101), channel_id=1, source_target_pairs={{0,2},{1,3},{2,0},{3,1},{4,6},{5,7},{6,4},{7,5},{8,10},{9,11},{10,... | collective-permute-start | bytes 442376 | tf_op jit(solution)/shard_map/ppermute | solution.py:716
  12.6 6.6 %collective-permute-start = (bf16[64,1152]{1,0:T(8,128)(2,1)S(1)}, bf16[64,1152]{1,0:T(8,128)(2,1)}, u32[]{:S(2)}, u32[]{:S(2)}) collective-permute-start(bf16[64,1152]{1,0:T(8,128)(2,1)S(1)} %get-tuple-element.102.refs_0_), channel_id=1, source_target_pairs={{0,1},{1,0},{2,3},{3,2},{4,5},{5,4},{6,7},{7,6},{8,9},{9,8},{10,11... | collective-permute-start | bytes 442376 | tf_op jit(solution)/shard_map/ppermute | solution.py:716
  18.7 1.8 %collective-permute-start.4 = (bf16[64,1152]{1,0:T(8,128)(2,1)}, bf16[64,1152]{1,0:T(8,128)(2,1)S(1)}, u32[]{:S(2)}, u32[]{:S(2)}) collective-permute-start(bf16[64,1152]{1,0:T(8,128)(2,1)} %collective-permute-done.1.refs_2_), channel_id=1, source_target_pairs={{0,1},{1,0},{2,3},{3,2},{4,5},{5,4},{6,7},{7,6},{8,9},{9,8},{10,11... | collective-permute-start | bytes 442376 | tf_op jit(solution)/shard_map/ppermute | solution.py:716
  18.7 1.8 %collective-permute-start.5 = (bf16[64,1152]{1,0:T(8,128)(2,1)S(1)}, bf16[64,1152]{1,0:T(8,128)(2,1)S(1)}, u32[]{:S(2)}, u32[]{:S(2)}) collective-permute-start(bf16[64,1152]{1,0:T(8,128)(2,1)S(1)} %collective-permute-done.2.refs_4_), channel_id=1, source_target_pairs={{0,1},{1,0},{2,3},{3,2},{4,5},{5,4},{6,7},{7,6},{8,9},{9,8},{10,11... | collective-permute-start | bytes 442376 | tf_op jit(solution)/shard_map/ppermute | solution.py:716
  31.5 18.1 %all-to-all-start.1 = ((bf16[32,16,384]{2,1,0:T(8,128)(2,1)}), bf16[32,16,384]{2,1,0:T(8,128)(2,1)S(1)}, u32[]{:S(2)}, u32[]{:S(2)}) async-start(bf16[32,16,384]{2,1,0:T(8,128)(2,1)} %get-tuple-element.58), calls=%async_computation.1 | async-start | bytes 786432 | tf_op jit(solution)/shard_map/all_to_all | solution.py:700
  64.8 16.0 %all-to-all-start.2 = ((bf16[32,16,384]{2,1,0:T(8,128)(2,1)}), bf16[32,16,384]{2,1,0:T(8,128)(2,1)S(1)}, u32[]{:S(2)}, u32[]{:S(2)}) async-start(bf16[32,16,384]{2,1,0:T(8,128)(2,1)} %get-tuple-element.65), calls=%async_computation.2 | async-start | bytes 786432 | tf_op jit(solution)/shard_map/all_to_all | solution.py:700
  70.9 1.6 %collective-permute-start.7 = (bf16[4,16,1152]{2,1,0:T(8,128)(2,1)}, bf16[4,16,1152]{2,1,0:T(8,128)(2,1)S(1)}, u32[]{:S(2)}, u32[]{:S(2)}) collective-permute-start(bf16[4,16,1152]{2,1,0:T(8,128)(2,1)} %get-tuple-element.68), channel_id=1, source_target_pairs={{0,1},{1,0},{2,3},{3,2},{4,5},{5,4},{6,7},{7,6},{8,9},{9,8},{10,11... | collective-permute-start | bytes 442376 | tf_op jit(solution)/shard_map/ppermute | solution.py:716
  91.2 2.5 %collective-permute-start.8 = (bf16[4,80,1152]{2,1,0:T(8,128)(2,1)}, bf16[4,80,1152]{2,1,0:T(8,128)(2,1)S(1)}, u32[]{:S(2)}, u32[]{:S(2)}) collective-permute-start(bf16[4,80,1152]{2,1,0:T(8,128)(2,1)} %get-tuple-element.74), channel_id=1, source_target_pairs={{0,1},{1,0},{2,3},{3,2},{4,5},{5,4},{6,7},{7,6},{8,9},{9,8},{10,11... | collective-permute-start | bytes 2211848 | tf_op jit(solution)/shard_map/ppermute | solution.py:716
  93.9 7.5 %collective-permute-start.9 = (bf16[80,1152]{1,0:T(8,128)(2,1)S(1)}, bf16[80,1152]{1,0:T(8,128)(2,1)S(1)}, u32[]{:S(2)}, u32[]{:S(2)}) collective-permute-start(bf16[80,1152]{1,0:T(8,128)(2,1)S(1)} %get-tuple-element.78), channel_id=1, source_target_pairs={{0,2},{1,3},{2,0},{3,1},{4,6},{5,7},{6,4},{7,5},{8,10},{9,11},{10,... | collective-permute-start | bytes 552968 | tf_op jit(solution)/shard_map/ppermute | solution.py:716
  94.6 10.8 %collective-permute-start.10 = (bf16[80,1152]{1,0:T(8,128)(2,1)S(1)}, bf16[80,1152]{1,0:T(8,128)(2,1)S(1)}, u32[]{:S(2)}, u32[]{:S(2)}) collective-permute-start(bf16[80,1152]{1,0:T(8,128)(2,1)S(1)} %get-tuple-element.84), channel_id=1, source_target_pairs={{0,4},{1,5},{2,6},{3,7},{4,0},{5,1},{6,2},{7,3},{8,12},{9,13},{10,... | collective-permute-start | bytes 552968 | tf_op jit(solution)/shard_map/ppermute | solution.py:716
  95.9 9.4 %collective-permute-start.11 = (bf16[80,1152]{1,0:T(8,128)(2,1)S(1)}, bf16[80,1152]{1,0:T(8,128)(2,1)S(1)}, u32[]{:S(2)}, u32[]{:S(2)}) collective-permute-start(bf16[80,1152]{1,0:T(8,128)(2,1)S(1)} %get-tuple-element.85), channel_id=1, source_target_pairs={{0,6},{1,7},{2,4},{3,5},{4,2},{5,3},{6,0},{7,1},{8,14},{9,15},{10,... | collective-permute-start | bytes 552968 | tf_op jit(solution)/shard_map/ppermute | solution.py:716
  101.5 6.6 %collective-permute-start.15 = (bf16[32,1152]{1,0:T(8,128)(2,1)S(1)}, bf16[32,1152]{1,0:T(8,128)(2,1)S(1)}, u32[]{:S(2)}, u32[]{:S(2)}) collective-permute-start(bf16[32,1152]{1,0:T(8,128)(2,1)S(1)} %copy-done.21), channel_id=1, source_target_pairs={{0,8},{8,16},{16,24},{24,0},{1,9},{9,17},{17,25},{25,1},{2,10},{10... | collective-permute-start | bytes 221192 | tf_op jit(solution)/shard_map/ppermute | solution.py:706
  102.5 8.1 %collective-permute-start.16 = (bf16[32,1152]{1,0:T(8,128)(2,1)S(1)}, bf16[32,1152]{1,0:T(8,128)(2,1)S(1)}, u32[]{:S(2)}, u32[]{:S(2)}) collective-permute-start(bf16[32,1152]{1,0:T(8,128)(2,1)S(1)} %copy-done.20), channel_id=1, source_target_pairs={{0,16},{8,24},{16,0},{24,8},{1,17},{9,25},{17,1},{25,9},{2,18},{10... | collective-permute-start | bytes 221192 | tf_op jit(solution)/shard_map/ppermute | solution.py:706
  103.1 7.5 %collective-permute-start.17 = (bf16[32,1152]{1,0:T(8,128)(2,1)S(1)}, bf16[32,1152]{1,0:T(8,128)(2,1)S(1)}, u32[]{:S(2)}, u32[]{:S(2)}) collective-permute-start(bf16[32,1152]{1,0:T(8,128)(2,1)S(1)} %copy-done.19), channel_id=1, source_target_pairs={{0,24},{8,0},{16,8},{24,16},{1,25},{9,1},{17,9},{25,17},{2,26},{10... | collective-permute-start | bytes 221192 | tf_op jit(solution)/shard_map/ppermute | solution.py:706
  105.4 6.4 %collective-permute-start.14 = (bf16[16,1152]{1,0:T(8,128)(2,1)S(1)}, bf16[16,1152]{1,0:T(8,128)(2,1)S(1)}, u32[]{:S(2)}, u32[]{:S(2)}) collective-permute-start(bf16[16,1152]{1,0:T(8,128)(2,1)S(1)} %shard_map.155.refs_0_), channel_id=1, source_target_pairs={{0,24},{8,0},{16,8},{24,16},{1,25},{9,1},{17,9},{25,17},{2,26},{10... | collective-permute-start | bytes 110600 | tf_op jit(solution)/shard_map/ppermute | solution.py:706
  107.0 6.3 %collective-permute-start.13 = (bf16[16,1152]{1,0:T(8,128)(2,1)S(1)}, bf16[16,1152]{1,0:T(8,128)(2,1)S(1)}, u32[]{:S(2)}, u32[]{:S(2)}) collective-permute-start(bf16[16,1152]{1,0:T(8,128)(2,1)S(1)} %shard_map.155.refs_0_), channel_id=1, source_target_pairs={{0,16},{8,24},{16,0},{24,8},{1,17},{9,25},{17,1},{25,9},{2,18},{10... | collective-permute-start | bytes 110600 | tf_op jit(solution)/shard_map/ppermute | solution.py:706
  108.0 5.8 %collective-permute-start.12 = (bf16[16,1152]{1,0:T(8,128)(2,1)S(1)}, bf16[16,1152]{1,0:T(8,128)(2,1)S(1)}, u32[]{:S(2)}, u32[]{:S(2)}) collective-permute-start(bf16[16,1152]{1,0:T(8,128)(2,1)S(1)} %shard_map.155.refs_0_), channel_id=1, source_target_pairs={{0,8},{8,16},{16,24},{24,0},{1,9},{9,17},{17,25},{25,1},{2,10},{10... | collective-permute-start | bytes 110600 | tf_op jit(solution)/shard_map/ppermute | solution.py:706
  114.0 4.9 %collective-permute-start.23 = (bf16[144,128]{1,0:T(8,128)(2,1)S(1)}, bf16[144,128]{1,0:T(8,128)(2,1)S(1)}, u32[]{:S(2)}, u32[]{:S(2)}) collective-permute-start(bf16[144,128]{1,0:T(8,128)(2,1)S(1)} %shard_map.157.refs_0_), channel_id=1, source_target_pairs={{0,6},{1,7},{2,4},{3,5},{4,2},{5,3},{6,0},{7,1},{8,14},{9,15},{10,... | collective-permute-start | bytes 110600 | tf_op jit(solution)/shard_map/ppermute | solution.py:716
  115.4 4.0 %collective-permute-start.21 = (bf16[144,128]{1,0:T(8,128)(2,1)S(1)}, bf16[144,128]{1,0:T(8,128)(2,1)S(1)}, u32[]{:S(2)}, u32[]{:S(2)}) collective-permute-start(bf16[144,128]{1,0:T(8,128)(2,1)S(1)} %shard_map.157.refs_0_), channel_id=1, source_target_pairs={{0,4},{1,5},{2,6},{3,7},{4,0},{5,1},{6,2},{7,3},{8,12},{9,13},{10,... | collective-permute-start | bytes 110600 | tf_op jit(solution)/shard_map/ppermute | solution.py:716
  116.4 4.0 %collective-permute-start.19 = (bf16[144,128]{1,0:T(8,128)(2,1)S(1)}, bf16[144,128]{1,0:T(8,128)(2,1)S(1)}, u32[]{:S(2)}, u32[]{:S(2)}) collective-permute-start(bf16[144,128]{1,0:T(8,128)(2,1)S(1)} %shard_map.157.refs_0_), channel_id=1, source_target_pairs={{0,2},{1,3},{2,0},{3,1},{4,6},{5,7},{6,4},{7,5},{8,10},{9,11},{10,... | collective-permute-start | bytes 110600 | tf_op jit(solution)/shard_map/ppermute | solution.py:716
  117.5 2.8 %collective-permute-start.18 = (bf16[144,128]{1,0:T(8,128)(2,1)S(1)}, bf16[144,128]{1,0:T(8,128)(2,1)S(1)}, u32[]{:S(2)}, u32[]{:S(2)}) collective-permute-start(bf16[144,128]{1,0:T(8,128)(2,1)S(1)} %shard_map.157.refs_0_), channel_id=1, source_target_pairs={{0,1},{1,0},{2,3},{3,2},{4,5},{5,4},{6,7},{7,6},{8,9},{9,8},{10,11... | collective-permute-start | bytes 110600 | tf_op jit(solution)/shard_map/ppermute | solution.py:716
  (26 other events, 233.7 us)

commit v5 on v4

--- a/solution.py
+++ b/solution.py
@@ -65,13 +65,21 @@
 
 def rotate(rows, blocks_ref):
     return jnp.concatenate(
-        [dot(rows[:, lanes_of(c)], blocks_ref[lanes_of(c), :]) for c in range(CHUNKS)], axis=1
-    )
-
-
-def rotate_transposed(rows, blocks_ref):
+        [
+            dot(rows[:, lanes_of(c)], blocks_ref[lanes_of(c), :]).astype(BF16)
+            for c in range(CHUNKS)
+        ],
+        axis=1,
+    )
+
+
+def rotate_transposed(rows, blocks_ref, dtype=BF16):
     return jnp.concatenate(
-        [dot_nt(rows[:, lanes_of(c)], blocks_ref[lanes_of(c), :]) for c in range(CHUNKS)], axis=1
+        [
+            dot_nt(rows[:, lanes_of(c)], blocks_ref[lanes_of(c), :]).astype(dtype)
+            for c in range(CHUNKS)
+        ],
+        axis=1,
     )
 
 
@@ -276,7 +284,7 @@
             normed = normalize(rows[i : i + BLOCK, :].astype(F32))[0].astype(BF16)
             normed_out.ref[0, r * size + i : r * size + i + BLOCK, :] = normed
     normed_out.flush(0)
-    rotated = rotate(normed_out.ref[0], blocks().at[0]).astype(BF16)
+    rotated = rotate(normed_out.ref[0], blocks().at[0])
     stack_ref = stack_out.ref
     wait_all(copies)
     projected = dot(rotated, windows[...]).astype(BF16)
@@ -403,7 +411,7 @@
     rotation_gradient(normed()[0], rotated, diagonal_mask(), terms, 0)
     ordered[...] = jnp.zeros_like(ordered)
     order_terms(plan, terms, ordered, 3 * CHUNKS, CHUNKS)
-    back = rotate_transposed(rotated, blocks().at[0]).astype(BF16)
+    back = rotate_transposed(rotated, blocks().at[0])
     for r in list(range(1, plan.patch_ways, 2)) + list(range(0, plan.patch_ways, 2)):
         out = (even_out, odd_out)[r % 2]
         out_ref = out.ref.at[r // 2]
@@ -446,7 +454,7 @@
     outrot = dot_nt(top, weight()[...]).astype(BF16)
     out.ref[1] = outrot
     out.flush(1)
-    out.ref[2] = rotate_transposed(outrot, blocks().at[0]).astype(BF16)
+    out.ref[2] = rotate_transposed(outrot, blocks().at[0])
     out.flush(2)
 
 
@@ -506,7 +514,7 @@
                     tile = part if tile is None else tile + part
             attended_one[f * own : (f + 1) * own, lanes_of(c)] = tile
     factors.flush(3)
-    outrot_one = rotate(attended_one[...], outward().at[0]).astype(BF16)
+    outrot_one = rotate(attended_one[...], outward().at[0])
     out_weight = spatial_output()
     wait_all(piece_copies)
     hidden = (inputs[...].astype(F32) + dot(outrot_one, out_weight[...])).astype(BF16)
@@ -514,7 +522,7 @@
     normed_low = normed.astype(BF16)
     factors.ref[1] = normed_low
     factors.flush(1)
-    rotated = rotate(normed_low, inward().at[0]).astype(BF16)
+    rotated = rotate(normed_low, inward().at[0])
     total = None
     for (start, size), copy in zip(SPANS, weight_copies):
         copy.wait()
@@ -579,7 +587,7 @@
     adjoint_rotated = dot_nt(grads[...], project_weight[...]).astype(BF16)
     factors.ref[2] = adjoint_rotated
     factors.flush(2)
-    adjoint_normed = rotate_transposed(adjoint_rotated, inward().at[0])
+    adjoint_normed = rotate_transposed(adjoint_rotated, inward().at[0], F32)
     adjoint_hidden = early[0].astype(F32) + normalize_backward(adjoint_normed, normed, inverse)
     adjoint_hidden = adjoint_hidden.astype(BF16)
     inputs[...] = adjoint_hidden
@@ -591,7 +599,7 @@
     outrot_adjoint = dot_nt(adjoint_hidden, out_weight[...]).astype(BF16)
     factors.ref[4] = outrot_adjoint
     factors.flush(4)
-    adjoint_attended = rotate_transposed(outrot_adjoint, outward().at[0]).astype(BF16)
+    adjoint_attended = rotate_transposed(outrot_adjoint, outward().at[0])
     for f in range(plan.frames):
         z, inner = divmod(f, plan.frames_local)
         base = z * plan.patch_ways + inner * plan.groups

time: 124 us -> 124 us (level)
  no operation moved by 1% of the time
where the time goes in v5:
time: 124 us; the launch traced here: 123 us
  Pallas kernels  49.2 us (40%)
  starting transfers between devices  33.2 us (27%)
  waiting for transfers between devices  32.5 us (26%)
  local copies, waits for them, and re-layouts  7.57 us (6%)
    pallas_call x13, Pallas kernels, call(): pl.pallas_call(body, out_shape=tuple((out for _, out in outs)), in_specs=...  49.2 us
    ppermute x19, waiting for transfers between devices, swap(): return lax.ppermute(rows, 'patch', pairs)  17.7 us
    all_to_all x3, starting transfers between devices, per_device(): exchange = lambda rows, axis: lax.all_to_all(rows, axis, 0, 0, tiled=True)  14.5 us
    ppermute x19, starting transfers between devices, swap(): return lax.ppermute(rows, 'patch', pairs)  11.4 us
    all_to_all x3, waiting for transfers between devices, per_device(): exchange = lambda rows, axis: lax.all_to_all(rows, axis, 0, 0, tiled=True)  11.1 us
    ppermute x6, starting transfers between devices, shifted(): lax.ppermute(pieces[s], 'frame', [(i, (i + s) % ways) for i in range(ways)])  7.39 us
    unnamed x45, local copies, waits for them, and re-layouts  4.76 us
    ppermute x6, waiting for transfers between devices, shifted(): lax.ppermute(pieces[s], 'frame', [(i, (i + s) % ways) for i in range(ways)])  3.68 us
  transfers between devices with their start and end apart: 28, of which 19 were waited for; matrix products, arithmetic and copies ran while one was open for 3% of the time, Pallas kernels for 16%

profile of v5, /device:TPU:0, one launch (start us, length us, event | category | flops | bytes accessed | tf_op | source)
XLA Modules:
  0.0 123.4 jit_solution(2364745364827331311)
XLA Ops:
  0.7 2.0 %shard_map.148 = bf16[4,2,32,1152]{3,2,1,0:T(8,128)(2,1)} custom-call(bf16[2,64,1152]{2,1,0:T(8,128)(2,1)} %refs_8_.1, bf16[2,64,1152]{2,1,0:T(8,128)(2,1)} %refs_1_.2), custom_call_target="tpu_custom_call" | custom-call | tf_op jit(solution)/shard_map/pallas_call | solution.py:153
  2.7 6.3 %all-to-all-start = ((bf16[4,2,32,1152]{3,2,1,0:T(8,128)(2,1)}), bf16[4,2,32,1152]{3,2,1,0:T(8,128)(2,1)S(1)}, u32[]{:S(2)}, u32[]{:S(2)}) async-start(bf16[4,2,32,1152]{3,2,1,0:T(8,128)(2,1)} %shard_map.148), calls=%async_computation | async-start | bytes 1179648 | tf_op jit(solution)/shard_map/all_to_all | solution.py:708
  9.1 2.5 %collective-permute-start.3 = (bf16[64,1152]{1,0:T(8,128)(2,1)S(1)}, bf16[64,1152]{1,0:T(8,128)(2,1)S(1)}, u32[]{:S(2)}, u32[]{:S(2)}) collective-permute-start(bf16[64,1152]{1,0:T(8,128)(2,1)S(1)} %get-tuple-element.99), channel_id=1, source_target_pairs={{0,6},{1,7},{2,4},{3,5},{4,2},{5,3},{6,0},{7,1},{8,14},{9,15},{10,... | collective-permute-start | bytes 442376 | tf_op jit(solution)/shard_map/ppermute | solution.py:724
  14.3 1.7 %collective-permute-done.3.refs_6_ = bf16[64,1152]{1,0:T(8,128)(2,1)S(1)} collective-permute-done((bf16[64,1152]{1,0:T(8,128)(2,1)S(1)}, bf16[64,1152]{1,0:T(8,128)(2,1)S(1)}, u32[]{:S(2)}, u32[]{:S(2)}) %collective-permute-start.3) | collective-permute-done | bytes 147488 | tf_op jit(solution)/shard_map/ppermute | solution.py:724
  16.1 2.4 %collective-permute-done.2.refs_4_ = bf16[64,1152]{1,0:T(8,128)(2,1)S(1)} collective-permute-done((bf16[64,1152]{1,0:T(8,128)(2,1)S(1)}, bf16[64,1152]{1,0:T(8,128)(2,1)S(1)}, u32[]{:S(2)}, u32[]{:S(2)}) %collective-permute-start.2) | collective-permute-done | bytes 147488 | tf_op jit(solution)/shard_map/ppermute | solution.py:724
  21.8 9.7 %shard_map.147 = (bf16[1,512,1152]{2,1,0:T(8,128)(2,1)}, bf16[3,512,512]{2,1,0:T(8,128)(2,1)}, bf16[4,512,512]{2,1,0:T(8,128)(2,1)}, bf16[32,16,384]{2,1,0:T(8,128)(2,1)}) custom-call(bf16[64,1152]{1,0:T(8,128)(2,1)} %copy-done.10, bf16[64,1152]{1,0:T(8,128)(2,1)} %collective-permute-done.refs_1_, bf16[64,1152]{1,0:T(8,128)(2,1)} %collective-permute-done.1.refs_2_, ...), custom_call_target="tpu_custom_call" | custom-call | flops 1073741824 | bytes 8000000 | tf_op jit(solution)/shard_map/pallas_call | solution.py:153
  31.5 5.1 %all-to-all-start.1 = ((bf16[32,16,384]{2,1,0:T(8,128)(2,1)}), bf16[32,16,384]{2,1,0:T(8,128)(2,1)S(1)}, u32[]{:S(2)}, u32[]{:S(2)}) async-start(bf16[32,16,384]{2,1,0:T(8,128)(2,1)} %get-tuple-element.58), calls=%async_computation.1 | async-start | bytes 786432 | tf_op jit(solution)/shard_map/all_to_all | solution.py:708
  37.8 1.6 %copy.19 = f32[36,32,32]{2,1,0:T(8,128)S(1)} copy(f32[36,32,32]{0,2,1:T(8,128)} %param.21) | data formatting | bytes 294912 | tf_op jit(solution)/shard_map/optimization_barrier | solution.py:766
  42.0 4.8 %shard_map.150.refs_7_.refs_0_ = bf16[3,128,1152]{2,1,0:T(8,128)(2,1)} custom-call(bf16[4,2,32,1152]{3,2,1,0:T(8,128)(2,1)} %copy-done.8, s32[8]{0:T(128)} %refs_2_.3, bf16[1152,1152]{1,0:T(8,128)(2,1)} %refs_2_.2, bf16[1,1152,128]{2,1,0:T(8,128)(2,1)} %copy-done.5), custom_call_target="tpu_custom_call" | custom-call | flops 339738624 | bytes 4000000 | tf_op jit(solution)/shard_map/pallas_call | solution.py:153
  46.8 2.8 %all-to-all-done.1.refs_1_ = bf16[32,16,384]{2,1,0:T(8,128)(2,1)S(1)} async-done(((bf16[32,16,384]{2,1,0:T(8,128)(2,1)}), bf16[32,16,384]{2,1,0:T(8,128)(2,1)S(1)}, u32[]{:S(2)}, u32[]{:S(2)}) %all-to-all-start.1) | async-done | bytes 393248 | tf_op jit(solution)/shard_map/all_to_all | solution.py:708
  50.3 14.4 %shard_map.151 = (bf16[32,16,384]{2,1,0:T(8,128)(2,1)}, bf16[5,128,1152]{2,1,0:T(8,128)(2,1)}, bf16[32,1152]{1,0:T(8,128)(2,1)}, bf16[32,1152]{1,0:T(8,128)(2,1)...) custom-call(bf16[4,2,32,1152]{3,2,1,0:T(8,128)(2,1)} %copy-done.8, bf16[32,16,384]{2,1,0:T(8,128)(2,1)} %copy-done.9, ...), custom_call_target="tpu_custom_call" | custom-call | flops 2717908992 | bytes 12000000 | tf_op jit(solution)/shard_map/pallas_call | solution.py:153
  64.8 3.1 %all-to-all-start.2 = ((bf16[32,16,384]{2,1,0:T(8,128)(2,1)}), bf16[32,16,384]{2,1,0:T(8,128)(2,1)S(1)}, u32[]{:S(2)}, u32[]{:S(2)}) async-start(bf16[32,16,384]{2,1,0:T(8,128)(2,1)} %get-tuple-element.65), calls=%async_computation.2 | async-start | bytes 786432 | tf_op jit(solution)/shard_map/all_to_all | solution.py:708
  67.9 3.0 %shard_map.152 = (bf16[4,16,1152]{2,1,0:T(8,128)(2,1)}, bf16[4,16,1152]{2,1,0:T(8,128)(2,1)}) custom-call(bf16[3,128,1152]{2,1,0:T(8,128)(2,1)} %shard_map.150.refs_7_.refs_0_, bf16[5,128,1152]{2,1,0:T(8,128)(2,1)} %get-tuple-element.66.refs_1_), custom_call_target="tpu_custom_call" | custom-call | flops 1000000000 | bytes 4000000 | tf_op jit(solution)/shard_map/pallas_call | solution.py:153
  71.0 1.5 %collective-permute-done.7.refs_3_ = bf16[4,16,1152]{2,1,0:T(8,128)(2,1)S(1)} collective-permute-done((bf16[4,16,1152]{2,1,0:T(8,128)(2,1)}, bf16[4,16,1152]{2,1,0:T(8,128)(2,1)S(1)}, u32[]{:S(2)}, u32[]{:S(2)}) %collective-permute-start.7) | collective-permute-done | bytes 147488 | tf_op jit(solution)/shard_map/ppermute | solution.py:724
  72.5 8.3 %all-to-all-done.2.refs_0_ = bf16[32,16,384]{2,1,0:T(8,128)(2,1)S(1)} async-done(((bf16[32,16,384]{2,1,0:T(8,128)(2,1)}), bf16[32,16,384]{2,1,0:T(8,128)(2,1)S(1)}, u32[]{:S(2)}, u32[]{:S(2)}) %all-to-all-start.2) | async-done | bytes 393248 | tf_op jit(solution)/shard_map/all_to_all | solution.py:708
  80.9 10.3 %shard_map.153 = (bf16[4,80,1152]{2,1,0:T(8,128)(2,1)S(1)}, bf16[4,80,1152]{2,1,0:T(8,128)(2,1)}) custom-call(bf16[32,16,384]{2,1,0:T(8,128)(2,1)S(1)} %all-to-all-done.2.refs_0_, bf16[3,512,512]{2,1,0:T(8,128)(2,1)} %get-tuple-element.70.refs_1_, bf16[4,512,512]{2,1,0:T(8,128)(2,1)} %get-tuple-element.71.refs_2_, bf16[1,1152,128]{2,1,0:T(8,128)(2,1)S(1)} %copy-done.2, ...), custom_call_target="tpu_custom_call" | custom-call | flops 10000000000 | bytes 8000000 | tf_op jit(solution)/shard_map/pallas_call | solution.py:153
  91.3 2.4 %collective-permute-done.8.refs_1_ = bf16[4,80,1152]{2,1,0:T(8,128)(2,1)S(1)} collective-permute-done((bf16[4,80,1152]{2,1,0:T(8,128)(2,1)}, bf16[4,80,1152]{2,1,0:T(8,128)(2,1)S(1)}, u32[]{:S(2)}, u32[]{:S(2)}) %collective-permute-start.8) | collective-permute-done | bytes 737312 | tf_op jit(solution)/shard_map/ppermute | solution.py:724
  95.9 1.5 %collective-permute-start.11 = (bf16[80,1152]{1,0:T(8,128)(2,1)S(1)}, bf16[80,1152]{1,0:T(8,128)(2,1)S(1)}, u32[]{:S(2)}, u32[]{:S(2)}) collective-permute-start(bf16[80,1152]{1,0:T(8,128)(2,1)S(1)} %get-tuple-element.85), channel_id=1, source_target_pairs={{0,6},{1,7},{2,4},{3,5},{4,2},{5,3},{6,0},{7,1},{8,14},{9,15},{10,... | collective-permute-start | bytes 552968 | tf_op jit(solution)/shard_map/ppermute | solution.py:724
  97.5 4.0 %collective-permute-done.9.refs_1_.refs_5_ = bf16[80,1152]{1,0:T(8,128)(2,1)S(1)} collective-permute-done((bf16[80,1152]{1,0:T(8,128)(2,1)S(1)}, bf16[80,1152]{1,0:T(8,128)(2,1)S(1)}, u32[]{:S(2)}, u32[]{:S(2)}) %collective-permute-start.9) | collective-permute-done | bytes 184352 | tf_op jit(solution)/shard_map/ppermute | solution.py:724
  103.1 2.2 %collective-permute-start.17 = (bf16[32,1152]{1,0:T(8,128)(2,1)S(1)}, bf16[32,1152]{1,0:T(8,128)(2,1)S(1)}, u32[]{:S(2)}, u32[]{:S(2)}) collective-permute-start(bf16[32,1152]{1,0:T(8,128)(2,1)S(1)} %copy-done.19), channel_id=1, source_target_pairs={{0,24},{8,0},{16,8},{24,16},{1,25},{9,1},{17,9},{25,17},{2,26},{10... | collective-permute-start | bytes 221192 | tf_op jit(solution)/shard_map/ppermute | solution.py:714
  105.4 1.6 %collective-permute-start.14 = (bf16[16,1152]{1,0:T(8,128)(2,1)S(1)}, bf16[16,1152]{1,0:T(8,128)(2,1)S(1)}, u32[]{:S(2)}, u32[]{:S(2)}) collective-permute-start(bf16[16,1152]{1,0:T(8,128)(2,1)S(1)} %shard_map.155.refs_0_), channel_id=1, source_target_pairs={{0,24},{8,0},{16,8},{24,16},{1,25},{9,1},{17,9},{25,17},{2,26},{10... | collective-permute-start | bytes 110600 | tf_op jit(solution)/shard_map/ppermute | solution.py:714
  111.8 1.5 %collective-permute-done.13.refs_2_ = bf16[16,1152]{1,0:T(8,128)(2,1)S(1)} collective-permute-done((bf16[16,1152]{1,0:T(8,128)(2,1)S(1)}, bf16[16,1152]{1,0:T(8,128)(2,1)S(1)}, u32[]{:S(2)}, u32[]{:S(2)}) %collective-permute-start.13) | collective-permute-done | bytes 36896 | tf_op jit(solution)/shard_map/ppermute | solution.py:714
  114.0 1.5 %collective-permute-start.23 = (bf16[144,128]{1,0:T(8,128)(2,1)S(1)}, bf16[144,128]{1,0:T(8,128)(2,1)S(1)}, u32[]{:S(2)}, u32[]{:S(2)}) collective-permute-start(bf16[144,128]{1,0:T(8,128)(2,1)S(1)} %shard_map.157.refs_0_), channel_id=1, source_target_pairs={{0,6},{1,7},{2,4},{3,5},{4,2},{5,3},{6,0},{7,1},{8,14},{9,15},{10,... | collective-permute-start | bytes 110600 | tf_op jit(solution)/shard_map/ppermute | solution.py:724
  121.6 1.8 %shard_map.158 = (f32[32,32,36]{2,1,0:T(8,128)}, f32[32,32,36]{2,1,0:T(8,128)}, f32[32,32,36]{2,1,0:T(8,128)}, f32[32,32,36]{2,1,0:T(8,128)}) custom-call(bf16[144,128]{1,0:T(8,128)(2,1)S(1)} %shard_map.157.refs_0_, bf16[144,128]{1,0:T(8,128)(2,1)S(1)} %collective-permute-done.18.refs_1_, bf16[144,128]{1,0:T(8,128)(2,1)S(1)} %collective-permute-done.19.refs_2_, ...), custom_call_target="tpu_custom_call" | custom-call | tf_op jit(solution)/shard_map/pallas_call | solution.py:153
  (94 shorter events, 26.3 us)
Async XLA Ops:
  2.7 28.8 %all-to-all-start = ((bf16[4,2,32,1152]{3,2,1,0:T(8,128)(2,1)}), bf16[4,2,32,1152]{3,2,1,0:T(8,128)(2,1)S(1)}, u32[]{:S(2)}, u32[]{:S(2)}) async-start(bf16[4,2,32,1152]{3,2,1,0:T(8,128)(2,1)} %shard_map.148), calls=%async_computation | async-start | bytes 1179648 | tf_op jit(solution)/shard_map/all_to_all | solution.py:708
  9.1 7.0 %collective-permute-start.3 = (bf16[64,1152]{1,0:T(8,128)(2,1)S(1)}, bf16[64,1152]{1,0:T(8,128)(2,1)S(1)}, u32[]{:S(2)}, u32[]{:S(2)}) collective-permute-start(bf16[64,1152]{1,0:T(8,128)(2,1)S(1)} %get-tuple-element.99), channel_id=1, source_target_pairs={{0,6},{1,7},{2,4},{3,5},{4,2},{5,3},{6,0},{7,1},{8,14},{9,15},{10,... | collective-permute-start | bytes 442376 | tf_op jit(solution)/shard_map/ppermute | solution.py:724
  11.6 6.9 %collective-permute-start.2 = (bf16[64,1152]{1,0:T(8,128)(2,1)S(1)}, bf16[64,1152]{1,0:T(8,128)(2,1)S(1)}, u32[]{:S(2)}, u32[]{:S(2)}) collective-permute-start(bf16[64,1152]{1,0:T(8,128)(2,1)S(1)} %get-tuple-element.100), channel_id=1, source_target_pairs={{0,4},{1,5},{2,6},{3,7},{4,0},{5,1},{6,2},{7,3},{8,12},{9,13},{10,... | collective-permute-start | bytes 442376 | tf_op jit(solution)/shard_map/ppermute | solution.py:724
  12.1 6.6 %collective-permute-start.1 = (bf16[64,1152]{1,0:T(8,128)(2,1)S(1)}, bf16[64,1152]{1,0:T(8,128)(2,1)}, u32[]{:S(2)}, u32[]{:S(2)}) collective-permute-start(bf16[64,1152]{1,0:T(8,128)(2,1)S(1)} %get-tuple-element.101), channel_id=1, source_target_pairs={{0,2},{1,3},{2,0},{3,1},{4,6},{5,7},{6,4},{7,5},{8,10},{9,11},{10,... | collective-permute-start | bytes 442376 | tf_op jit(solution)/shard_map/ppermute | solution.py:724
  12.6 6.6 %collective-permute-start = (bf16[64,1152]{1,0:T(8,128)(2,1)S(1)}, bf16[64,1152]{1,0:T(8,128)(2,1)}, u32[]{:S(2)}, u32[]{:S(2)}) collective-permute-start(bf16[64,1152]{1,0:T(8,128)(2,1)S(1)} %get-tuple-element.102.refs_0_), channel_id=1, source_target_pairs={{0,1},{1,0},{2,3},{3,2},{4,5},{5,4},{6,7},{7,6},{8,9},{9,8},{10,11... | collective-permute-start | bytes 442376 | tf_op jit(solution)/shard_map/ppermute | solution.py:724
  18.7 1.8 %collective-permute-start.4 = (bf16[64,1152]{1,0:T(8,128)(2,1)}, bf16[64,1152]{1,0:T(8,128)(2,1)S(1)}, u32[]{:S(2)}, u32[]{:S(2)}) collective-permute-start(bf16[64,1152]{1,0:T(8,128)(2,1)} %collective-permute-done.1.refs_2_), channel_id=1, source_target_pairs={{0,1},{1,0},{2,3},{3,2},{4,5},{5,4},{6,7},{7,6},{8,9},{9,8},{10,11... | collective-permute-start | bytes 442376 | tf_op jit(solution)/shard_map/ppermute | solution.py:724
  18.7 1.8 %collective-permute-start.5 = (bf16[64,1152]{1,0:T(8,128)(2,1)S(1)}, bf16[64,1152]{1,0:T(8,128)(2,1)S(1)}, u32[]{:S(2)}, u32[]{:S(2)}) collective-permute-start(bf16[64,1152]{1,0:T(8,128)(2,1)S(1)} %collective-permute-done.2.refs_4_), channel_id=1, source_target_pairs={{0,1},{1,0},{2,3},{3,2},{4,5},{5,4},{6,7},{7,6},{8,9},{9,8},{10,11... | collective-permute-start | bytes 442376 | tf_op jit(solution)/shard_map/ppermute | solution.py:724
  31.5 18.1 %all-to-all-start.1 = ((bf16[32,16,384]{2,1,0:T(8,128)(2,1)}), bf16[32,16,384]{2,1,0:T(8,128)(2,1)S(1)}, u32[]{:S(2)}, u32[]{:S(2)}) async-start(bf16[32,16,384]{2,1,0:T(8,128)(2,1)} %get-tuple-element.58), calls=%async_computation.1 | async-start | bytes 786432 | tf_op jit(solution)/shard_map/all_to_all | solution.py:708
  64.8 16.0 %all-to-all-start.2 = ((bf16[32,16,384]{2,1,0:T(8,128)(2,1)}), bf16[32,16,384]{2,1,0:T(8,128)(2,1)S(1)}, u32[]{:S(2)}, u32[]{:S(2)}) async-start(bf16[32,16,384]{2,1,0:T(8,128)(2,1)} %get-tuple-element.65), calls=%async_computation.2 | async-start | bytes 786432 | tf_op jit(solution)/shard_map/all_to_all | solution.py:708
  70.9 1.6 %collective-permute-start.7 = (bf16[4,16,1152]{2,1,0:T(8,128)(2,1)}, bf16[4,16,1152]{2,1,0:T(8,128)(2,1)S(1)}, u32[]{:S(2)}, u32[]{:S(2)}) collective-permute-start(bf16[4,16,1152]{2,1,0:T(8,128)(2,1)} %get-tuple-element.68), channel_id=1, source_target_pairs={{0,1},{1,0},{2,3},{3,2},{4,5},{5,4},{6,7},{7,6},{8,9},{9,8},{10,11... | collective-permute-start | bytes 442376 | tf_op jit(solution)/shard_map/ppermute | solution.py:724
  91.2 2.5 %collective-permute-start.8 = (bf16[4,80,1152]{2,1,0:T(8,128)(2,1)}, bf16[4,80,1152]{2,1,0:T(8,128)(2,1)S(1)}, u32[]{:S(2)}, u32[]{:S(2)}) collective-permute-start(bf16[4,80,1152]{2,1,0:T(8,128)(2,1)} %get-tuple-element.74), channel_id=1, source_target_pairs={{0,1},{1,0},{2,3},{3,2},{4,5},{5,4},{6,7},{7,6},{8,9},{9,8},{10,11... | collective-permute-start | bytes 2211848 | tf_op jit(solution)/shard_map/ppermute | solution.py:724
  93.9 7.5 %collective-permute-start.9 = (bf16[80,1152]{1,0:T(8,128)(2,1)S(1)}, bf16[80,1152]{1,0:T(8,128)(2,1)S(1)}, u32[]{:S(2)}, u32[]{:S(2)}) collective-permute-start(bf16[80,1152]{1,0:T(8,128)(2,1)S(1)} %get-tuple-element.78), channel_id=1, source_target_pairs={{0,2},{1,3},{2,0},{3,1},{4,6},{5,7},{6,4},{7,5},{8,10},{9,11},{10,... | collective-permute-start | bytes 552968 | tf_op jit(solution)/shard_map/ppermute | solution.py:724
  94.6 10.8 %collective-permute-start.10 = (bf16[80,1152]{1,0:T(8,128)(2,1)S(1)}, bf16[80,1152]{1,0:T(8,128)(2,1)S(1)}, u32[]{:S(2)}, u32[]{:S(2)}) collective-permute-start(bf16[80,1152]{1,0:T(8,128)(2,1)S(1)} %get-tuple-element.84), channel_id=1, source_target_pairs={{0,4},{1,5},{2,6},{3,7},{4,0},{5,1},{6,2},{7,3},{8,12},{9,13},{10,... | collective-permute-start | bytes 552968 | tf_op jit(solution)/shard_map/ppermute | solution.py:724
  95.9 9.4 %collective-permute-start.11 = (bf16[80,1152]{1,0:T(8,128)(2,1)S(1)}, bf16[80,1152]{1,0:T(8,128)(2,1)S(1)}, u32[]{:S(2)}, u32[]{:S(2)}) collective-permute-start(bf16[80,1152]{1,0:T(8,128)(2,1)S(1)} %get-tuple-element.85), channel_id=1, source_target_pairs={{0,6},{1,7},{2,4},{3,5},{4,2},{5,3},{6,0},{7,1},{8,14},{9,15},{10,... | collective-permute-start | bytes 552968 | tf_op jit(solution)/shard_map/ppermute | solution.py:724
  101.5 6.6 %collective-permute-start.15 = (bf16[32,1152]{1,0:T(8,128)(2,1)S(1)}, bf16[32,1152]{1,0:T(8,128)(2,1)S(1)}, u32[]{:S(2)}, u32[]{:S(2)}) collective-permute-start(bf16[32,1152]{1,0:T(8,128)(2,1)S(1)} %copy-done.21), channel_id=1, source_target_pairs={{0,8},{8,16},{16,24},{24,0},{1,9},{9,17},{17,25},{25,1},{2,10},{10... | collective-permute-start | bytes 221192 | tf_op jit(solution)/shard_map/ppermute | solution.py:714
  102.5 8.1 %collective-permute-start.16 = (bf16[32,1152]{1,0:T(8,128)(2,1)S(1)}, bf16[32,1152]{1,0:T(8,128)(2,1)S(1)}, u32[]{:S(2)}, u32[]{:S(2)}) collective-permute-start(bf16[32,1152]{1,0:T(8,128)(2,1)S(1)} %copy-done.20), channel_id=1, source_target_pairs={{0,16},{8,24},{16,0},{24,8},{1,17},{9,25},{17,1},{25,9},{2,18},{10... | collective-permute-start | bytes 221192 | tf_op jit(solution)/shard_map/ppermute | solution.py:714
  103.1 7.5 %collective-permute-start.17 = (bf16[32,1152]{1,0:T(8,128)(2,1)S(1)}, bf16[32,1152]{1,0:T(8,128)(2,1)S(1)}, u32[]{:S(2)}, u32[]{:S(2)}) collective-permute-start(bf16[32,1152]{1,0:T(8,128)(2,1)S(1)} %copy-done.19), channel_id=1, source_target_pairs={{0,24},{8,0},{16,8},{24,16},{1,25},{9,1},{17,9},{25,17},{2,26},{10... | collective-permute-start | bytes 221192 | tf_op jit(solution)/shard_map/ppermute | solution.py:714
  105.4 6.4 %collective-permute-start.14 = (bf16[16,1152]{1,0:T(8,128)(2,1)S(1)}, bf16[16,1152]{1,0:T(8,128)(2,1)S(1)}, u32[]{:S(2)}, u32[]{:S(2)}) collective-permute-start(bf16[16,1152]{1,0:T(8,128)(2,1)S(1)} %shard_map.155.refs_0_), channel_id=1, source_target_pairs={{0,24},{8,0},{16,8},{24,16},{1,25},{9,1},{17,9},{25,17},{2,26},{10... | collective-permute-start | bytes 110600 | tf_op jit(solution)/shard_map/ppermute | solution.py:714
  107.0 6.3 %collective-permute-start.13 = (bf16[16,1152]{1,0:T(8,128)(2,1)S(1)}, bf16[16,1152]{1,0:T(8,128)(2,1)S(1)}, u32[]{:S(2)}, u32[]{:S(2)}) collective-permute-start(bf16[16,1152]{1,0:T(8,128)(2,1)S(1)} %shard_map.155.refs_0_), channel_id=1, source_target_pairs={{0,16},{8,24},{16,0},{24,8},{1,17},{9,25},{17,1},{25,9},{2,18},{10... | collective-permute-start | bytes 110600 | tf_op jit(solution)/shard_map/ppermute | solution.py:714
  108.0 5.8 %collective-permute-start.12 = (bf16[16,1152]{1,0:T(8,128)(2,1)S(1)}, bf16[16,1152]{1,0:T(8,128)(2,1)S(1)}, u32[]{:S(2)}, u32[]{:S(2)}) collective-permute-start(bf16[16,1152]{1,0:T(8,128)(2,1)S(1)} %shard_map.155.refs_0_), channel_id=1, source_target_pairs={{0,8},{8,16},{16,24},{24,0},{1,9},{9,17},{17,25},{25,1},{2,10},{10... | collective-permute-start | bytes 110600 | tf_op jit(solution)/shard_map/ppermute | solution.py:714
  114.0 4.9 %collective-permute-start.23 = (bf16[144,128]{1,0:T(8,128)(2,1)S(1)}, bf16[144,128]{1,0:T(8,128)(2,1)S(1)}, u32[]{:S(2)}, u32[]{:S(2)}) collective-permute-start(bf16[144,128]{1,0:T(8,128)(2,1)S(1)} %shard_map.157.refs_0_), channel_id=1, source_target_pairs={{0,6},{1,7},{2,4},{3,5},{4,2},{5,3},{6,0},{7,1},{8,14},{9,15},{10,... | collective-permute-start | bytes 110600 | tf_op jit(solution)/shard_map/ppermute | solution.py:724
  115.4 4.0 %collective-permute-start.21 = (bf16[144,128]{1,0:T(8,128)(2,1)S(1)}, bf16[144,128]{1,0:T(8,128)(2,1)S(1)}, u32[]{:S(2)}, u32[]{:S(2)}) collective-permute-start(bf16[144,128]{1,0:T(8,128)(2,1)S(1)} %shard_map.157.refs_0_), channel_id=1, source_target_pairs={{0,4},{1,5},{2,6},{3,7},{4,0},{5,1},{6,2},{7,3},{8,12},{9,13},{10,... | collective-permute-start | bytes 110600 | tf_op jit(solution)/shard_map/ppermute | solution.py:724
  116.4 4.0 %collective-permute-start.19 = (bf16[144,128]{1,0:T(8,128)(2,1)S(1)}, bf16[144,128]{1,0:T(8,128)(2,1)S(1)}, u32[]{:S(2)}, u32[]{:S(2)}) collective-permute-start(bf16[144,128]{1,0:T(8,128)(2,1)S(1)} %shard_map.157.refs_0_), channel_id=1, source_target_pairs={{0,2},{1,3},{2,0},{3,1},{4,6},{5,7},{6,4},{7,5},{8,10},{9,11},{10,... | collective-permute-start | bytes 110600 | tf_op jit(solution)/shard_map/ppermute | solution.py:724
  117.5 2.8 %collective-permute-start.18 = (bf16[144,128]{1,0:T(8,128)(2,1)S(1)}, bf16[144,128]{1,0:T(8,128)(2,1)S(1)}, u32[]{:S(2)}, u32[]{:S(2)}) collective-permute-start(bf16[144,128]{1,0:T(8,128)(2,1)S(1)} %shard_map.157.refs_0_), channel_id=1, source_target_pairs={{0,1},{1,0},{2,3},{3,2},{4,5},{5,4},{6,7},{7,6},{8,9},{9,8},{10,11... | collective-permute-start | bytes 110600 | tf_op jit(solution)/shard_map/ppermute | solution.py:724
  (26 other events, 233.7 us)
